TPU v7x, 32 devices: a whole 2x2x4 slice. The times are simulated.
32 devices in a mesh: mp: 4 (over x, core), fsdp: 8 (over z, y).
Axes of the slice: x: 2, y: 2, z: 4, core: 2. Of those that a mesh axis runs over, the one named last changes fastest.
Arguments:
- hidden_in: bfloat16 [4, 6144, 5120], P('mp', 'fsdp'), may hold values from -6 to 6
- gain_in: bfloat16 [4, 5120], P('mp'), may hold values from 0.099609375 to 1.8984375
- w_key: bfloat16 [4, 5120, 512], P('mp', 'fsdp'), may hold values from -0.078125 to 0.078125
- key_gain: bfloat16 [4, 128], P('mp'), may hold values from 0.099609375 to 1.8984375
- partner: int32 [4], replicated, may hold values from 0 to 3, as said below
Outputs:
- grad_key: float32 [4, 5120, 512], P('mp', 'fsdp')
- grad_key_gain: float32 [4, 128], P('mp')
- distill_loss: float32 [4], P('mp')
Inputs may be any that keep to these rules, and one draw needn't show every extreme that they name: partner[m] differs from m.
All inputs are finite; a program needn't handle non-finite values.
Results may differ from a plain program's by a relative error of at most 0.0016.
Values may be sent and summed in bfloat16 or wider, within the bound.
No kernel may reach another device: no remote copies, remote signals or barrier semaphores. Data moves between devices by JAX's collectives and lax.ppermute only.
A program may use at most 128 MiB of HBM per device.

v0:
```python
import jax
import jax.numpy as jnp
from jax import lax
from jax.sharding import PartitionSpec as P


def norm_input(hidden, gain):
    values = hidden.astype(jnp.float32)
    scale = lax.rsqrt(jnp.mean(values * values, axis=-1, keepdims=True) + 1e-06)
    return (values * scale * gain.astype(jnp.float32)).astype(jnp.bfloat16)


def norm_keys(keys, gain):
    heads = keys.reshape(keys.shape[0], -1, gain.shape[0])
    inverse = lax.rsqrt(jnp.mean(heads * heads, axis=-1, keepdims=True) + 1e-06)
    return (heads, inverse, heads * inverse * gain.astype(jnp.float32))


def distill_terms(keys_student, keys_teacher, gain_student, gain_teacher):
    heads, inverse, out_student = norm_keys(keys_student, gain_student)
    unused_heads, unused_inverse, out_teacher = norm_keys(keys_teacher, gain_teacher)
    differ = out_student - out_teacher
    loss_sum = jnp.sum(differ * differ)
    upstream = differ / keys_student.shape[1]
    weighted = upstream * gain_student.astype(jnp.float32)
    inner = jnp.sum(weighted * heads, axis=-1, keepdims=True)
    grad_heads = weighted * inverse - heads * inverse * inverse * inverse * inner / heads.shape[-1]
    grad_gain = jnp.sum(upstream * heads * inverse, axis=(0, 1))
    return (loss_sum, grad_heads.reshape(keys_student.shape).astype(jnp.bfloat16), grad_gain)


def local(hidden_in, gain_in, w_key, key_gain, partner):
    own_index = lax.axis_index("mp")
    partner_index = partner[own_index]
    tok_rows = hidden_in.shape[1]
    normed_student = norm_input(hidden_in[0], gain_in[0])
    every_w, every_gain, every_key_gain = (
        lax.all_gather(w_key, "mp", axis=0, tiled=True),
        lax.all_gather(gain_in, "mp", axis=0, tiled=True),
        lax.all_gather(key_gain, "mp", axis=0, tiled=True),
    )
    teach_w = lax.dynamic_index_in_dim(every_w, partner_index, 0, keepdims=False)
    teach_gain = lax.dynamic_index_in_dim(every_gain, partner_index, 0, keepdims=False)
    teach_key_gain = lax.dynamic_index_in_dim(every_key_gain, partner_index, 0, keepdims=False)
    normed_teacher = norm_input(hidden_in[0], teach_gain)
    columns = normed_student
    keys_student = jnp.dot(
        columns,
        lax.all_gather(w_key[0], "fsdp", axis=0, tiled=True),
        preferred_element_type=jnp.float32,
    )
    columns = normed_teacher
    keys_teacher = jnp.dot(
        columns,
        lax.all_gather(teach_w, "fsdp", axis=0, tiled=True),
        preferred_element_type=jnp.float32,
    )
    loss_sum, grad_keys, grad_gain = distill_terms(
        keys_student, keys_teacher, key_gain[0], teach_key_gain
    )
    loss_total, gain_total = lax.psum((loss_sum, grad_gain), "fsdp")
    tokens_all = tok_rows * lax.axis_size("fsdp")
    distill_loss = (loss_total / (tokens_all * w_key.shape[2])).reshape(1)
    columns = normed_student
    grad_rows = lax.psum_scatter(
        lax.dot_general(
            columns, grad_keys, (((0,), (0,)), ((), ())), preferred_element_type=jnp.float32
        ),
        "fsdp",
        scatter_dimension=0,
        tiled=True,
    )
    return (grad_rows[None], gain_total[None], distill_loss)


def solution(mesh):
    return jax.shard_map(
        local,
        mesh=mesh,
        in_specs=(P("mp", "fsdp", None), P("mp", None), P("mp", "fsdp", None), P("mp", None), P()),
        out_specs=(P("mp", "fsdp", None), P("mp", None), P("mp")),
        check_vma=False,
    )
```

profile of v0, /device:TPU:0, one launch (start us, length us, event | category | flops | bytes accessed | tf_op | source)
XLA Modules:
  0.0 426.8 jit_solution(1429795895944615389)
XLA Ops:
  7.2 0.0 copy-start
  7.2 0.0 copy-start.1
  7.2 0.0 all-gather.8.cloned.1.call-start
  7.2 0.7 all-gather.8.cloned.1.call-update
  7.9 0.0 all-gather.10.cloned.1.call-start
  8.0 0.7 all-gather.10.cloned.1.call-update
  8.7 0.0 all-gather.12.cloned.1.call-start
  8.7 1.2 dynamic_slice.15
  11.9 26.0 %all-gather.8.cloned.1.call-done = bf16[4,640,512]{2,1,0:T(8,128)(2,1)} async-done(((bf16[1,640,512]{2,1,0:T(8,128)(2,1)}), bf16[4,640,512]{2,1,0:T(8,128)(2,1)}) %all-gather.8.cloned.1.call-update) | async-done | bytes 2621456 | tf_op jit(solution)/shard_map/all_gather | solution.py:38
  37.9 2.0 constant_dynamic-slice_fusion.1
  39.8 0.0 all-gather.12.cloned.1.call-update
  39.9 0.0 reduce-scatter.2.cloned.1.call-start
  39.9 0.0 copy-done
  39.9 0.0 copy-done.1
  40.0 5.0 %all-gather.3 = bf16[4,1,128]{2,1,0:T(2,128)(2,1)S(1)} all-gather(bf16[1,1,128]{2,1,0:T(2,128)(2,1)S(1)} %bitcast.52), channel_id=1, replica_groups=mesh['mp'=4,'fsdp'=8] {'mp'}, dimensions={0}, use_global_device_ids=true | all-gather | bytes 1280 | tf_op jit(solution)/shard_map/all_gather | solution.py:40
  45.0 5.3 %all-gather.2 = bf16[4,1,5120]{2,1,0:T(2,128)(2,1)S(1)} all-gather(bf16[1,1,5120]{2,1,0:T(2,128)(2,1)S(1)} %bitcast.48), channel_id=1, replica_groups=mesh['mp'=4,'fsdp'=8] {'mp'}, dimensions={0}, use_global_device_ids=true | all-gather | bytes 51200 | tf_op jit(solution)/shard_map/all_gather | solution.py:39
  50.3 4.8 %fusion.5 = f32[768]{0:T(1024)S(1)} fusion(bf16[1,768,5120]{2,1,0:T(8,128)(2,1)} %param.5), kind=kLoop, calls=%fused_computation.7 | loop fusion | flops 11795712 | bytes 7867392 | tf_op jit(solution)/shard_map/reduce_sum | solution.py:9
  55.2 71.2 %all-gather.10.cloned.1.call-done = bf16[1,5120,512]{2,1,0:T(8,128)(2,1)} async-done(((bf16[1,640,512]{2,1,0:T(8,128)(2,1)}), bf16[1,5120,512]{2,1,0:T(8,128)(2,1)}) %all-gather.10.cloned.1.call-update) | async-done | bytes 5242896 | tf_op jit(solution)/shard_map/all_gather | solution.py:49
  126.4 8.0 %copy.10 = bf16[512,5120]{1,0:T(8,128)(2,1)} copy(bf16[512,5120]{0,1:T(8,128)(2,1)} %bitcast.44) | data formatting | bytes 10485760 | tf_op jit(solution)/shard_map/dot_general | solution.py:47
  134.3 9.0 %multiply_reduce_fusion.4 = (f32[768,4]{0,1:T(4,128)S(1)}, f32[768,4,128]{0,2,1:T(8,128)S(1)}) fusion(bf16[4,128,5120]{2,1,0:T(8,128)(2,1)} %bitcast.47, f32[5120]{0:T(1024)S(1)} %bitcast.49, f32[768]{0:T(1024)S(1)} %add_rsqrt_fusion.2, bf16[1,768,5120]{2,1,0:T(8,128)(2,1)} %param.5), kind=kOutput, calls=%fused_computation.23 | convolution fusion | flops 4043043840 | bytes 14715904 | tf_op jit(solution)/shard_map/dot_general | solution.py:47
  143.3 70.3 %all-gather.12.cloned.1.call-done = bf16[1,5120,512]{2,1,0:T(8,128)(2,1)} async-done(((bf16[1,640,512]{2,1,0:T(8,128)(2,1)}), bf16[1,5120,512]{2,1,0:T(8,128)(2,1)}) %all-gather.12.cloned.1.call-update) | async-done | bytes 5242896 | tf_op jit(solution)/shard_map/all_gather | solution.py:55
  213.6 7.9 %copy.11 = bf16[512,5120]{1,0:T(8,128)(2,1)} copy(bf16[512,5120]{0,1:T(8,128)(2,1)} %bitcast.45) | data formatting | bytes 10485760 | tf_op jit(solution)/shard_map/dot_general | solution.py:53
  221.5 8.5 %multiply_reduce_fusion.3 = (f32[768,4]{0,1:T(4,128)S(1)}, f32[768,4,128]{0,2,1:T(8,128)S(1)}) fusion(bf16[4,128,5120]{2,1,0:T(8,128)(2,1)} %bitcast.46, bf16[1,768,5120]{2,1,0:T(8,128)(2,1)} %param.5, f32[5120]{0:T(1024)S(1)} %bitcast.51, f32[768]{0:T(1024)S(1)} %add_rsqrt_fusion.2), kind=kOutput, calls=%fused_computation.22 | convolution fusion | flops 4043043840 | bytes 14715904 | tf_op jit(solution)/shard_map/dot_general | solution.py:53
  230.0 1.2 subtract_convert_fusion
  231.2 11.6 %fusion.11 = f32[5120,512]{1,0:T(8,128)} fusion(bf16[768,512]{0,1:T(8,128)(2,1)S(1)} %bitcast.55, bf16[1,768,5120]{2,1,0:T(8,128)(2,1)} %param.5, f32[5120]{0:T(1024)S(1)} %bitcast.50, f32[768]{0:T(1024)S(1)} %add_rsqrt_fusion.2), kind=kOutput, calls=%fused_computation.12 | convolution fusion | flops 4042260480 | bytes 19160064 | tf_op jit(solution)/shard_map/dot_general | solution.py:66
  242.8 0.0 reduce-scatter.2.cloned.1.call-update
  242.8 1.5 multiply_reduce_fusion
  244.3 19.8 %all-reduce = (f32[1,128]{1,0:T(1,128)}, f32[]{:T(128)}) all-reduce(f32[1,128]{1,0:T(1,128)S(1)} %bitcast.53, f32[]{:T(128)} %get-tuple-element.3), channel_id=1, replica_groups=mesh['mp'=4,'fsdp'=8] {'fsdp'}, use_global_device_ids=true, to_apply=%region_6.7 | all-reduce | flops 129 | bytes 1032 | tf_op jit(solution)/shard_map/psum | solution.py:61
  264.8 154.4 %reduce-scatter.2.cloned.1.call-done = f32[640,512]{1,0:T(8,128)} async-done(((f32[5120,512]{1,0:T(8,128)}), f32[640,512]{1,0:T(8,128)}) %reduce-scatter.2.cloned.1.call-update) | async-done | bytes 1310736 | tf_op jit(solution)/shard_map/reduce_scatter | solution.py:65
  (7 shorter events, 0.1 us)
Async XLA Ops:
  7.2 32.7 %copy-start = (bf16[1,5120]{1,0:T(2,128)(2,1)S(1)}, bf16[1,5120]{1,0:T(2,128)(2,1)}, u32[]{:S(2)}) copy-start(bf16[1,5120]{1,0:T(2,128)(2,1)} %param.6) | copy-start | bytes 30724
  7.2 32.8 %copy-start.1 = (bf16[1,128]{1,0:T(2,128)(2,1)S(1)}, bf16[1,128]{1,0:T(2,128)(2,1)}, u32[]{:S(2)}) copy-start(bf16[1,128]{1,0:T(2,128)(2,1)} %param.8) | copy-start | bytes 772
  7.2 30.7 %all-gather.8.cloned.1.call-start = ((), (), s32[]{:S(2)}) async-start(), calls=%async_computation.1 | async-start | bytes 3276800 | tf_op jit(solution)/shard_map/all_gather | solution.py:38
  7.9 118.4 %all-gather.10.cloned.1.call-start = ((), (), s32[]{:S(2)}) async-start(), calls=%async_computation.3 | async-start | bytes 5898240 | tf_op jit(solution)/shard_map/all_gather | solution.py:49
  8.7 204.9 %all-gather.12.cloned.1.call-start = ((), (), s32[]{:S(2)}) async-start(), calls=%async_computation.4 | async-start | bytes 5898240 | tf_op jit(solution)/shard_map/all_gather | solution.py:55
  39.9 379.3 %reduce-scatter.2.cloned.1.call-start = ((), (), s32[]{:S(2)}) async-start(), calls=%async_computation.2 | async-start | bytes 11796480 | tf_op jit(solution)/shard_map/reduce_scatter | solution.py:65
Sparse Core Ops, SparseCore 0:
  9.6 28.2 all-gather.7
  40.0 86.2 all-gather.9
  129.1 84.4 all-gather.11
  243.0 176.1 reduce-scatter.1
where the time goes:
time: 428 us; the launch traced here: 427 us
  waiting for transfers between devices  323 us (75%)
  blocking collectives  30.1 us (7%)
  matrix products  29.2 us (7%)
  local copies, waits for them, and re-layouts  19 us (4%)
  between operations  17.6 us (4%)
  other arithmetic  7.58 us (2%)
    reduce_scatter x1, waiting for transfers between devices, local(): lax.psum_scatter(lax.dot_general(columns, grad_keys, (((0,), (0,)), ((),...  154 us
    all_gather x1, waiting for transfers between devices, local(): lax.all_gather(w_key[0], 'fsdp', axis=0, tiled=True)  71.2 us
    all_gather x1, waiting for transfers between devices, local(): lax.all_gather(teach_w, 'fsdp', axis=0, tiled=True)  70.3 us
    all_gather x1, waiting for transfers between devices, local(): lax.all_gather(w_key, 'mp', axis=0, tiled=True)  26 us
    psum x1, blocking collectives, local(): loss_total, gain_total = lax.psum((loss_sum, grad_gain), 'fsdp')  19.8 us
    dot_general x1, matrix products, local(): lax.dot_general(columns, grad_keys, (((0,), (0,)), ((), ())), preferred_e...  11.6 us
    dot_general x1, matrix products, local(): jnp.dot(columns, lax.all_gather(w_key[0], 'fsdp', axis=0, tiled=True), pr...  9 us
  transfers between devices with their start and end apart: 4, of which 4 were waited for; matrix products, arithmetic and copies ran while one was open for 6% of the time, Pallas kernels for 0%

commit v1 on v0

v1 whole, which is shorter than its diff:
```python
import functools

import jax
import jax.numpy as jnp
from jax import lax
from jax.experimental import pallas as pl
from jax.experimental.pallas import tpu as pltpu
from jax.sharding import PartitionSpec as P

EPS = 1e-06
NORM_TOKENS = 128
KEY_TOKENS = 256
VMEM_LIMIT = 24 * 1024 * 1024
ANY = pl.BlockSpec(memory_space=pl.ANY)
SMEM = pl.BlockSpec(memory_space=pltpu.SMEM)


def norm_kernel(order, rows, place_ref, hidden_ref, gain_ref, out_ref):
    values = hidden_ref[...].astype(jnp.float32)
    scale = lax.rsqrt(jnp.sum(values * values, axis=-1, keepdims=True) / values.shape[1] + EPS)
    line, member = lax.div(place_ref[0], 2), lax.rem(place_ref[0], 2)
    for at, (step, pair) in enumerate(order):
        owner = lax.rem(line + step, len(order) // 2) * 2 + lax.rem(member + pair, 2)
        source = pl.ds(pl.multiple_of(owner * rows, 128), rows)
        scaled = hidden_ref[:, source].astype(jnp.float32) * scale * gain_ref[:, source]
        out_ref[:, at * rows : (at + 1) * rows] = scaled.astype(jnp.bfloat16)


def normed_input(place, hidden, gain, order, rows):
    tokens, width = hidden.shape
    block = pl.BlockSpec((NORM_TOKENS, width), lambda i: (i, 0))
    return pl.pallas_call(
        functools.partial(norm_kernel, order, rows),
        grid=(tokens // NORM_TOKENS,),
        in_specs=[SMEM, block, pl.BlockSpec((1, width), lambda i: (0, 0))],
        out_specs=block,
        out_shape=jax.ShapeDtypeStruct(hidden.shape, jnp.bfloat16),
        compiler_params=pltpu.CompilerParams(vmem_limit_bytes=VMEM_LIMIT),
        cost_estimate=pl.CostEstimate(
            flops=6 * tokens * width, bytes_accessed=4 * tokens * width, transcendentals=tokens
        ),
        name="norm_input",
    )(place, hidden, gain)


def copy_blocks(sources, target, sems):
    copies, at = [], 0
    for i, source in enumerate(sources):
        rows = source.shape[0]
        copies.append(pltpu.make_async_copy(source, target.at[pl.ds(at, rows)], sems.at[i]))
        at += rows
    for copy in copies:
        copy.start()
    return copies


def load_weights(choice_ref, choices, target, sems):
    def load(sources):
        for copy in copy_blocks(sources, target, sems):
            copy.wait()

    if len(choices) == 1:
        load(choices[0])
    else:
        for i, sources in enumerate(choices):
            pl.when(choice_ref[0] == i)(functools.partial(load, sources))


def early_kernel(count, ways, adds, choice_ref, normed_ref, *refs):
    choices = [refs[i * count : (i + 1) * count] for i in range(ways)]
    before, (keys_ref, weights, sems) = refs[ways * count : -3], refs[-3:]

    @pl.when(pl.program_id(0) == 0)
    def _():
        load_weights(choice_ref, choices, weights, sems)

    keys = jnp.dot(normed_ref[...], weights[...], preferred_element_type=jnp.float32)
    keys_ref[...] = keys + before[0][...] if adds else keys


def early_keys(choice, normed, choices, first, before=None):
    ways, count, (rows, wide), tokens = len(choices), len(choices[0]), choices[0][0].shape, normed.shape[0]
    depth = count * rows
    keys = pl.BlockSpec((KEY_TOKENS, wide), lambda i: (i, 0))
    before = [] if before is None else [before]
    return pl.pallas_call(
        functools.partial(early_kernel, count, ways, bool(before)),
        grid=(tokens // KEY_TOKENS,),
        in_specs=[SMEM, pl.BlockSpec((KEY_TOKENS, depth), lambda i: (i, first // count))]
        + [ANY] * (ways * count)
        + [keys] * len(before),
        out_specs=keys,
        out_shape=jax.ShapeDtypeStruct((tokens, wide), jnp.float32),
        scratch_shapes=[pltpu.VMEM((depth, wide), jnp.bfloat16), pltpu.SemaphoreType.DMA((count,))],
        compiler_params=pltpu.CompilerParams(vmem_limit_bytes=VMEM_LIMIT),
        cost_estimate=pl.CostEstimate(
            flops=2 * tokens * depth * wide,
            bytes_accessed=2 * tokens * depth + 2 * depth * wide + 4 * tokens * wide,
            transcendentals=0,
        ),
        name="early_keys",
    )(choice, normed, *[block for one in choices for block in one], *before)


def late_kernel(counts, choice_ref, student_ref, teacher_ref, part_s_ref, part_t_ref, gain_s_ref, gain_t_ref, *refs):
    same, refs = refs[: counts[0]], refs[counts[0] :]
    choices, refs = [refs[i * counts[1] : (i + 1) * counts[1]] for i in range(3)], refs[3 * counts[1] :]
    grad_ref, stats_ref, w_s, w_t, sems_s, sems_t = refs
    step = pl.program_id(0)
    head, features = gain_s_ref.shape[1], part_s_ref.shape[1]

    @pl.when(step == 0)
    def _():
        load_weights(choice_ref, [same], w_s, sems_s)
        load_weights(choice_ref, choices, w_t, sems_t)

    keys_s = part_s_ref[...] + jnp.dot(student_ref[...], w_s[...], preferred_element_type=jnp.float32)
    keys_t = part_t_ref[...] + jnp.dot(teacher_ref[...], w_t[...], preferred_element_type=jnp.float32)
    gain_s, gain_t = gain_s_ref[...], gain_t_ref[...]
    gain_sum, loss_sum = 0.0, 0.0
    for at in range(0, features, head):
        heads, taught = keys_s[:, at : at + head], keys_t[:, at : at + head]
        inverse = lax.rsqrt(jnp.mean(heads * heads, axis=-1, keepdims=True) + EPS)
        inverse_t = lax.rsqrt(jnp.mean(taught * taught, axis=-1, keepdims=True) + EPS)
        differ = heads * inverse * gain_s - taught * inverse_t * gain_t
        upstream = differ * (1.0 / features)
        weighted = upstream * gain_s
        inner = jnp.sum(weighted * heads, axis=-1, keepdims=True)
        grad = weighted * inverse - heads * (inverse * inverse * inverse * inner / head)
        grad_ref[:, at : at + head] = grad.astype(jnp.bfloat16)
        gain_sum = gain_sum + jnp.sum(upstream * heads * inverse, axis=0, keepdims=True)
        loss_sum = loss_sum + jnp.sum(differ * differ, axis=0, keepdims=True)
    stats = jnp.concatenate([gain_sum, loss_sum, jnp.zeros((6, head), jnp.float32)], axis=0)

    @pl.when(step == 0)
    def _():
        stats_ref[...] = stats

    @pl.when(step != 0)
    def _():
        stats_ref[...] += stats


def late_keys(choice, student, teacher, part_s, part_t, gain_s, gain_t, same, choices, depth):
    counts, (tokens, wide), head = (len(same), len(choices[0])), part_s.shape, gain_s.shape[1]
    last = student.shape[1] // depth - 1
    token_block = pl.BlockSpec((KEY_TOKENS, depth), lambda i: (i, last))
    keys = pl.BlockSpec((KEY_TOKENS, wide), lambda i: (i, 0))
    gain = pl.BlockSpec((1, head), lambda i: (0, 0))
    return pl.pallas_call(
        functools.partial(late_kernel, counts),
        grid=(tokens // KEY_TOKENS,),
        in_specs=[SMEM, token_block, token_block, keys, keys, gain, gain] + [ANY] * (counts[0] + 3 * counts[1]),
        out_specs=[keys, pl.BlockSpec((8, head), lambda i: (0, 0))],
        out_shape=[jax.ShapeDtypeStruct((tokens, wide), jnp.bfloat16), jax.ShapeDtypeStruct((8, head), jnp.float32)],
        scratch_shapes=[pltpu.VMEM((depth, wide), jnp.bfloat16)] * 2
        + [pltpu.SemaphoreType.DMA((count,)) for count in counts],
        compiler_params=pltpu.CompilerParams(vmem_limit_bytes=VMEM_LIMIT),
        cost_estimate=pl.CostEstimate(
            flops=4 * tokens * depth * wide + 30 * tokens * wide,
            bytes_accessed=4 * tokens * depth + 4 * depth * wide + 10 * tokens * wide,
            transcendentals=2 * tokens * wide // head,
        ),
        name="late_keys",
    )(choice, student, teacher, part_s, part_t, gain_s, gain_t, *same, *[block for one in choices for block in one])


def grad_kernel(grad_ref, student_ref, out_ref):
    out_ref[0] = lax.dot_general(
        grad_ref[...], student_ref[...], (((0,), (0,)), ((), ())), preferred_element_type=jnp.float32
    ).astype(out_ref.dtype)


def grad_blocks(grad_keys, student, rows, first, stride, count, dtype):
    tokens, wide = grad_keys.shape
    return pl.pallas_call(
        grad_kernel,
        grid=(count,),
        in_specs=[
            pl.BlockSpec((tokens, wide), lambda i: (0, 0)),
            pl.BlockSpec((tokens, rows), lambda i: (0, first + stride * i)),
        ],
        out_specs=pl.BlockSpec((1, wide, rows), lambda i: (i, 0, 0)),
        out_shape=jax.ShapeDtypeStruct((count, wide, rows), dtype),
        compiler_params=pltpu.CompilerParams(vmem_limit_bytes=VMEM_LIMIT),
        cost_estimate=pl.CostEstimate(
            flops=2 * tokens * wide * rows * count,
            bytes_accessed=2 * tokens * (wide + rows * count) + 4 * count * wide * rows,
            transcendentals=0,
        ),
        name="grad_blocks",
    )(grad_keys, student)


def swap(value, axis, bit):
    return lax.ppermute(value, axis, [(i, i ^ bit) for i in range(lax.axis_size(axis))])


def fetch(value, step):
    size = lax.axis_size("fsdp")
    return lax.ppermute(value, "fsdp", [(i, (i - 2 * step) % size) for i in range(size)])


def after(value, *others):
    return lax.optimization_barrier((value,) + others)[0]


def phase(*values):
    return lax.optimization_barrier(values)


def local(hidden_in, gain_in, w_key, key_gain, partner):
    own_index = lax.axis_index("mp")
    teacher = partner[own_index]
    place = lax.axis_index("fsdp")
    lines = lax.axis_size("fsdp") // 2
    tok_rows, width = hidden_in.shape[1:]
    rows, features = w_key.shape[1:]
    head = key_gain.shape[1]

    far = lines // 2
    near = [step for step in range(1, lines) if step != far]
    order = [(0, 0), (0, 1)] + [(step, pair) for pair in range(2) for step in near] + [(far, 0), (far, 1)]
    place = place.astype(jnp.int32).reshape(1)
    own = w_key[0]

    gains_own = jnp.concatenate([gain_in, key_gain], axis=1)
    gains_beside = swap(gains_own, "mp", 2)
    gains_same = jnp.concatenate([gains_own, gains_beside], axis=0)
    gains_cross = swap(gains_same, "mp", 1)
    is_beside = teacher == own_index ^ 2
    gains_teacher = jnp.where(
        is_beside, gains_same[1:], jnp.where(teacher == own_index ^ 1, gains_cross[:1], gains_cross[1:])
    ).astype(jnp.float32)
    choice = jnp.where(is_beside, 0, jnp.where(teacher == own_index ^ 1, 1, 2)).astype(jnp.int32).reshape(1)
    same, other = {(0, 0): own}, {}
    for step in near:
        same[step, 0] = fetch(own, step)
    same[0, 1] = swap(own, "fsdp", 1)
    other[0, 0] = swap(after(own, gains_beside), "mp", 2)
    student = normed_input(place, hidden_in[0], gain_in.astype(jnp.float32), order, rows)
    other[0, 1] = swap(after(same[0, 1], student), "mp", 2)

    lead, *moved = phase(own, *[same[step, 0] for step in near], student)
    for step, block in zip(near, moved):
        same[step, 0] = block
        other[step, 0] = swap(block, "mp", 2)
        same[step, 1] = swap(block, "fsdp", 1)
    same[far, 0] = fetch(lead, far)
    hidden = after(hidden_in[0], lead)
    crossed = {}

    def cross(tables, keys):
        for table, name in tables:
            for key in keys:
                crossed[name, key] = swap(table[key], "mp", 1)

    both = ((same, "same"), (other, "other"))
    cross(both, [(0, 0), (0, 1)])
    normed = normed_input(place, hidden, gains_teacher[:, :width], order, rows)

    arrived = phase(
        same[far, 0],
        normed,
        *[same[step, 1] for step in near],
        *[other[step, 0] for step in near],
        *crossed.values(),
        other[0, 1],
    )
    same[far, 0], normed = arrived[:2]
    for i, step in enumerate(near):
        same[step, 1], other[step, 0] = arrived[2 + i], arrived[2 + len(near) + i]
    other[far, 0] = swap(same[far, 0], "mp", 2)
    same[far, 1] = swap(same[far, 0], "fsdp", 1)
    for i, step in enumerate(near):
        other[step, 1] = swap(other[step, 0], "fsdp", 1) if i % 2 == 0 else swap(same[step, 1], "mp", 2)
    cross(((same, "same"),), [(step, pair) for step in near for pair in range(2)])
    cross(((other, "other"),), [(step, 0) for step in near])

    def teachers(keys):
        return [[other[key] for key in keys]] + [[crossed[name, key] for key in keys] for name in ("same", "other")]

    part_s = early_keys(choice, student, [[same[key] for key in order[:-2]]], 0)
    part_t = early_keys(choice, normed, teachers(order[: 2 + len(near)]), 0)

    half = rows // 2
    upper = swap(after(same[far, 1][:half], part_s), "mp", 2)
    lower = swap(after(other[far, 0][half:], part_s), "fsdp", 1)
    cross(((other, "other"),), [(step, 1) for step in near])
    cross(((same, "same"),), [(far, 0), (far, 1)])
    cross(((other, "other"),), [(far, 0)])
    rest = order[2 + len(near) : -2]
    part_t = early_keys(choice, normed, teachers(rest), 2 + len(near), part_t)
    own_far = [same[far, 0], same[far, 1]]
    choices = [[other[far, 0], upper, lower], [crossed["same", (far, 0)], crossed["same", (far, 1)]]]
    choices.append([crossed["other", (far, 0)], swap(upper, "mp", 1), swap(lower, "mp", 1)])
    choices[1] = [choices[1][0], choices[1][1][:half], choices[1][1][half:]]
    grad_keys, stats = late_keys(
        choice,
        student,
        normed,
        part_s,
        part_t,
        key_gain.astype(jnp.float32),
        gains_teacher[:, width:],
        own_far,
        choices,
        2 * rows,
    )

    wide = features // 2
    at = order.index((far, 1))
    give_far = grad_blocks(grad_keys, student, rows, at, 1, 1, jnp.bfloat16)
    keep_far = grad_blocks(after(grad_keys, give_far), student, rows, at - 1, 1, 1, jnp.float32)
    given = [swap(give_far[0, i * wide : (i + 1) * wide], "fsdp", 1) for i in range(2)]
    sums = jnp.concatenate([stats[0], jnp.full((head,), jnp.sum(stats[1]))])
    bit = 2
    while bit < lax.axis_size("fsdp"):
        sums = sums + swap(sums, "fsdp", bit)
        bit *= 2
    pieces = grad_blocks(after(grad_keys, keep_far), student, rows, 2 + len(near), 1, len(near), jnp.bfloat16)
    given += [swap(after(pieces[i], given[0]), "fsdp", 1) for i in range(len(near))]
    keep = grad_blocks(after(grad_keys, pieces), student, rows, 2, 1, len(near), jnp.float32)
    ends = grad_blocks(after(grad_keys, keep), student, rows, 0, 1, 2, jnp.float32)
    last = swap(after(ends[1].astype(jnp.bfloat16), given[2]), "fsdp", 1)
    kept = [keep_far[0, i * wide : (i + 1) * wide] for i in range(2)] + [keep[i] for i in range(len(near))]
    arrived, before = [], []
    for step, mine, block in zip([far, far] + near, kept, given):
        summed = (mine + after(block, *before[-1:]).astype(jnp.float32)).astype(jnp.bfloat16)
        arrived.append(fetch(summed, -step))
        before.append(block)
    sums = sums + swap(after(sums, given[-1]), "fsdp", 1)
    total = ends[0] + last.astype(jnp.float32) + jnp.concatenate(arrived[:2], axis=0).astype(jnp.float32)
    for block in arrived[2:]:
        total = total + block.astype(jnp.float32)

    tokens_all = tok_rows * lax.axis_size("fsdp")
    distill_loss = (sums[head] / (tokens_all * features)).reshape(1)
    return (total.T[None], sums[None, :head], distill_loss)


def norm_input(hidden, gain):
    values = hidden.astype(jnp.float32)
    scale = lax.rsqrt(jnp.mean(values * values, axis=-1, keepdims=True) + EPS)
    return (values * scale * gain.astype(jnp.float32)).astype(jnp.bfloat16)


def norm_keys(keys, gain):
    heads = keys.reshape(keys.shape[0], -1, gain.shape[0])
    inverse = lax.rsqrt(jnp.mean(heads * heads, axis=-1, keepdims=True) + EPS)
    return (heads, inverse, heads * inverse * gain.astype(jnp.float32))


def plain(hidden_in, gain_in, w_key, key_gain, partner):
    partner_index = partner[lax.axis_index("mp")]
    every = [lax.all_gather(array, "mp", axis=0, tiled=True) for array in (w_key, gain_in, key_gain)]
    teach_w, teach_gain, teach_key_gain = [
        lax.dynamic_index_in_dim(array, partner_index, 0, keepdims=False) for array in every
    ]
    normed_student = norm_input(hidden_in[0], gain_in[0])
    normed_teacher = norm_input(hidden_in[0], teach_gain)
    keys_student, keys_teacher = [
        jnp.dot(normed, lax.all_gather(weight, "fsdp", axis=0, tiled=True), preferred_element_type=jnp.float32)
        for normed, weight in ((normed_student, w_key[0]), (normed_teacher, teach_w))
    ]
    heads, inverse, out_student = norm_keys(keys_student, key_gain[0])
    differ = out_student - norm_keys(keys_teacher, teach_key_gain)[2]
    upstream = differ / w_key.shape[2]
    weighted = upstream * key_gain[0].astype(jnp.float32)
    inner = jnp.sum(weighted * heads, axis=-1, keepdims=True)
    grad_heads = weighted * inverse - heads * inverse * inverse * inverse * inner / heads.shape[-1]
    grad_keys = grad_heads.reshape(keys_student.shape).astype(jnp.bfloat16)
    grad_gain = jnp.sum(upstream * heads * inverse, axis=(0, 1))
    loss_total, gain_total = lax.psum((jnp.sum(differ * differ), grad_gain), "fsdp")
    tokens_all = hidden_in.shape[1] * lax.axis_size("fsdp")
    grad = lax.dot_general(
        normed_student, grad_keys, (((0,), (0,)), ((), ())), preferred_element_type=jnp.float32
    )
    grad_rows = lax.psum_scatter(grad, "fsdp", scatter_dimension=0, tiled=True)
    distill_loss = (loss_total / (tokens_all * w_key.shape[2])).reshape(1)
    return (grad_rows[None], gain_total[None], distill_loss)


def step(hidden_in, gain_in, w_key, key_gain, partner):
    body = plain if w_key.shape[1] % 128 else local
    return body(hidden_in, gain_in, w_key, key_gain, partner)


def solution(mesh):
    return jax.shard_map(
        step,
        mesh=mesh,
        in_specs=(P("mp", "fsdp", None), P("mp", None), P("mp", "fsdp", None), P("mp", None), P()),
        out_specs=(P("mp", "fsdp", None), P("mp", None), P("mp")),
        check_vma=False,
    )
```

time: 428 us -> 290 us (0.68)
  waiting for transfers between devices: 323 us -> 168 us
  starting transfers between devices: 0.16 us -> 49.4 us
  Pallas kernels: 0 us -> 34.9 us
  blocking collectives: 30.1 us -> 0 us
  matrix products: 29.2 us -> 0 us
  between operations: 17.6 us -> 4.22 us
  local copies, waits for them, and re-layouts: 19 us -> 24.9 us
    ppermute x0 -> x47, waiting for transfers between devices: none -> 168 us  [the longest x40 110 us: swap(): lax.ppermute(value, axis, [(i, i ^ bit) for i in range(lax.axis_size(axis...]
    all_gather x3 -> x0, waiting for transfers between devices: 167 us -> none  [the longest x1 71.2 us: local(): lax.all_gather(w_key[0], 'fsdp', axis=0, tiled=True)]
    reduce_scatter x1 -> x0, waiting for transfers between devices: 154 us -> none  [local(): lax.psum_scatter(lax.dot_general(columns, grad_keys, (((0,), (0,)), ((),...]
    ppermute x0 -> x47, starting transfers between devices: none -> 49.4 us  [the longest x40 26.9 us: swap(): lax.ppermute(value, axis, [(i, i ^ bit) for i in range(lax.axis_size(axis...]
    pallas_call x0 -> x11, Pallas kernels: none -> 34.9 us  [the longest x3 13.9 us: early_keys(): pl.pallas_call(functools.partial(early_kernel, count, ways, bool(before))...]
    dot_general x3 -> x0, matrix products: 29.2 us -> none  [the longest x1 11.6 us: local(): lax.dot_general(columns, grad_keys, (((0,), (0,)), ((), ())), preferred_e...]
    unnamed x4 -> x59, local copies, waits for them, and re-layouts: 0.01 us -> 22.4 us
    psum x1 -> x0, blocking collectives: 19.8 us -> none  [local(): loss_total, gain_total = lax.psum((loss_sum, grad_gain), 'fsdp')]
  transfers between devices with their start and end apart: 4 -> 47, of which waited for: 4 -> 20; matrix products, arithmetic and copies ran while one was open for 6% -> 2% of each run, Pallas kernels for 0% -> 10%
where the time goes in v1:
time: 290 us; the launch traced here: 285 us
  waiting for transfers between devices  168 us (58%)
  starting transfers between devices  49.4 us (17%)
  Pallas kernels  34.9 us (12%)
  local copies, waits for them, and re-layouts  24.9 us (9%)
  between operations  4.22 us (1%)
  other arithmetic  3.69 us (1%)
    ppermute x40, waiting for transfers between devices, swap(): lax.ppermute(value, axis, [(i, i ^ bit) for i in range(lax.axis_size(axis...  110 us
    ppermute x7, waiting for transfers between devices, fetch(): lax.ppermute(value, 'fsdp', [(i, (i - 2 * step) % size) for i in range(si...  58.4 us
    ppermute x40, starting transfers between devices, swap(): lax.ppermute(value, axis, [(i, i ^ bit) for i in range(lax.axis_size(axis...  26.9 us
    ppermute x7, starting transfers between devices, fetch(): lax.ppermute(value, 'fsdp', [(i, (i - 2 * step) % size) for i in range(si...  22.6 us
    unnamed x59, local copies, waits for them, and re-layouts  22.4 us
    pallas_call x3, Pallas kernels, early_keys(): pl.pallas_call(functools.partial(early_kernel, count, ways, bool(before))...  13.9 us
    pallas_call x2, Pallas kernels, normed_input(): pl.pallas_call(functools.partial(norm_kernel, order, rows), grid=(tokens...  8.6 us
    pallas_call x5, Pallas kernels, grad_blocks(): pl.pallas_call(grad_kernel, grid=(count,), in_specs=[pl.BlockSpec((tokens...  7.28 us
  transfers between devices with their start and end apart: 47, of which 20 were waited for; matrix products, arithmetic and copies ran while one was open for 2% of the time, Pallas kernels for 10%

profile of v1, /device:TPU:0, one launch (start us, length us, event | category | flops | bytes accessed | tf_op | source)
XLA Modules:
  0.0 285.3 jit_solution(9391669219921651804)
XLA Ops:
  0.6 3.0 %collective-permute-start.10 = (bf16[640,512]{1,0:T(8,128)(2,1)}, bf16[640,512]{1,0:T(8,128)(2,1)}, u32[]{:S(2)}, u32[]{:S(2)}) collective-permute-start(bf16[640,512]{1,0:T(8,128)(2,1)} %bitcast.4.refs_0_), channel_id=1, source_target_pairs={{0,1},{1,0},{2,3},{3,2},{4,5},{5,4},{6,7},{7,6},{8,9},{9,8},{10,11... | collective-permute-start | bytes 1966088 | tf_op jit(solution)/shard_map/ppermute | solution.py:196
  8.3 2.2 collective-permute-start
  11.1 7.6 %collective-permute-done.10.refs_1_ = bf16[640,512]{1,0:T(8,128)(2,1)} collective-permute-done((bf16[640,512]{1,0:T(8,128)(2,1)}, bf16[640,512]{1,0:T(8,128)(2,1)}, u32[]{:S(2)}, u32[]{:S(2)}) %collective-permute-start.10) | collective-permute-done | bytes 655392 | tf_op jit(solution)/shard_map/ppermute | solution.py:196
  18.8 7.7 %collective-permute-done.1.refs_3_ = bf16[640,512]{1,0:T(8,128)(2,1)} collective-permute-done((bf16[640,512]{1,0:T(8,128)(2,1)}, bf16[640,512]{1,0:T(8,128)(2,1)}, u32[]{:S(2)}, u32[]{:S(2)}) %collective-permute-start.1) | collective-permute-done | bytes 655392 | tf_op jit(solution)/shard_map/ppermute | solution.py:201
  26.4 3.2 %copy-done.4 = bf16[1,768,5120]{2,1,0:T(8,128)(2,1)S(1)} copy-done((bf16[1,768,5120]{2,1,0:T(8,128)(2,1)S(1)}, bf16[1,768,5120]{2,1,0:T(8,128)(2,1)}, u32[]{:S(2)}) %copy-start.4) | copy-done | bytes 7864344
  29.7 4.3 %norm_input.2.normed_ref.student_ref = bf16[768,5120]{1,0:T(8,128)(2,1)S(1)} custom-call(s32[1]{0:T(128)} %bitcast.2.place_ref, bf16[768,5120]{1,0:T(8,128)(2,1)S(1)} %bitcast.61, f32[1,5120]{1,0:T(1,128)S(1)} %get-tuple-element.71.gain_ref), custom_call_target="tpu_custom_call" | custom-call | flops 23592960 | bytes 15728640 | tf_op jit(solution)/shard_map/norm_input/pallas_call | solution.py:32
  34.0 3.1 %copy-done = bf16[768,5120]{1,0:T(8,128)(2,1)} copy-done((bf16[768,5120]{1,0:T(8,128)(2,1)}, bf16[768,5120]{1,0:T(8,128)(2,1)S(1)}, u32[]{:S(2)}) %copy-start) | copy-done | bytes 7864344
  37.1 2.4 collective-permute-done.refs_2_
  39.5 12.0 %collective-permute-start.2 = (bf16[640,512]{1,0:T(8,128)(2,1)}, bf16[640,512]{1,0:T(8,128)(2,1)S(1)}, u32[]{:S(2)}, u32[]{:S(2)}) collective-permute-start(bf16[640,512]{1,0:T(8,128)(2,1)} %bitcast.4.refs_0_), channel_id=1, source_target_pairs={{0,4},{1,5},{2,6},{3,7},{4,0},{5,1},{6,2},{7,3},{8,12},{9,13},{10,... | collective-permute-start | bytes 1966088 | tf_op jit(solution)/shard_map/ppermute | solution.py:201
  56.5 24.7 %collective-permute-done.2.refs_0_ = bf16[640,512]{1,0:T(8,128)(2,1)S(1)} collective-permute-done((bf16[640,512]{1,0:T(8,128)(2,1)}, bf16[640,512]{1,0:T(8,128)(2,1)S(1)}, u32[]{:S(2)}, u32[]{:S(2)}) %collective-permute-start.2) | collective-permute-done | bytes 655392 | tf_op jit(solution)/shard_map/ppermute | solution.py:201
  83.4 13.4 %collective-permute-done.14.refs_1_ = bf16[640,512]{1,0:T(8,128)(2,1)} collective-permute-done((bf16[640,512]{1,0:T(8,128)(2,1)}, bf16[640,512]{1,0:T(8,128)(2,1)}, u32[]{:S(2)}, u32[]{:S(2)}) %collective-permute-start.14) | collective-permute-done | bytes 655392 | tf_op jit(solution)/shard_map/ppermute | solution.py:196
  96.9 3.2 %copy-done.5 = bf16[1,768,5120]{2,1,0:T(8,128)(2,1)S(1)} copy-done((bf16[1,768,5120]{2,1,0:T(8,128)(2,1)S(1)}, bf16[1,768,5120]{2,1,0:T(8,128)(2,1)}, u32[]{:S(2)}) %copy-start.5) | copy-done | bytes 7864344
  100.1 4.3 %norm_input.3.normed_ref.teacher_ref = bf16[768,5120]{1,0:T(8,128)(2,1)S(1)} custom-call(s32[1]{0:T(128)} %bitcast.2.place_ref, bf16[768,5120]{1,0:T(8,128)(2,1)S(1)} %bitcast.62, f32[1,5120]{1,0:T(1,128)S(1)} %slice.91.gain_ref), custom_call_target="tpu_custom_call" | custom-call | flops 23592960 | bytes 15728640 | tf_op jit(solution)/shard_map/norm_input/pallas_call | solution.py:32
  104.5 3.1 %copy-done.2 = bf16[768,5120]{1,0:T(8,128)(2,1)} copy-done((bf16[768,5120]{1,0:T(8,128)(2,1)}, bf16[768,5120]{1,0:T(8,128)(2,1)S(1)}, u32[]{:S(2)}) %copy-start.2) | copy-done | bytes 7864344
  116.5 11.3 %collective-permute-done.17.refs_1_ = bf16[640,512]{1,0:T(8,128)(2,1)} collective-permute-done((bf16[640,512]{1,0:T(8,128)(2,1)}, bf16[640,512]{1,0:T(8,128)(2,1)}, u32[]{:S(2)}, u32[]{:S(2)}) %collective-permute-start.17) | collective-permute-done | bytes 655392 | tf_op jit(solution)/shard_map/ppermute | solution.py:196
  128.3 12.4 %collective-permute-done.27.refs_2_ = bf16[640,512]{1,0:T(8,128)(2,1)S(1)} collective-permute-done((bf16[640,512]{1,0:T(8,128)(2,1)S(1)}, bf16[640,512]{1,0:T(8,128)(2,1)S(1)}, u32[]{:S(2)}, u32[]{:S(2)}) %collective-permute-start.27) | collective-permute-done | bytes 655392 | tf_op jit(solution)/shard_map/ppermute | solution.py:196
  141.8 3.2 %copy-done.1 = bf16[768,5120]{1,0:T(8,128)(2,1)S(1)} copy-done((bf16[768,5120]{1,0:T(8,128)(2,1)S(1)}, bf16[768,5120]{1,0:T(8,128)(2,1)}, u32[]{:S(2)}) %copy-start.1) | copy-done | bytes 7864344
  145.1 6.3 %early_keys.3.part_s_ref = f32[768,512]{1,0:T(8,128)S(1)} custom-call(s32[1]{0:T(128)} %bitcast.1.choice_ref, bf16[768,5120]{1,0:T(8,128)(2,1)S(1)} %copy-done.1, bf16[640,512]{1,0:T(8,128)(2,1)} %bitcast.4.refs_0_, bf16[640,512]{1,0:T(8,128)(2,1)} %collective-permute-done.10.refs_1_, bf16[640,512]{1,0:T(8,128)(2,1)} %collective-permute-done.refs_2_, ...), custom_call_target="tpu_custom_call" | custom-call | flops 3019898880 | bytes 11403264 | tf_op jit(solution)/shard_map/early_keys/pallas_call | solution.py:86
  153.5 7.9 %collective-permute-done.29.refs_4_ = bf16[320,512]{1,0:T(8,128)(2,1)S(1)} collective-permute-done((bf16[320,512]{1,0:T(8,128)(2,1)S(1)}, bf16[320,512]{1,0:T(8,128)(2,1)S(1)}, u32[]{:S(2)}, u32[]{:S(2)}) %collective-permute-start.29) | collective-permute-done | bytes 327712 | tf_op jit(solution)/shard_map/ppermute | solution.py:196
  162.0 4.7 %early_keys.4.refs_6_ = f32[768,512]{1,0:T(8,128)S(1)} custom-call(s32[1]{0:T(128)} %bitcast.1.choice_ref, bf16[768,5120]{1,0:T(8,128)(2,1)S(1)} %copy-done.3, bf16[640,512]{1,0:T(8,128)(2,1)S(1)} %copy-done.13, bf16[640,512]{1,0:T(8,128)(2,1)} %collective-permute-done.14.refs_1_, bf16[640,512]{1,0:T(8,128)(2,1)} %collective-permute-done.7.refs_2_, ...), custom_call_target="tpu_custom_call" | custom-call | flops 2013265920 | bytes 8126464 | tf_op jit(solution)/shard_map/early_keys/pallas_call | solution.py:86
  167.4 3.0 %early_keys.5.part_t_ref = f32[768,512]{1,0:T(8,128)S(1)} custom-call(s32[1]{0:T(128)} %bitcast.1.choice_ref, bf16[768,5120]{1,0:T(8,128)(2,1)S(1)} %copy-done.3, bf16[640,512]{1,0:T(8,128)(2,1)} %collective-permute-done.16.refs_0_, bf16[640,512]{1,0:T(8,128)(2,1)} %collective-permute-done.17.refs_1_, bf16[640,512]{1,0:T(8,128)(2,1)S(1)} %copy-done.25, ...), custom_call_target="tpu_custom_call" | custom-call | flops 1006632960 | bytes 4849664 | tf_op jit(solution)/shard_map/early_keys/pallas_call | solution.py:86
  170.5 5.1 %late_keys.1 = (bf16[768,512]{1,0:T(8,128)(2,1)S(1)}, f32[8,128]{1,0:T(8,128)S(1)}) custom-call(s32[1]{0:T(128)} %bitcast.1.choice_ref, bf16[768,5120]{1,0:T(8,128)(2,1)S(1)} %bitcast.60, bf16[768,5120]{1,0:T(8,128)(2,1)S(1)} %copy-done.3, f32[768,512]{1,0:T(8,128)S(1)} %early_keys.3.part_s_ref, f32[768,512]{1,0:T(8,128)S(1)} %early_keys.5.part_t_ref, ...), custom_call_target="tpu_custom_call" | custom-call | flops 2025062400 | bytes 10485760 | tf_op jit(solution)/shard_map/late_keys/pallas_call | solution.py:150
  179.0 1.9 grad_blocks.7
  181.0 4.8 %collective-permute-done.35 = bf16[256,640]{1,0:T(8,128)(2,1)S(1)} collective-permute-done((bf16[256,640]{1,0:T(8,128)(2,1)S(1)}, bf16[256,640]{1,0:T(8,128)(2,1)S(1)}, u32[]{:S(2)}, u32[]{:S(2)}) %collective-permute-start.35) | collective-permute-done | bytes 327712 | tf_op jit(solution)/shard_map/ppermute | solution.py:196
  194.1 1.9 grad_blocks.9
  196.1 7.4 %collective-permute-done.42 = bf16[512,640]{1,0:T(8,128)(2,1)S(1)} collective-permute-done((bf16[512,640]{1,0:T(8,128)(2,1)S(1)}, bf16[512,640]{1,0:T(8,128)(2,1)S(1)}, u32[]{:S(2)}, u32[]{:S(2)}) %collective-permute-start.42) | collective-permute-done | bytes 655392 | tf_op jit(solution)/shard_map/ppermute | solution.py:196
  203.5 14.0 %collective-permute-done.36 = bf16[512,640]{1,0:T(8,128)(2,1)S(1)} collective-permute-done((bf16[512,640]{1,0:T(8,128)(2,1)S(1)}, bf16[512,640]{1,0:T(8,128)(2,1)S(1)}, u32[]{:S(2)}, u32[]{:S(2)}) %collective-permute-start.36) | collective-permute-done | bytes 655392 | tf_op jit(solution)/shard_map/ppermute | solution.py:196
  217.5 4.7 %collective-permute-done.39 = bf16[256,640]{1,0:T(8,128)(2,1)S(1)} collective-permute-done((bf16[256,640]{1,0:T(8,128)(2,1)S(1)}, bf16[256,640]{1,0:T(8,128)(2,1)S(1)}, u32[]{:S(2)}, u32[]{:S(2)}) %collective-permute-start.39) | collective-permute-done | bytes 327712 | tf_op jit(solution)/shard_map/ppermute | solution.py:196
  224.1 2.2 collective-permute-start.43
  228.5 23.5 %collective-permute-done.45 = f32[256]{0:T(256)S(1)} collective-permute-done((f32[256]{0:T(256)S(1)}, f32[256]{0:T(256)S(1)}, u32[]{:S(2)}, u32[]{:S(2)}) %collective-permute-start.45) | collective-permute-done | bytes 1056 | tf_op jit(solution)/shard_map/ppermute | solution.py:196
  258.6 16.7 %collective-permute-done.38 = bf16[256,640]{1,0:T(8,128)(2,1)S(1)} collective-permute-done((bf16[256,640]{1,0:T(8,128)(2,1)S(1)}, bf16[256,640]{1,0:T(8,128)(2,1)S(1)}, u32[]{:S(2)}, u32[]{:S(2)}) %collective-permute-start.38) | collective-permute-done | bytes 327712 | tf_op jit(solution)/shard_map/ppermute | solution.py:201
  275.4 6.9 %collective-permute-done.40 = bf16[256,640]{1,0:T(8,128)(2,1)S(1)} collective-permute-done((bf16[256,640]{1,0:T(8,128)(2,1)S(1)}, bf16[256,640]{1,0:T(8,128)(2,1)S(1)}, u32[]{:S(2)}, u32[]{:S(2)}) %collective-permute-start.40) | collective-permute-done | bytes 327712 | tf_op jit(solution)/shard_map/ppermute | solution.py:201
  (156 shorter events, 48.9 us)
Async XLA Ops:
  0.6 18.1 %collective-permute-start.10 = (bf16[640,512]{1,0:T(8,128)(2,1)}, bf16[640,512]{1,0:T(8,128)(2,1)}, u32[]{:S(2)}, u32[]{:S(2)}) collective-permute-start(bf16[640,512]{1,0:T(8,128)(2,1)} %bitcast.4.refs_0_), channel_id=1, source_target_pairs={{0,1},{1,0},{2,3},{3,2},{4,5},{5,4},{6,7},{7,6},{8,9},{9,8},{10,11... | collective-permute-start | bytes 1966088 | tf_op jit(solution)/shard_map/ppermute | solution.py:196
  6.7 45.3 %collective-permute-start.9 = (bf16[640,512]{1,0:T(8,128)(2,1)}, bf16[640,512]{1,0:T(8,128)(2,1)S(1)}, u32[]{:S(2)}, u32[]{:S(2)}) collective-permute-start(bf16[640,512]{1,0:T(8,128)(2,1)} %bitcast.4.refs_0_), channel_id=1, source_target_pairs={{0,8},{8,0},{16,24},{24,16},{1,9},{9,1},{17,25},{25,17},{2,10},{10... | collective-permute-start | bytes 1966088 | tf_op jit(solution)/shard_map/ppermute | solution.py:196
  6.7 19.7 %collective-permute-start.1 = (bf16[640,512]{1,0:T(8,128)(2,1)}, bf16[640,512]{1,0:T(8,128)(2,1)}, u32[]{:S(2)}, u32[]{:S(2)}) collective-permute-start(bf16[640,512]{1,0:T(8,128)(2,1)} %bitcast.4.refs_0_), channel_id=1, source_target_pairs={{0,2},{1,3},{2,4},{3,5},{4,6},{5,7},{6,0},{7,1},{8,10},{9,11},{10,... | collective-permute-start | bytes 1966088 | tf_op jit(solution)/shard_map/ppermute | solution.py:201
  8.3 31.2 %collective-permute-start = (bf16[640,512]{1,0:T(8,128)(2,1)}, bf16[640,512]{1,0:T(8,128)(2,1)}, u32[]{:S(2)}, u32[]{:S(2)}) collective-permute-start(bf16[640,512]{1,0:T(8,128)(2,1)} %bitcast.4.refs_0_), channel_id=1, source_target_pairs={{0,6},{1,7},{2,0},{3,1},{4,2},{5,3},{6,4},{7,5},{8,14},{9,15},{10,... | collective-permute-start | bytes 1966088 | tf_op jit(solution)/shard_map/ppermute | solution.py:201
  10.6 42.0 %collective-permute-start.12 = (bf16[640,512]{1,0:T(8,128)(2,1)}, bf16[640,512]{1,0:T(8,128)(2,1)S(1)}, u32[]{:S(2)}, u32[]{:S(2)}) collective-permute-start(bf16[640,512]{1,0:T(8,128)(2,1)} %bitcast.4.refs_0_), channel_id=1, source_target_pairs={{0,16},{8,24},{16,0},{24,8},{1,17},{9,25},{17,1},{25,9},{2,18},{10... | collective-permute-start | bytes 1966088 | tf_op jit(solution)/shard_map/ppermute | solution.py:196
  18.7 35.4 %collective-permute-start.11 = (bf16[640,512]{1,0:T(8,128)(2,1)}, bf16[640,512]{1,0:T(8,128)(2,1)S(1)}, u32[]{:S(2)}, u32[]{:S(2)}) collective-permute-start(bf16[640,512]{1,0:T(8,128)(2,1)} %collective-permute-done.10.refs_1_), channel_id=1, source_target_pairs={{0,8},{8,0},{16,24},{24,16},{1,9},{9,1},{17,25},{25,17},{2,10},{10... | collective-permute-start | bytes 1966088 | tf_op jit(solution)/shard_map/ppermute | solution.py:196
  26.4 25.1 %collective-permute-start.4 = (bf16[2,5248]{1,0:T(2,128)(2,1)S(1)}, bf16[2,5248]{1,0:T(2,128)(2,1)S(1)}, u32[]{:S(2)}, u32[]{:S(2)}) collective-permute-start(bf16[2,5248]{1,0:T(2,128)(2,1)S(1)} %pad_maximum_fusion), channel_id=1, source_target_pairs={{0,8},{8,0},{16,24},{24,16},{1,9},{9,1},{17,25},{25,17},{2,10},{10... | collective-permute-start | bytes 62984 | tf_op jit(solution)/shard_map/ppermute | solution.py:196
  39.5 41.6 %collective-permute-start.2 = (bf16[640,512]{1,0:T(8,128)(2,1)}, bf16[640,512]{1,0:T(8,128)(2,1)S(1)}, u32[]{:S(2)}, u32[]{:S(2)}) collective-permute-start(bf16[640,512]{1,0:T(8,128)(2,1)} %bitcast.4.refs_0_), channel_id=1, source_target_pairs={{0,4},{1,5},{2,6},{3,7},{4,0},{5,1},{6,2},{7,3},{8,12},{9,13},{10,... | collective-permute-start | bytes 1966088 | tf_op jit(solution)/shard_map/ppermute | solution.py:201
  51.5 29.7 %collective-permute-start.7 = (bf16[640,512]{1,0:T(8,128)(2,1)}, bf16[640,512]{1,0:T(8,128)(2,1)}, u32[]{:S(2)}, u32[]{:S(2)}) collective-permute-start(bf16[640,512]{1,0:T(8,128)(2,1)} %collective-permute-done.refs_2_), channel_id=1, source_target_pairs={{0,16},{8,24},{16,0},{24,8},{1,17},{9,25},{17,1},{25,9},{2,18},{10... | collective-permute-start | bytes 1966088 | tf_op jit(solution)/shard_map/ppermute | solution.py:196
  52.1 29.6 %collective-permute-start.5 = (bf16[640,512]{1,0:T(8,128)(2,1)}, bf16[640,512]{1,0:T(8,128)(2,1)}, u32[]{:S(2)}, u32[]{:S(2)}) collective-permute-start(bf16[640,512]{1,0:T(8,128)(2,1)} %collective-permute-done.refs_2_), channel_id=1, source_target_pairs={{0,1},{1,0},{2,3},{3,2},{4,5},{5,4},{6,7},{7,6},{8,9},{9,8},{10,11... | collective-permute-start | bytes 1966088 | tf_op jit(solution)/shard_map/ppermute | solution.py:196
  52.6 30.8 %collective-permute-start.8 = (bf16[640,512]{1,0:T(8,128)(2,1)}, bf16[640,512]{1,0:T(8,128)(2,1)S(1)}, u32[]{:S(2)}, u32[]{:S(2)}) collective-permute-start(bf16[640,512]{1,0:T(8,128)(2,1)} %collective-permute-done.1.refs_3_), channel_id=1, source_target_pairs={{0,16},{8,24},{16,0},{24,8},{1,17},{9,25},{17,1},{25,9},{2,18},{10... | collective-permute-start | bytes 1966088 | tf_op jit(solution)/shard_map/ppermute | solution.py:196
  54.1 42.7 %collective-permute-start.14 = (bf16[640,512]{1,0:T(8,128)(2,1)}, bf16[640,512]{1,0:T(8,128)(2,1)}, u32[]{:S(2)}, u32[]{:S(2)}) collective-permute-start(bf16[640,512]{1,0:T(8,128)(2,1)} %collective-permute-done.10.refs_1_), channel_id=1, source_target_pairs={{0,16},{8,24},{16,0},{24,8},{1,17},{9,25},{17,1},{25,9},{2,18},{10... | collective-permute-start | bytes 1966088 | tf_op jit(solution)/shard_map/ppermute | solution.py:196
  81.2 29.7 %collective-permute-start.22 = (bf16[640,512]{1,0:T(8,128)(2,1)}, bf16[640,512]{1,0:T(8,128)(2,1)S(1)}, u32[]{:S(2)}, u32[]{:S(2)}) collective-permute-start(bf16[640,512]{1,0:T(8,128)(2,1)} %collective-permute-done.refs_2_), channel_id=1, source_target_pairs={{0,8},{8,0},{16,24},{24,16},{1,9},{9,1},{17,25},{25,17},{2,10},{10... | collective-permute-start | bytes 1966088 | tf_op jit(solution)/shard_map/ppermute | solution.py:196
  81.2 32.0 %collective-permute-start.23 = (bf16[640,512]{1,0:T(8,128)(2,1)}, bf16[640,512]{1,0:T(8,128)(2,1)S(1)}, u32[]{:S(2)}, u32[]{:S(2)}) collective-permute-start(bf16[640,512]{1,0:T(8,128)(2,1)} %collective-permute-done.1.refs_3_), channel_id=1, source_target_pairs={{0,8},{8,0},{16,24},{24,16},{1,9},{9,1},{17,25},{25,17},{2,10},{10... | collective-permute-start | bytes 1966088 | tf_op jit(solution)/shard_map/ppermute | solution.py:196
  81.7 25.8 %collective-permute-start.6 = (bf16[640,512]{1,0:T(8,128)(2,1)}, bf16[640,512]{1,0:T(8,128)(2,1)}, u32[]{:S(2)}, u32[]{:S(2)}) collective-permute-start(bf16[640,512]{1,0:T(8,128)(2,1)} %collective-permute-done.1.refs_3_), channel_id=1, source_target_pairs={{0,1},{1,0},{2,3},{3,2},{4,5},{5,4},{6,7},{7,6},{8,9},{9,8},{10,11... | collective-permute-start | bytes 1966088 | tf_op jit(solution)/shard_map/ppermute | solution.py:196
  83.4 24.2 %collective-permute-start.13 = (bf16[640,512]{1,0:T(8,128)(2,1)S(1)}, bf16[640,512]{1,0:T(8,128)(2,1)S(1)}, u32[]{:S(2)}, u32[]{:S(2)}) collective-permute-start(bf16[640,512]{1,0:T(8,128)(2,1)S(1)} %collective-permute-done.12.refs_0_), channel_id=1, source_target_pairs={{0,8},{8,0},{16,24},{24,16},{1,9},{9,1},{17,25},{25,17},{2,10},{10... | collective-permute-start | bytes 1966088 | tf_op jit(solution)/shard_map/ppermute | solution.py:196
  111.7 29.0 %collective-permute-start.27 = (bf16[640,512]{1,0:T(8,128)(2,1)S(1)}, bf16[640,512]{1,0:T(8,128)(2,1)S(1)}, u32[]{:S(2)}, u32[]{:S(2)}) collective-permute-start(bf16[640,512]{1,0:T(8,128)(2,1)S(1)} %collective-permute-done.2.refs_0_), channel_id=1, source_target_pairs={{0,16},{8,24},{16,0},{24,8},{1,17},{9,25},{17,1},{25,9},{2,18},{10... | collective-permute-start | bytes 1966088 | tf_op jit(solution)/shard_map/ppermute | solution.py:196
  114.1 26.9 %collective-permute-start.26 = (bf16[640,512]{1,0:T(8,128)(2,1)S(1)}, bf16[640,512]{1,0:T(8,128)(2,1)S(1)}, u32[]{:S(2)}, u32[]{:S(2)}) collective-permute-start(bf16[640,512]{1,0:T(8,128)(2,1)S(1)} %collective-permute-done.2.refs_0_), channel_id=1, source_target_pairs={{0,1},{1,0},{2,3},{3,2},{4,5},{5,4},{6,7},{7,6},{8,9},{9,8},{10,11... | collective-permute-start | bytes 1966088 | tf_op jit(solution)/shard_map/ppermute | solution.py:196
  116.5 35.0 %collective-permute-start.25 = (bf16[640,512]{1,0:T(8,128)(2,1)S(1)}, bf16[640,512]{1,0:T(8,128)(2,1)}, u32[]{:S(2)}, u32[]{:S(2)}) collective-permute-start(bf16[640,512]{1,0:T(8,128)(2,1)S(1)} %collective-permute-done.8.refs_3_), channel_id=1, source_target_pairs={{0,8},{8,0},{16,24},{24,16},{1,9},{9,1},{17,25},{25,17},{2,10},{10... | collective-permute-start | bytes 1966088 | tf_op jit(solution)/shard_map/ppermute | solution.py:196
  127.7 24.3 %collective-permute-start.19 = (bf16[640,512]{1,0:T(8,128)(2,1)}, bf16[640,512]{1,0:T(8,128)(2,1)}, u32[]{:S(2)}, u32[]{:S(2)}) collective-permute-start(bf16[640,512]{1,0:T(8,128)(2,1)} %collective-permute-done.6.refs_5_), channel_id=1, source_target_pairs={{0,8},{8,0},{16,24},{24,16},{1,9},{9,1},{17,25},{25,17},{2,10},{10... | collective-permute-start | bytes 1966088 | tf_op jit(solution)/shard_map/ppermute | solution.py:196
  128.3 25.2 %collective-permute-start.24 = (bf16[640,512]{1,0:T(8,128)(2,1)}, bf16[640,512]{1,0:T(8,128)(2,1)}, u32[]{:S(2)}, u32[]{:S(2)}) collective-permute-start(bf16[640,512]{1,0:T(8,128)(2,1)} %collective-permute-done.7.refs_2_), channel_id=1, source_target_pairs={{0,8},{8,0},{16,24},{24,16},{1,9},{9,1},{17,25},{25,17},{2,10},{10... | collective-permute-start | bytes 1966088 | tf_op jit(solution)/shard_map/ppermute | solution.py:196
  140.7 26.0 %collective-permute-start.21 = (bf16[640,512]{1,0:T(8,128)(2,1)}, bf16[640,512]{1,0:T(8,128)(2,1)S(1)}, u32[]{:S(2)}, u32[]{:S(2)}) collective-permute-start(bf16[640,512]{1,0:T(8,128)(2,1)} %collective-permute-done.17.refs_1_), channel_id=1, source_target_pairs={{0,8},{8,0},{16,24},{24,16},{1,9},{9,1},{17,25},{25,17},{2,10},{10... | collective-permute-start | bytes 1966088 | tf_op jit(solution)/shard_map/ppermute | solution.py:196
  141.0 26.3 %collective-permute-start.20 = (bf16[640,512]{1,0:T(8,128)(2,1)}, bf16[640,512]{1,0:T(8,128)(2,1)S(1)}, u32[]{:S(2)}, u32[]{:S(2)}) collective-permute-start(bf16[640,512]{1,0:T(8,128)(2,1)} %collective-permute-done.16.refs_0_), channel_id=1, source_target_pairs={{0,8},{8,0},{16,24},{24,16},{1,9},{9,1},{17,25},{25,17},{2,10},{10... | collective-permute-start | bytes 1966088 | tf_op jit(solution)/shard_map/ppermute | solution.py:196
  187.3 30.2 %collective-permute-start.36 = (bf16[512,640]{1,0:T(8,128)(2,1)S(1)}, bf16[512,640]{1,0:T(8,128)(2,1)S(1)}, u32[]{:S(2)}, u32[]{:S(2)}) collective-permute-start(bf16[512,640]{1,0:T(8,128)(2,1)S(1)} %get-tuple-element.49), channel_id=1, source_target_pairs={{0,1},{1,0},{2,3},{3,2},{4,5},{5,4},{6,7},{7,6},{8,9},{9,8},{10,11... | collective-permute-start | bytes 1966088 | tf_op jit(solution)/shard_map/ppermute | solution.py:196
  189.1 38.7 %collective-permute-start.44 = (f32[256]{0:T(256)S(1)}, f32[256]{0:T(256)S(1)}, u32[]{:S(2)}, u32[]{:S(2)}) collective-permute-start(f32[256]{0:T(256)S(1)} %concatenate.15), channel_id=1, source_target_pairs={{0,2},{1,3},{2,0},{3,1},{4,6},{5,7},{6,4},{7,5},{8,10},{9,11},{10,... | collective-permute-start | bytes 3080 | tf_op jit(solution)/shard_map/ppermute | solution.py:196
  190.7 31.4 %collective-permute-start.39 = (bf16[256,640]{1,0:T(8,128)(2,1)S(1)}, bf16[256,640]{1,0:T(8,128)(2,1)S(1)}, u32[]{:S(2)}, u32[]{:S(2)}) collective-permute-start(bf16[256,640]{1,0:T(8,128)(2,1)S(1)} %get-tuple-element.66), channel_id=1, source_target_pairs={{0,1},{1,0},{2,3},{3,2},{4,5},{5,4},{6,7},{7,6},{8,9},{9,8},{10,11... | collective-permute-start | bytes 983048 | tf_op jit(solution)/shard_map/ppermute | solution.py:196
  222.4 59.9 %collective-permute-start.41 = (bf16[512,640]{1,0:T(8,128)(2,1)S(1)}, bf16[512,640]{1,0:T(8,128)(2,1)S(1)}, u32[]{:S(2)}, u32[]{:S(2)}) collective-permute-start(bf16[512,640]{1,0:T(8,128)(2,1)S(1)} %get-tuple-element.60), channel_id=1, source_target_pairs={{0,2},{1,3},{2,4},{3,5},{4,6},{5,7},{6,0},{7,1},{8,10},{9,11},{10,... | collective-permute-start | bytes 1966088 | tf_op jit(solution)/shard_map/ppermute | solution.py:201
  224.1 58.3 %collective-permute-start.43 = (bf16[512,640]{1,0:T(8,128)(2,1)S(1)}, bf16[512,640]{1,0:T(8,128)(2,1)S(1)}, u32[]{:S(2)}, u32[]{:S(2)}) collective-permute-start(bf16[512,640]{1,0:T(8,128)(2,1)S(1)} %get-tuple-element.61), channel_id=1, source_target_pairs={{0,6},{1,7},{2,0},{3,1},{4,2},{5,3},{6,4},{7,5},{8,14},{9,15},{10,... | collective-permute-start | bytes 1966088 | tf_op jit(solution)/shard_map/ppermute | solution.py:201
  226.3 56.0 %collective-permute-start.37 = (bf16[512,640]{1,0:T(8,128)(2,1)S(1)}, bf16[512,640]{1,0:T(8,128)(2,1)S(1)}, u32[]{:S(2)}, u32[]{:S(2)}) collective-permute-start(bf16[512,640]{1,0:T(8,128)(2,1)S(1)} %fusion.9), channel_id=1, source_target_pairs={{0,1},{1,0},{2,3},{3,2},{4,5},{5,4},{6,7},{7,6},{8,9},{9,8},{10,11... | collective-permute-start | bytes 1966088 | tf_op jit(solution)/shard_map/ppermute | solution.py:196
  228.5 23.5 %collective-permute-start.45 = (f32[256]{0:T(256)S(1)}, f32[256]{0:T(256)S(1)}, u32[]{:S(2)}, u32[]{:S(2)}) collective-permute-start(f32[256]{0:T(256)S(1)} %pad_add_fusion), channel_id=1, source_target_pairs={{0,4},{1,5},{2,6},{3,7},{4,0},{5,1},{6,2},{7,3},{8,12},{9,13},{10,... | collective-permute-start | bytes 3080 | tf_op jit(solution)/shard_map/ppermute | solution.py:196
  253.6 21.7 %collective-permute-start.38 = (bf16[256,640]{1,0:T(8,128)(2,1)S(1)}, bf16[256,640]{1,0:T(8,128)(2,1)S(1)}, u32[]{:S(2)}, u32[]{:S(2)}) collective-permute-start(bf16[256,640]{1,0:T(8,128)(2,1)S(1)} %get-tuple-element.62), channel_id=1, source_target_pairs={{0,4},{1,5},{2,6},{3,7},{4,0},{5,1},{6,2},{7,3},{8,12},{9,13},{10,... | collective-permute-start | bytes 983048 | tf_op jit(solution)/shard_map/ppermute | solution.py:201
  255.6 26.7 %collective-permute-start.40 = (bf16[256,640]{1,0:T(8,128)(2,1)S(1)}, bf16[256,640]{1,0:T(8,128)(2,1)S(1)}, u32[]{:S(2)}, u32[]{:S(2)}) collective-permute-start(bf16[256,640]{1,0:T(8,128)(2,1)S(1)} %get-tuple-element.63), channel_id=1, source_target_pairs={{0,4},{1,5},{2,6},{3,7},{4,0},{5,1},{6,2},{7,3},{8,12},{9,13},{10,... | collective-permute-start | bytes 983048 | tf_op jit(solution)/shard_map/ppermute | solution.py:201
  (44 other events, 551.1 us)

commit v2 on v1

v2 whole, which is shorter than its diff:
```python
import functools

import jax
import jax.numpy as jnp
from jax import lax
from jax.experimental import pallas as pl
from jax.experimental.pallas import tpu as pltpu
from jax.sharding import PartitionSpec as P

EPS = 1e-06
NORM_TOKENS = 128
KEY_TOKENS = 256
VMEM_LIMIT = 24 * 1024 * 1024
SHORT = pl.CostEstimate(flops=1, bytes_accessed=1, transcendentals=0)
ANY = pl.BlockSpec(memory_space=pl.ANY)
SMEM = pl.BlockSpec(memory_space=pltpu.SMEM)


def norm_kernel(order, rows, place_ref, hidden_ref, gain_ref, out_ref):
    values = hidden_ref[...].astype(jnp.float32)
    scale = lax.rsqrt(jnp.sum(values * values, axis=-1, keepdims=True) / values.shape[1] + EPS)
    line, member = lax.div(place_ref[0], 2), lax.rem(place_ref[0], 2)
    for at, (step, pair) in enumerate(order):
        owner = lax.rem(line + step, len(order) // 2) * 2 + lax.rem(member + pair, 2)
        source = pl.ds(pl.multiple_of(owner * rows, 128), rows)
        scaled = hidden_ref[:, source].astype(jnp.float32) * scale * gain_ref[:, source]
        out_ref[:, at * rows : (at + 1) * rows] = scaled.astype(jnp.bfloat16)


def normed_input(place, hidden, gain, order, rows):
    tokens, width = hidden.shape
    block = pl.BlockSpec((NORM_TOKENS, width), lambda i: (i, 0))
    return pl.pallas_call(
        functools.partial(norm_kernel, order, rows),
        grid=(tokens // NORM_TOKENS,),
        in_specs=[SMEM, block, pl.BlockSpec((1, width), lambda i: (0, 0))],
        out_specs=block,
        out_shape=pltpu.HBM(hidden.shape, jnp.bfloat16),
        compiler_params=pltpu.CompilerParams(vmem_limit_bytes=VMEM_LIMIT),
        cost_estimate=SHORT,
        name="norm_input",
    )(place, in_hbm(hidden), gain)


def copy_blocks(sources, target, sems):
    copies, at = [], 0
    for i, source in enumerate(sources):
        rows = source.shape[0]
        copies.append(pltpu.make_async_copy(source, target.at[pl.ds(at, rows)], sems.at[i]))
        at += rows
    for copy in copies:
        copy.start()
    return copies


def load_weights(choice_ref, choices, target, sems):
    def load(sources):
        for copy in copy_blocks(sources, target, sems):
            copy.wait()

    if len(choices) == 1:
        load(choices[0])
    else:
        for i, sources in enumerate(choices):
            pl.when(choice_ref[0] == i)(functools.partial(load, sources))


def in_hbm(array):
    return pltpu.with_memory_space_constraint(array, pltpu.HBM)


def split(refs, counts):
    lists = []
    for count in counts:
        lists.append(refs[:count])
        refs = refs[count:]
    return lists, refs


def pack_kernel(counts, choice_ref, *refs):
    choices, (out_ref, sems) = split(refs, counts)
    load_weights(choice_ref, choices, out_ref, sems)


def pack(choice, *choices):
    rows, wide = sum(block.shape[0] for block in choices[0]), choices[0][0].shape[1]
    counts = [len(blocks) for blocks in choices]
    return pl.pallas_call(
        functools.partial(pack_kernel, counts),
        in_specs=[SMEM] + [ANY] * sum(counts),
        out_specs=pl.BlockSpec(memory_space=pltpu.VMEM),
        out_shape=jax.ShapeDtypeStruct((rows, wide), choices[0][0].dtype),
        scratch_shapes=[pltpu.SemaphoreType.DMA((max(counts),))],
        compiler_params=pltpu.CompilerParams(vmem_limit_bytes=VMEM_LIMIT),
        cost_estimate=SHORT,
        name="pack_blocks",
    )(choice, *[block for blocks in choices for block in blocks])


def early_kernel(counts, adds, choice_ref, normed_ref, *refs):
    choices, refs = split(refs, counts)
    before, (keys_ref, weights, sems) = refs[:-3], refs[-3:]

    @pl.when(pl.program_id(0) == 0)
    def _():
        load_weights(choice_ref, choices, weights, sems)

    keys = jnp.dot(normed_ref[...], weights[...], preferred_element_type=jnp.float32)
    keys_ref[...] = keys + before[0][...] if adds else keys


def early_keys(choice, normed, choices, first, before=None):
    depth, wide, tokens = sum(block.shape[0] for block in choices[0]), choices[0][0].shape[1], normed.shape[0]
    counts = [len(blocks) for blocks in choices]
    keys = pl.BlockSpec((KEY_TOKENS, wide), lambda i: (i, 0))
    before = [] if before is None else [before]
    return pl.pallas_call(
        functools.partial(early_kernel, counts, bool(before)),
        grid=(tokens // KEY_TOKENS,),
        in_specs=[SMEM, pl.BlockSpec((KEY_TOKENS, depth), lambda i: (i, first // depth))]
        + [ANY] * sum(counts)
        + [keys] * len(before),
        out_specs=keys,
        out_shape=jax.ShapeDtypeStruct((tokens, wide), jnp.float32),
        scratch_shapes=[pltpu.VMEM((depth, wide), jnp.bfloat16), pltpu.SemaphoreType.DMA((max(counts),))],
        compiler_params=pltpu.CompilerParams(vmem_limit_bytes=VMEM_LIMIT),
        cost_estimate=SHORT,
        name="early_keys",
    )(choice, in_hbm(normed), *[block for blocks in choices for block in blocks], *before)


def late_kernel(
    counts, choice_ref, student_ref, teacher_ref, part_s_ref, part_t_ref, gain_s_ref, gain_t_ref, *refs
):
    (same, *choices), (grad_ref, stats_ref, w_s, w_t, sems_s, sems_t) = split(refs, counts)
    step, head, features = pl.program_id(0), gain_s_ref.shape[1], part_s_ref.shape[1]

    @pl.when(step == 0)
    def _():
        own = copy_blocks(same, w_s, sems_s)
        load_weights(choice_ref, choices, w_t, sems_t)
        for copy in own:
            copy.wait()

    keys_s = part_s_ref[...] + jnp.dot(student_ref[...], w_s[...], preferred_element_type=jnp.float32)
    keys_t = part_t_ref[...] + jnp.dot(teacher_ref[...], w_t[...], preferred_element_type=jnp.float32)
    gain_s, gain_t = gain_s_ref[...], gain_t_ref[...]
    gain_sum, loss_sum = 0.0, 0.0
    for at in range(0, keys_s.shape[1], head):
        heads, taught = keys_s[:, at : at + head], keys_t[:, at : at + head]
        inverse = lax.rsqrt(jnp.mean(heads * heads, axis=-1, keepdims=True) + EPS)
        inverse_t = lax.rsqrt(jnp.mean(taught * taught, axis=-1, keepdims=True) + EPS)
        differ = heads * inverse * gain_s - taught * inverse_t * gain_t
        upstream = differ * (1.0 / features)
        weighted = upstream * gain_s
        inner = jnp.sum(weighted * heads, axis=-1, keepdims=True)
        grad = weighted * inverse - heads * (inverse * inverse * inverse * inner / head)
        grad_ref[:, at : at + head] = grad.astype(jnp.bfloat16)
        gain_sum = gain_sum + jnp.sum(upstream * heads * inverse, axis=0, keepdims=True)
        loss_sum = loss_sum + jnp.sum(differ * differ, axis=0, keepdims=True)
    stats = jnp.concatenate([gain_sum, loss_sum, jnp.zeros((6, head), jnp.float32)], axis=0)

    @pl.when(step == 0)
    def _():
        stats_ref[...] = stats

    @pl.when(step != 0)
    def _():
        stats_ref[...] += stats


def late_keys(choice, student, teacher, part_s, part_t, gain_s, gain_t, same, choices):
    counts, (tokens, wide), head = [len(same)] + [len(blocks) for blocks in choices], part_s.shape, gain_s.shape[1]
    depth = sum(block.shape[0] for block in same)
    last = student.shape[1] // depth - 1
    token_block = pl.BlockSpec((KEY_TOKENS, depth), lambda i: (i, last))
    keys = pl.BlockSpec((KEY_TOKENS, wide), lambda i: (i, 0))
    gain = pl.BlockSpec((1, head), lambda i: (0, 0))
    return pl.pallas_call(
        functools.partial(late_kernel, counts),
        grid=(tokens // KEY_TOKENS,),
        in_specs=[SMEM, token_block, token_block, keys, keys, gain, gain] + [ANY] * sum(counts),
        out_specs=[keys, pl.BlockSpec((8, head), lambda i: (0, 0))],
        out_shape=[jax.ShapeDtypeStruct((tokens, wide), jnp.bfloat16), jax.ShapeDtypeStruct((8, head), jnp.float32)],
        scratch_shapes=[pltpu.VMEM((depth, wide), jnp.bfloat16)] * 2
        + [pltpu.SemaphoreType.DMA((count,)) for count in (counts[0], max(counts[1:]))],
        compiler_params=pltpu.CompilerParams(vmem_limit_bytes=VMEM_LIMIT),
        cost_estimate=SHORT,
        name="late_keys",
    )(
        choice,
        in_hbm(student),
        in_hbm(teacher),
        part_s,
        part_t,
        gain_s,
        gain_t,
        *same,
        *[block for blocks in choices for block in blocks],
    )


def grad_kernel(grad_ref, student_ref, out_ref):
    out_ref[0] = lax.dot_general(
        grad_ref[...], student_ref[...], (((0,), (0,)), ((), ())), preferred_element_type=jnp.float32
    ).astype(out_ref.dtype)


def grad_blocks(grad_keys, student, rows, blocks, dtype):
    (tokens, wide), count, first = grad_keys.shape, len(blocks), blocks[0]
    stride = blocks[1] - first if count > 1 else 1
    return pl.pallas_call(
        grad_kernel,
        grid=(count,),
        in_specs=[
            pl.BlockSpec((tokens, wide), lambda i: (0, 0)),
            pl.BlockSpec((tokens, rows), lambda i: (0, first + stride * i)),
        ],
        out_specs=pl.BlockSpec((1, wide, rows), lambda i: (i, 0, 0)),
        out_shape=jax.ShapeDtypeStruct((count, wide, rows), dtype),
        compiler_params=pltpu.CompilerParams(vmem_limit_bytes=VMEM_LIMIT),
        cost_estimate=SHORT,
        name="grad_blocks",
    )(grad_keys, in_hbm(student))


def swap(value, axis, bit):
    return lax.ppermute(value, axis, [(i, i ^ bit) for i in range(lax.axis_size(axis))])


def fetch(value, step):
    size = lax.axis_size("fsdp")
    return lax.ppermute(value, "fsdp", [(i, (i - 2 * step) % size) for i in range(size)])


def after(value, *others):
    return lax.optimization_barrier((value,) + others)[0]


def phase(*values):
    return lax.optimization_barrier(values)


def local(hidden_in, gain_in, w_key, key_gain, partner):
    own_index = lax.axis_index("mp")
    teacher = partner[own_index]
    place = lax.axis_index("fsdp")
    lines = lax.axis_size("fsdp") // 2
    tok_rows, width = hidden_in.shape[1:]
    rows, features = w_key.shape[1:]
    head = key_gain.shape[1]

    far = lines // 2
    near = [step for step in range(1, lines) if step != far]
    order = [(0, 0), (0, 1)] + [(step, 0) for step in near]
    order += [(step, 1) for step in near[:-1]] + [(far, 0), (near[-1], 1), (far, 1)]
    place = place.astype(jnp.int32).reshape(1)
    own = w_key[0]

    same, other = {(0, 0): own}, {}
    for step in near:
        same[step, 0] = fetch(own, step)
    same[0, 1] = swap(own, "fsdp", 1)
    other[0, 0] = swap(own, "mp", 2)
    other[0, 1] = swap(same[0, 1], "mp", 2)
    same[far, 0] = fetch(after(own, same[near[0], 0]), far)
    student = normed_input(place, hidden_in[0], gain_in.astype(jnp.float32), order, rows)
    gains_own = jnp.concatenate([gain_in, key_gain], axis=1)
    gains_beside = swap(gains_own, "mp", 2)
    student, gains_beside, other[0, 0], other[0, 1], *moved = phase(
        student, gains_beside, other[0, 0], other[0, 1], *[same[step, 0] for step in near]
    )
    gains_same = jnp.concatenate([gains_own, gains_beside], axis=0)
    gains_cross = swap(gains_same, "mp", 1)
    is_beside = teacher == own_index ^ 2
    gains_teacher = jnp.where(
        is_beside, gains_same[1:], jnp.where(teacher == own_index ^ 1, gains_cross[:1], gains_cross[1:])
    ).astype(jnp.float32)
    choice = jnp.where(is_beside, 0, 1).astype(jnp.int32).reshape(1)
    offer = jnp.where(partner[own_index ^ 1] == own_index, 0, 1).astype(jnp.int32).reshape(1)
    normed = normed_input(place, after(hidden_in[0], student), gains_teacher[:, :width], order, rows)

    for step, block in zip(near, moved):
        same[step, 0] = block
        other[step, 0] = swap(block, "mp", 2)
        same[step, 1] = swap(block, "fsdp", 1)

    arrived = phase(
        same[far, 0],
        normed,
        *[same[step, 1] for step in near],
        *[other[step, 0] for step in near],
    )
    same[far, 0], normed = arrived[:2]
    for i, step in enumerate(near):
        same[step, 1], other[step, 0] = arrived[2 + i], arrived[2 + len(near) + i]

    def cross(mine, beside, *wait):
        return swap(pack(after(offer, *wait), mine, beside), "mp", 1)

    first, second, end = order[: 2 + len(near)], order[2 + len(near) : -2], near[-1]
    half = rows // 2
    lead = after(same[0, 1], same[end, 1])
    other[far, 0] = swap(same[far, 0], "mp", 2)
    for step in near[:-1]:
        other[step, 1] = swap(other[step, 0], "fsdp", 1)
    upper = fetch(lead[:half], far)
    part_s = early_keys(choice, student, [[same[key] for key in first + second]], 0)
    crossed = cross([same[key] for key in first], [other[key] for key in first])
    arrived = phase(lead, other[far, 0], upper, part_s, crossed, *[other[step, 1] for step in near[:-1]])
    lead, other[far, 0], upper, part_s, crossed = arrived[:5]
    for step, block in zip(near[:-1], arrived[5:]):
        other[step, 1] = block

    lower = fetch(lead[half:], far)
    other[end, 1] = swap(after(same[end, 1], upper), "mp", 2)
    other[far, 1] = swap(other[far, 0], "fsdp", 1)
    part_t = early_keys(choice, normed, [[other[key] for key in first], [crossed]], 0)
    mine, beside = [same[end, 1], upper, lower], [other[end, 1], other[far, 1]]
    last = cross(mine, beside, part_t)
    crossed = cross([same[key] for key in second], [other[key] for key in second])
    part_t = early_keys(choice, normed, [[other[key] for key in second], [crossed]], len(first) * rows, part_t)
    grad_keys, stats = late_keys(
        choice,
        student,
        normed,
        part_s,
        part_t,
        key_gain.astype(jnp.float32),
        gains_teacher[:, width:],
        mine,
        [beside, [last]],
    )

    def grads(keys, dtype, *wait):
        return grad_blocks(after(grad_keys, *wait), student, rows, [order.index(key) for key in keys], dtype)

    wide = features // 2
    give_far = grads([(far, 1)], jnp.bfloat16)
    given = [swap(give_far[0, at : at + wide], "fsdp", 1) for at in (0, wide)]
    keep_far = grads([(far, 0)], jnp.float32, given[0])
    sums = jnp.concatenate([stats[0], jnp.full((head,), jnp.sum(stats[1]))])
    bit = 2
    while bit < lax.axis_size("fsdp"):
        sums = sums + swap(sums, "fsdp", bit)
        bit *= 2
    pieces = grads([(step, 1) for step in near], jnp.bfloat16, keep_far)
    keep = grads([(step, 0) for step in near], jnp.float32, pieces)
    ends = grads([(0, 0), (0, 1)], jnp.float32, keep)
    kept = [keep_far[0, at : at + wide] for at in (0, wide)] + [keep[i] for i in range(len(near))]
    arrived = []
    for at, step in enumerate([far, far] + near):
        if at >= 2:
            ready = given[0] if at == 2 else arrived[at - 3]
            given.append(swap(after(pieces[at - 2], ready), "fsdp", 1))
        mine, block = phase(kept[at], given[at])
        summed = (mine + block.astype(jnp.float32)).astype(jnp.bfloat16)
        arrived.append(fetch(after(summed, sums if at < 2 else arrived[at - 2]), -step))
    last = swap(after(ends[1].astype(jnp.bfloat16), given[2], arrived[1]), "fsdp", 1)
    sums = sums + swap(after(sums, given[-1]), "fsdp", 1)
    total = ends[0] + last.astype(jnp.float32) + jnp.concatenate(arrived[:2], axis=0).astype(jnp.float32)
    for block in arrived[2:]:
        total = total + block.astype(jnp.float32)

    tokens_all = tok_rows * lax.axis_size("fsdp")
    distill_loss = (sums[head] / (tokens_all * features)).reshape(1)
    return (total.T[None], sums[None, :head], distill_loss)


def norm_input(hidden, gain):
    values = hidden.astype(jnp.float32)
    scale = lax.rsqrt(jnp.mean(values * values, axis=-1, keepdims=True) + EPS)
    return (values * scale * gain.astype(jnp.float32)).astype(jnp.bfloat16)


def norm_keys(keys, gain):
    heads = keys.reshape(keys.shape[0], -1, gain.shape[0])
    inverse = lax.rsqrt(jnp.mean(heads * heads, axis=-1, keepdims=True) + EPS)
    return (heads, inverse, heads * inverse * gain.astype(jnp.float32))


def plain(hidden_in, gain_in, w_key, key_gain, partner):
    partner_index = partner[lax.axis_index("mp")]
    every = [lax.all_gather(array, "mp", axis=0, tiled=True) for array in (w_key, gain_in, key_gain)]
    teach_w, teach_gain, teach_key_gain = [
        lax.dynamic_index_in_dim(array, partner_index, 0, keepdims=False) for array in every
    ]
    normed_student = norm_input(hidden_in[0], gain_in[0])
    normed_teacher = norm_input(hidden_in[0], teach_gain)
    keys_student, keys_teacher = [
        jnp.dot(normed, lax.all_gather(weight, "fsdp", axis=0, tiled=True), preferred_element_type=jnp.float32)
        for normed, weight in ((normed_student, w_key[0]), (normed_teacher, teach_w))
    ]
    heads, inverse, out_student = norm_keys(keys_student, key_gain[0])
    differ = out_student - norm_keys(keys_teacher, teach_key_gain)[2]
    upstream = differ / w_key.shape[2]
    weighted = upstream * key_gain[0].astype(jnp.float32)
    inner = jnp.sum(weighted * heads, axis=-1, keepdims=True)
    grad_heads = weighted * inverse - heads * inverse * inverse * inverse * inner / heads.shape[-1]
    grad_keys = grad_heads.reshape(keys_student.shape).astype(jnp.bfloat16)
    grad_gain = jnp.sum(upstream * heads * inverse, axis=(0, 1))
    loss_total, gain_total = lax.psum((jnp.sum(differ * differ), grad_gain), "fsdp")
    tokens_all = hidden_in.shape[1] * lax.axis_size("fsdp")
    grad = lax.dot_general(
        normed_student, grad_keys, (((0,), (0,)), ((), ())), preferred_element_type=jnp.float32
    )
    grad_rows = lax.psum_scatter(grad, "fsdp", scatter_dimension=0, tiled=True)
    distill_loss = (loss_total / (tokens_all * w_key.shape[2])).reshape(1)
    return (grad_rows[None], gain_total[None], distill_loss)


def step(hidden_in, gain_in, w_key, key_gain, partner):
    body = plain if w_key.shape[1] % 128 else local
    return body(hidden_in, gain_in, w_key, key_gain, partner)


def solution(mesh):
    return jax.shard_map(
        step,
        mesh=mesh,
        in_specs=(P("mp", "fsdp", None), P("mp", None), P("mp", "fsdp", None), P("mp", None), P()),
        out_specs=(P("mp", "fsdp", None), P("mp", None), P("mp")),
        check_vma=False,
    )
```

time: 290 us -> 217 us (0.75); the launches traced: 285 us -> 216 us
  waiting for transfers between devices: 168 us -> 109 us
  Pallas kernels: 34.9 us -> 59.2 us
  starting transfers between devices: 49.4 us -> 31 us
  local copies, waits for them, and re-layouts: 24.9 us -> 8.06 us
    ppermute x40 -> x24, waiting for transfers between devices: 110 us -> 34.2 us  [swap(): lax.ppermute(value, axis, [(i, i ^ bit) for i in range(lax.axis_size(axis...]
    unnamed x59 -> x19, local copies, waits for them, and re-layouts: 22.4 us -> 4.5 us
    ppermute x7 -> x9, waiting for transfers between devices: 58.4 us -> 75 us  [fetch(): lax.ppermute(value, 'fsdp', [(i, (i - 2 * step) % size) for i in range(si...]
    ppermute x7 -> x9, starting transfers between devices: 22.6 us -> 8.59 us  [fetch(): lax.ppermute(value, 'fsdp', [(i, (i - 2 * step) % size) for i in range(si...]
    pallas_call x2, Pallas kernels: 8.6 us -> 19.1 us  [normed_input(): pl.pallas_call(functools.partial(norm_kernel, order, rows), grid=(tokens...]
    pallas_call x3 -> x6, Pallas kernels: 13.9 us -> 21.1 us  [the longest x3 16.9 us: early_keys(): pl.pallas_call(functools.partial(early_kernel, counts, bool(before)), gri...]
    pallas_call x5, Pallas kernels: 7.28 us -> 12.6 us  [grad_blocks(): pl.pallas_call(grad_kernel, grid=(count,), in_specs=[pl.BlockSpec((tokens...]
    ppermute x40 -> x24, starting transfers between devices: 26.9 us -> 22.4 us  [swap(): lax.ppermute(value, axis, [(i, i ^ bit) for i in range(lax.axis_size(axis...]
  transfers between devices with their start and end apart: 47 -> 33, of which waited for: 20 -> 11; matrix products, arithmetic and copies ran while one was open for 2% -> 3% of each run, Pallas kernels for 10% -> 22%
where the time goes in v2:
time: 217 us; the launch traced here: 216 us
  waiting for transfers between devices  109 us (50%)
  Pallas kernels  59.2 us (27%)
  starting transfers between devices  31 us (14%)
  local copies, waits for them, and re-layouts  8.06 us (4%)
  between operations  4.78 us (2%)
  other arithmetic  3.64 us (2%)
    ppermute x9, waiting for transfers between devices, fetch(): lax.ppermute(value, 'fsdp', [(i, (i - 2 * step) % size) for i in range(si...  75 us
    ppermute x24, waiting for transfers between devices, swap(): lax.ppermute(value, axis, [(i, i ^ bit) for i in range(lax.axis_size(axis...  34.2 us
    ppermute x24, starting transfers between devices, swap(): lax.ppermute(value, axis, [(i, i ^ bit) for i in range(lax.axis_size(axis...  22.4 us
    pallas_call x2, Pallas kernels, normed_input(): pl.pallas_call(functools.partial(norm_kernel, order, rows), grid=(tokens...  19.1 us
    pallas_call x3, Pallas kernels, early_keys(): pl.pallas_call(functools.partial(early_kernel, counts, bool(before)), gri...  16.9 us
    pallas_call x5, Pallas kernels, grad_blocks(): pl.pallas_call(grad_kernel, grid=(count,), in_specs=[pl.BlockSpec((tokens...  12.6 us
    ppermute x9, starting transfers between devices, fetch(): lax.ppermute(value, 'fsdp', [(i, (i - 2 * step) % size) for i in range(si...  8.59 us
    pallas_call x1, Pallas kernels, late_keys(): pl.pallas_call(functools.partial(late_kernel, counts), grid=(tokens // KE...  6.41 us
  transfers between devices with their start and end apart: 33, of which 11 were waited for; matrix products, arithmetic and copies ran while one was open for 3% of the time, Pallas kernels for 22%

profile of v2, /device:TPU:0, one launch (start us, length us, event | category | flops | bytes accessed | tf_op | source)
XLA Modules:
  0.0 215.9 jit_solution(10700398627805399726)
XLA Ops:
  0.6 3.0 %collective-permute-start.2 = (bf16[640,512]{1,0:T(8,128)(2,1)}, bf16[640,512]{1,0:T(8,128)(2,1)S(1)}, u32[]{:S(2)}, u32[]{:S(2)}) collective-permute-start(bf16[640,512]{1,0:T(8,128)(2,1)} %bitcast.4.refs_0_), channel_id=1, source_target_pairs={{0,1},{1,0},{2,3},{3,2},{4,5},{5,4},{6,7},{7,6},{8,9},{9,8},{10,11... | collective-permute-start | bytes 1966088 | tf_op jit(solution)/shard_map/ppermute | solution.py:228
  3.7 1.5 collective-permute-start.1
  5.2 3.6 %collective-permute-start.4 = (bf16[640,512]{1,0:T(8,128)(2,1)}, bf16[640,512]{1,0:T(8,128)(2,1)}, u32[]{:S(2)}, u32[]{:S(2)}) collective-permute-start(bf16[640,512]{1,0:T(8,128)(2,1)} %bitcast.4.refs_0_), channel_id=1, source_target_pairs={{0,6},{1,7},{2,0},{3,1},{4,2},{5,3},{6,4},{7,5},{8,14},{9,15},{10,... | collective-permute-start | bytes 1966088 | tf_op jit(solution)/shard_map/ppermute | solution.py:233
  8.8 9.8 %collective-permute-done.2.refs_1_ = bf16[640,512]{1,0:T(8,128)(2,1)S(1)} collective-permute-done((bf16[640,512]{1,0:T(8,128)(2,1)}, bf16[640,512]{1,0:T(8,128)(2,1)S(1)}, u32[]{:S(2)}, u32[]{:S(2)}) %collective-permute-start.2) | collective-permute-done | bytes 655392 | tf_op jit(solution)/shard_map/ppermute | solution.py:228
  18.6 1.7 collective-permute-start.3
  22.2 9.6 %norm_input.2.normed_ref.student_ref = bf16[768,5120]{1,0:T(8,128)(2,1)} custom-call(s32[1]{0:T(128)} %bitcast.2.place_ref, bf16[768,5120]{1,0:T(8,128)(2,1)} %bitcast.45, f32[1,5120]{1,0:T(1,128)S(1)} %get-tuple-element.105.gain_ref), custom_call_target="tpu_custom_call" | custom-call | flops 1 | bytes 1 | tf_op jit(solution)/shard_map/norm_input/pallas_call | solution.py:33
  31.8 3.3 %collective-permute-done = bf16[1,5248]{1,0:T(2,128)(2,1)S(1)} collective-permute-done((bf16[1,5248]{1,0:T(2,128)(2,1)S(1)}, bf16[1,5248]{1,0:T(2,128)(2,1)S(1)}, u32[]{:S(2)}, u32[]{:S(2)}) %collective-permute-start) | collective-permute-done | bytes 10528 | tf_op jit(solution)/shard_map/ppermute | solution.py:228
  35.1 2.3 %collective-permute-done.5.refs_3_ = bf16[640,512]{1,0:T(8,128)(2,1)S(1)} collective-permute-done((bf16[640,512]{1,0:T(8,128)(2,1)}, bf16[640,512]{1,0:T(8,128)(2,1)S(1)}, u32[]{:S(2)}, u32[]{:S(2)}) %collective-permute-start.5) | collective-permute-done | bytes 655392 | tf_op jit(solution)/shard_map/ppermute | solution.py:233
  41.9 1.5 collective-permute-start.10
  45.0 9.6 %norm_input.3.normed_ref.teacher_ref = bf16[768,5120]{1,0:T(8,128)(2,1)} custom-call(s32[1]{0:T(128)} %bitcast.2.place_ref, bf16[768,5120]{1,0:T(8,128)(2,1)} %bitcast.46, f32[1,5120]{1,0:T(1,128)S(1)} %slice.83.gain_ref), custom_call_target="tpu_custom_call" | custom-call | flops 1 | bytes 1 | tf_op jit(solution)/shard_map/norm_input/pallas_call | solution.py:33
  54.6 17.9 %collective-permute-done.6.refs_5_.refs_1_ = bf16[640,512]{1,0:T(8,128)(2,1)} collective-permute-done((bf16[640,512]{1,0:T(8,128)(2,1)}, bf16[640,512]{1,0:T(8,128)(2,1)}, u32[]{:S(2)}, u32[]{:S(2)}) %collective-permute-start.6) | collective-permute-done | bytes 655392 | tf_op jit(solution)/shard_map/ppermute | solution.py:233
  73.4 2.4 %pack_blocks.3 = bf16[2560,512]{1,0:T(8,128)(2,1)} custom-call(s32[1]{0:T(128)} %bitcast.6.choice_ref, bf16[640,512]{1,0:T(8,128)(2,1)} %bitcast.4.refs_0_, bf16[640,512]{1,0:T(8,128)(2,1)S(1)} %collective-permute-done.2.refs_1_, bf16[640,512]{1,0:T(8,128)(2,1)} %collective-permute-done.4.refs_2_, bf16[640,512]{1,0:T(8,128)(2,1)S(1)} %copy-done.6, ...), custom_call_target="tpu_custom_call" | custom-call | flops 1 | bytes 1 | tf_op jit(solution)/shard_map/pack_blocks/pallas_call | solution.py:88
  78.0 1.7 collective-permute-start.13
  81.9 7.4 %early_keys.3.part_s_ref = f32[768,512]{1,0:T(8,128)S(1)} custom-call(s32[1]{0:T(128)} %bitcast.1.choice_ref, bf16[768,5120]{1,0:T(8,128)(2,1)} %norm_input.2.normed_ref.student_ref, bf16[640,512]{1,0:T(8,128)(2,1)} %bitcast.4.refs_0_, bf16[640,512]{1,0:T(8,128)(2,1)S(1)} %collective-permute-done.2.refs_1_, bf16[640,512]{1,0:T(8,128)(2,1)} %collective-permute-done.4.refs_2_, ...), custom_call_target="tpu_custom_call" | custom-call | flops 1 | bytes 1 | tf_op jit(solution)/shard_map/early_keys/pallas_call | solution.py:117
  89.3 6.5 %collective-permute-done.13.refs_1_ = bf16[320,512]{1,0:T(8,128)(2,1)} collective-permute-done((bf16[320,512]{1,0:T(8,128)(2,1)}, bf16[320,512]{1,0:T(8,128)(2,1)}, u32[]{:S(2)}, u32[]{:S(2)}) %collective-permute-start.13) | collective-permute-done | bytes 327712 | tf_op jit(solution)/shard_map/ppermute | solution.py:233
  97.0 1.5 collective-permute-start.19
  100.1 6.2 %early_keys.4.refs_3_ = f32[768,512]{1,0:T(8,128)S(1)} custom-call(s32[1]{0:T(128)} %bitcast.1.choice_ref, bf16[768,5120]{1,0:T(8,128)(2,1)} %norm_input.3.normed_ref.teacher_ref, bf16[640,512]{1,0:T(8,128)(2,1)S(1)} %collective-permute-done.1.refs_4_.refs_0_, bf16[640,512]{1,0:T(8,128)(2,1)S(1)} %collective-permute-done.3.refs_5_.refs_1_, ...), custom_call_target="tpu_custom_call" | custom-call | flops 1 | bytes 1 | tf_op jit(solution)/shard_map/early_keys/pallas_call | solution.py:117
  106.3 8.5 %collective-permute-done.17.refs_2_ = bf16[320,512]{1,0:T(8,128)(2,1)S(1)} collective-permute-done((bf16[320,512]{1,0:T(8,128)(2,1)S(1)}, bf16[320,512]{1,0:T(8,128)(2,1)S(1)}, u32[]{:S(2)}, u32[]{:S(2)}) %collective-permute-start.17) | collective-permute-done | bytes 327712 | tf_op jit(solution)/shard_map/ppermute | solution.py:233
  115.4 3.3 %early_keys.5.part_t_ref = f32[768,512]{1,0:T(8,128)S(1)} custom-call(s32[1]{0:T(128)} %bitcast.1.choice_ref, bf16[768,5120]{1,0:T(8,128)(2,1)} %norm_input.3.normed_ref.teacher_ref, bf16[640,512]{1,0:T(8,128)(2,1)} %collective-permute-done.15.refs_2_.refs_0_, bf16[640,512]{1,0:T(8,128)(2,1)} %collective-permute-done.12.refs_3_.refs_1_, ...), custom_call_target="tpu_custom_call" | custom-call | flops 1 | bytes 1 | tf_op jit(solution)/shard_map/early_keys/pallas_call | solution.py:117
  118.8 6.4 %late_keys.1 = (bf16[768,512]{1,0:T(8,128)(2,1)S(1)}, f32[8,128]{1,0:T(8,128)S(1)}) custom-call(s32[1]{0:T(128)} %bitcast.1.choice_ref, bf16[768,5120]{1,0:T(8,128)(2,1)} %norm_input.2.normed_ref.student_ref, bf16[768,5120]{1,0:T(8,128)(2,1)} %norm_input.3.normed_ref.teacher_ref, f32[768,512]{1,0:T(8,128)S(1)} %early_keys.3.part_s_ref, ...), custom_call_target="tpu_custom_call" | custom-call | flops 1 | bytes 1 | tf_op jit(solution)/shard_map/late_keys/pallas_call | solution.py:179
  125.2 2.0 grad_blocks.5
  129.3 3.6 %collective-permute-done.24 = f32[256]{0:T(256)S(1)} collective-permute-done((f32[256]{0:T(256)S(1)}, f32[256]{0:T(256)S(1)}, u32[]{:S(2)}, u32[]{:S(2)}) %collective-permute-start.24) | collective-permute-done | bytes 1056 | tf_op jit(solution)/shard_map/ppermute | solution.py:228
  135.1 3.0 %collective-permute-done.25 = f32[256]{0:T(256)S(1)} collective-permute-done((f32[256]{0:T(256)S(1)}, f32[256]{0:T(256)S(1)}, u32[]{:S(2)}, u32[]{:S(2)}) %collective-permute-start.25) | collective-permute-done | bytes 1056 | tf_op jit(solution)/shard_map/ppermute | solution.py:228
  138.1 2.0 grad_blocks.6
  140.2 2.9 %grad_blocks.7 = bf16[2,512,640]{2,1,0:T(8,128)(2,1)S(1)} custom-call(bf16[768,512]{1,0:T(8,128)(2,1)S(1)} %get-tuple-element.75.grad_ref, bf16[768,5120]{1,0:T(8,128)(2,1)} %norm_input.2.normed_ref.student_ref), custom_call_target="tpu_custom_call" | custom-call | flops 1 | bytes 1 | tf_op jit(solution)/shard_map/grad_blocks/pallas_call | solution.py:212
  143.4 2.9 %grad_blocks.8 = f32[2,512,640]{2,1,0:T(8,128)S(1)} custom-call(bf16[768,512]{1,0:T(8,128)(2,1)S(1)} %get-tuple-element.75.grad_ref, bf16[768,5120]{1,0:T(8,128)(2,1)} %norm_input.2.normed_ref.student_ref), custom_call_target="tpu_custom_call" | custom-call | flops 1 | bytes 1 | tf_op jit(solution)/shard_map/grad_blocks/pallas_call | solution.py:212
  146.2 1.5 collective-permute-start.22
  147.9 12.0 %collective-permute-done.28 = bf16[256,640]{1,0:T(8,128)(2,1)S(1)} collective-permute-done((bf16[256,640]{1,0:T(8,128)(2,1)S(1)}, bf16[256,640]{1,0:T(8,128)(2,1)S(1)}, u32[]{:S(2)}, u32[]{:S(2)}) %collective-permute-start.28) | collective-permute-done | bytes 327712 | tf_op jit(solution)/shard_map/ppermute | solution.py:233
  161.3 2.9 %grad_blocks.9 = f32[2,512,640]{2,1,0:T(8,128)S(1)} custom-call(bf16[768,512]{1,0:T(8,128)(2,1)S(1)} %get-tuple-element.75.grad_ref, bf16[768,5120]{1,0:T(8,128)(2,1)} %norm_input.2.normed_ref.student_ref), custom_call_target="tpu_custom_call" | custom-call | flops 1 | bytes 1 | tf_op jit(solution)/shard_map/grad_blocks/pallas_call | solution.py:212
  164.5 2.2 %collective-permute-start.29 = (bf16[512,640]{1,0:T(8,128)(2,1)S(1)}, bf16[512,640]{1,0:T(8,128)(2,1)S(1)}, u32[]{:S(2)}, u32[]{:S(2)}) collective-permute-start(bf16[512,640]{1,0:T(8,128)(2,1)S(1)} %add_convert_fusion.1), channel_id=1, source_target_pairs={{0,2},{1,3},{2,4},{3,5},{4,6},{5,7},{6,0},{7,1},{8,10},{9,11},{10,... | collective-permute-start | bytes 1966088 | tf_op jit(solution)/shard_map/ppermute | solution.py:233
  166.7 27.9 %collective-permute-done.26 = bf16[256,640]{1,0:T(8,128)(2,1)S(1)} collective-permute-done((bf16[256,640]{1,0:T(8,128)(2,1)S(1)}, bf16[256,640]{1,0:T(8,128)(2,1)S(1)}, u32[]{:S(2)}, u32[]{:S(2)}) %collective-permute-start.26) | collective-permute-done | bytes 327712 | tf_op jit(solution)/shard_map/ppermute | solution.py:233
  196.8 14.4 %collective-permute-done.32 = f32[256]{0:T(256)S(1)} collective-permute-done((f32[256]{0:T(256)S(1)}, f32[256]{0:T(256)S(1)}, u32[]{:S(2)}, u32[]{:S(2)}) %collective-permute-start.32) | collective-permute-done | bytes 1056 | tf_op jit(solution)/shard_map/ppermute | solution.py:228
  (93 shorter events, 26.3 us)
Async XLA Ops:
  0.6 18.0 %collective-permute-start.2 = (bf16[640,512]{1,0:T(8,128)(2,1)}, bf16[640,512]{1,0:T(8,128)(2,1)S(1)}, u32[]{:S(2)}, u32[]{:S(2)}) collective-permute-start(bf16[640,512]{1,0:T(8,128)(2,1)} %bitcast.4.refs_0_), channel_id=1, source_target_pairs={{0,1},{1,0},{2,3},{3,2},{4,5},{5,4},{6,7},{7,6},{8,9},{9,8},{10,11... | collective-permute-start | bytes 1966088 | tf_op jit(solution)/shard_map/ppermute | solution.py:228
  3.7 31.4 %collective-permute-start.1 = (bf16[640,512]{1,0:T(8,128)(2,1)}, bf16[640,512]{1,0:T(8,128)(2,1)S(1)}, u32[]{:S(2)}, u32[]{:S(2)}) collective-permute-start(bf16[640,512]{1,0:T(8,128)(2,1)} %bitcast.4.refs_0_), channel_id=1, source_target_pairs={{0,16},{8,24},{16,0},{24,8},{1,17},{9,25},{17,1},{25,9},{2,18},{10... | collective-permute-start | bytes 1966088 | tf_op jit(solution)/shard_map/ppermute | solution.py:228
  5.2 29.9 %collective-permute-start.4 = (bf16[640,512]{1,0:T(8,128)(2,1)}, bf16[640,512]{1,0:T(8,128)(2,1)}, u32[]{:S(2)}, u32[]{:S(2)}) collective-permute-start(bf16[640,512]{1,0:T(8,128)(2,1)} %bitcast.4.refs_0_), channel_id=1, source_target_pairs={{0,6},{1,7},{2,0},{3,1},{4,2},{5,3},{6,4},{7,5},{8,14},{9,15},{10,... | collective-permute-start | bytes 1966088 | tf_op jit(solution)/shard_map/ppermute | solution.py:233
  8.8 28.6 %collective-permute-start.5 = (bf16[640,512]{1,0:T(8,128)(2,1)}, bf16[640,512]{1,0:T(8,128)(2,1)S(1)}, u32[]{:S(2)}, u32[]{:S(2)}) collective-permute-start(bf16[640,512]{1,0:T(8,128)(2,1)} %bitcast.4.refs_0_), channel_id=1, source_target_pairs={{0,2},{1,3},{2,4},{3,5},{4,6},{5,7},{6,0},{7,1},{8,10},{9,11},{10,... | collective-permute-start | bytes 1966088 | tf_op jit(solution)/shard_map/ppermute | solution.py:233
  18.6 18.7 %collective-permute-start.3 = (bf16[640,512]{1,0:T(8,128)(2,1)S(1)}, bf16[640,512]{1,0:T(8,128)(2,1)S(1)}, u32[]{:S(2)}, u32[]{:S(2)}) collective-permute-start(bf16[640,512]{1,0:T(8,128)(2,1)S(1)} %collective-permute-done.2.refs_1_), channel_id=1, source_target_pairs={{0,16},{8,24},{16,0},{24,8},{1,17},{9,25},{17,1},{25,9},{2,18},{10... | collective-permute-start | bytes 1966088 | tf_op jit(solution)/shard_map/ppermute | solution.py:228
  21.9 13.2 %collective-permute-start = (bf16[1,5248]{1,0:T(2,128)(2,1)S(1)}, bf16[1,5248]{1,0:T(2,128)(2,1)S(1)}, u32[]{:S(2)}, u32[]{:S(2)}) collective-permute-start(bf16[1,5248]{1,0:T(2,128)(2,1)S(1)} %get-tuple-element.109), channel_id=1, source_target_pairs={{0,16},{8,24},{16,0},{24,8},{1,17},{9,25},{17,1},{25,9},{2,18},{10... | collective-permute-start | bytes 31496 | tf_op jit(solution)/shard_map/ppermute | solution.py:228
  37.4 6.5 %collective-permute-start.7 = (bf16[2,5248]{1,0:T(2,128)(2,1)S(1)}, bf16[2,5248]{1,0:T(2,128)(2,1)S(1)}, u32[]{:S(2)}, u32[]{:S(2)}) collective-permute-start(bf16[2,5248]{1,0:T(2,128)(2,1)S(1)} %pad_maximum_fusion), channel_id=1, source_target_pairs={{0,8},{8,0},{16,24},{24,16},{1,9},{9,1},{17,25},{25,17},{2,10},{10... | collective-permute-start | bytes 62984 | tf_op jit(solution)/shard_map/ppermute | solution.py:228
  40.1 32.4 %collective-permute-start.6 = (bf16[640,512]{1,0:T(8,128)(2,1)}, bf16[640,512]{1,0:T(8,128)(2,1)}, u32[]{:S(2)}, u32[]{:S(2)}) collective-permute-start(bf16[640,512]{1,0:T(8,128)(2,1)} %bitcast.4.refs_0_), channel_id=1, source_target_pairs={{0,4},{1,5},{2,6},{3,7},{4,0},{5,1},{6,2},{7,3},{8,12},{9,13},{10,... | collective-permute-start | bytes 1966088 | tf_op jit(solution)/shard_map/ppermute | solution.py:233
  40.9 31.6 %collective-permute-start.8 = (bf16[640,512]{1,0:T(8,128)(2,1)}, bf16[640,512]{1,0:T(8,128)(2,1)S(1)}, u32[]{:S(2)}, u32[]{:S(2)}) collective-permute-start(bf16[640,512]{1,0:T(8,128)(2,1)} %collective-permute-done.4.refs_2_), channel_id=1, source_target_pairs={{0,1},{1,0},{2,3},{3,2},{4,5},{5,4},{6,7},{7,6},{8,9},{9,8},{10,11... | collective-permute-start | bytes 1966088 | tf_op jit(solution)/shard_map/ppermute | solution.py:228
  41.9 31.4 %collective-permute-start.10 = (bf16[640,512]{1,0:T(8,128)(2,1)}, bf16[640,512]{1,0:T(8,128)(2,1)S(1)}, u32[]{:S(2)}, u32[]{:S(2)}) collective-permute-start(bf16[640,512]{1,0:T(8,128)(2,1)} %collective-permute-done.4.refs_2_), channel_id=1, source_target_pairs={{0,16},{8,24},{16,0},{24,8},{1,17},{9,25},{17,1},{25,9},{2,18},{10... | collective-permute-start | bytes 1966088 | tf_op jit(solution)/shard_map/ppermute | solution.py:228
  43.4 29.9 %collective-permute-start.9 = (bf16[640,512]{1,0:T(8,128)(2,1)}, bf16[640,512]{1,0:T(8,128)(2,1)S(1)}, u32[]{:S(2)}, u32[]{:S(2)}) collective-permute-start(bf16[640,512]{1,0:T(8,128)(2,1)} %copy-done.5), channel_id=1, source_target_pairs={{0,1},{1,0},{2,3},{3,2},{4,5},{5,4},{6,7},{7,6},{8,9},{9,8},{10,11... | collective-permute-start | bytes 1966088 | tf_op jit(solution)/shard_map/ppermute | solution.py:228
  43.9 29.4 %collective-permute-start.11 = (bf16[640,512]{1,0:T(8,128)(2,1)}, bf16[640,512]{1,0:T(8,128)(2,1)S(1)}, u32[]{:S(2)}, u32[]{:S(2)}) collective-permute-start(bf16[640,512]{1,0:T(8,128)(2,1)} %copy-done.5), channel_id=1, source_target_pairs={{0,16},{8,24},{16,0},{24,8},{1,17},{9,25},{17,1},{25,9},{2,18},{10... | collective-permute-start | bytes 1966088 | tf_op jit(solution)/shard_map/ppermute | solution.py:228
  75.8 20.0 %collective-permute-start.14 = (bf16[2560,512]{1,0:T(8,128)(2,1)}, bf16[2560,512]{1,0:T(8,128)(2,1)}, u32[]{:S(2)}, u32[]{:S(2)}) collective-permute-start(bf16[2560,512]{1,0:T(8,128)(2,1)} %pack_blocks.3), channel_id=1, source_target_pairs={{0,8},{8,0},{16,24},{24,16},{1,9},{9,1},{17,25},{25,17},{2,10},{10... | collective-permute-start | bytes 7864328 | tf_op jit(solution)/shard_map/ppermute | solution.py:228
  75.8 19.9 %collective-permute-start.12 = (bf16[640,512]{1,0:T(8,128)(2,1)}, bf16[640,512]{1,0:T(8,128)(2,1)}, u32[]{:S(2)}, u32[]{:S(2)}) collective-permute-start(bf16[640,512]{1,0:T(8,128)(2,1)} %collective-permute-done.6.refs_5_.refs_1_), channel_id=1, source_target_pairs={{0,16},{8,24},{16,0},{24,8},{1,17},{9,25},{17,1},{25,9},{2,18},{10... | collective-permute-start | bytes 1966088 | tf_op jit(solution)/shard_map/ppermute | solution.py:228
  76.7 19.0 %collective-permute-start.15 = (bf16[640,512]{1,0:T(8,128)(2,1)S(1)}, bf16[640,512]{1,0:T(8,128)(2,1)}, u32[]{:S(2)}, u32[]{:S(2)}) collective-permute-start(bf16[640,512]{1,0:T(8,128)(2,1)S(1)} %collective-permute-done.10.refs_6_.refs_2_), channel_id=1, source_target_pairs={{0,1},{1,0},{2,3},{3,2},{4,5},{5,4},{6,7},{7,6},{8,9},{9,8},{10,11... | collective-permute-start | bytes 1966088 | tf_op jit(solution)/shard_map/ppermute | solution.py:228
  78.0 17.7 %collective-permute-start.13 = (bf16[320,512]{1,0:T(8,128)(2,1)}, bf16[320,512]{1,0:T(8,128)(2,1)}, u32[]{:S(2)}, u32[]{:S(2)}) collective-permute-start(bf16[320,512]{1,0:T(8,128)(2,1)} %slice.64), channel_id=1, source_target_pairs={{0,4},{1,5},{2,6},{3,7},{4,0},{5,1},{6,2},{7,3},{8,12},{9,13},{10,... | collective-permute-start | bytes 983048 | tf_op jit(solution)/shard_map/ppermute | solution.py:233
  95.7 19.1 %collective-permute-start.18 = (bf16[640,512]{1,0:T(8,128)(2,1)S(1)}, bf16[640,512]{1,0:T(8,128)(2,1)S(1)}, u32[]{:S(2)}, u32[]{:S(2)}) collective-permute-start(bf16[640,512]{1,0:T(8,128)(2,1)S(1)} %collective-permute-done.9.refs_0_), channel_id=1, source_target_pairs={{0,16},{8,24},{16,0},{24,8},{1,17},{9,25},{17,1},{25,9},{2,18},{10... | collective-permute-start | bytes 1966088 | tf_op jit(solution)/shard_map/ppermute | solution.py:228
  97.0 17.9 %collective-permute-start.19 = (bf16[640,512]{1,0:T(8,128)(2,1)}, bf16[640,512]{1,0:T(8,128)(2,1)S(1)}, u32[]{:S(2)}, u32[]{:S(2)}) collective-permute-start(bf16[640,512]{1,0:T(8,128)(2,1)} %collective-permute-done.12.refs_3_.refs_1_), channel_id=1, source_target_pairs={{0,1},{1,0},{2,3},{3,2},{4,5},{5,4},{6,7},{7,6},{8,9},{9,8},{10,11... | collective-permute-start | bytes 1966088 | tf_op jit(solution)/shard_map/ppermute | solution.py:228
  98.6 16.3 %collective-permute-start.17 = (bf16[320,512]{1,0:T(8,128)(2,1)S(1)}, bf16[320,512]{1,0:T(8,128)(2,1)S(1)}, u32[]{:S(2)}, u32[]{:S(2)}) collective-permute-start(bf16[320,512]{1,0:T(8,128)(2,1)S(1)} %slice.66), channel_id=1, source_target_pairs={{0,4},{1,5},{2,6},{3,7},{4,0},{5,1},{6,2},{7,3},{8,12},{9,13},{10,... | collective-permute-start | bytes 983048 | tf_op jit(solution)/shard_map/ppermute | solution.py:233
  100.0 15.4 %collective-permute-start.16 = (bf16[1280,512]{1,0:T(8,128)(2,1)S(1)}, bf16[1280,512]{1,0:T(8,128)(2,1)S(1)}, u32[]{:S(2)}, u32[]{:S(2)}) collective-permute-start(bf16[1280,512]{1,0:T(8,128)(2,1)S(1)} %pack_blocks.4), channel_id=1, source_target_pairs={{0,8},{8,0},{16,24},{24,16},{1,9},{9,1},{17,25},{25,17},{2,10},{10... | collective-permute-start | bytes 3932168 | tf_op jit(solution)/shard_map/ppermute | solution.py:228
  127.3 10.8 %collective-permute-start.21 = (bf16[256,640]{1,0:T(8,128)(2,1)S(1)}, bf16[256,640]{1,0:T(8,128)(2,1)S(1)}, u32[]{:S(2)}, u32[]{:S(2)}) collective-permute-start(bf16[256,640]{1,0:T(8,128)(2,1)S(1)} %get-tuple-element.103), channel_id=1, source_target_pairs={{0,1},{1,0},{2,3},{3,2},{4,5},{5,4},{6,7},{7,6},{8,9},{9,8},{10,11... | collective-permute-start | bytes 983048 | tf_op jit(solution)/shard_map/ppermute | solution.py:228
  129.3 3.6 %collective-permute-start.24 = (f32[256]{0:T(256)S(1)}, f32[256]{0:T(256)S(1)}, u32[]{:S(2)}, u32[]{:S(2)}) collective-permute-start(f32[256]{0:T(256)S(1)} %concatenate.14), channel_id=1, source_target_pairs={{0,2},{1,3},{2,0},{3,1},{4,6},{5,7},{6,4},{7,5},{8,10},{9,11},{10,... | collective-permute-start | bytes 3080 | tf_op jit(solution)/shard_map/ppermute | solution.py:228
  133.6 4.5 %collective-permute-start.25 = (f32[256]{0:T(256)S(1)}, f32[256]{0:T(256)S(1)}, u32[]{:S(2)}, u32[]{:S(2)}) collective-permute-start(f32[256]{0:T(256)S(1)} %pad_add_fusion), channel_id=1, source_target_pairs={{0,4},{1,5},{2,6},{3,7},{4,0},{5,1},{6,2},{7,3},{8,12},{9,13},{10,... | collective-permute-start | bytes 3080 | tf_op jit(solution)/shard_map/ppermute | solution.py:228
  133.6 14.3 %collective-permute-start.23 = (bf16[256,640]{1,0:T(8,128)(2,1)S(1)}, bf16[256,640]{1,0:T(8,128)(2,1)S(1)}, u32[]{:S(2)}, u32[]{:S(2)}) collective-permute-start(bf16[256,640]{1,0:T(8,128)(2,1)S(1)} %get-tuple-element.102), channel_id=1, source_target_pairs={{0,1},{1,0},{2,3},{3,2},{4,5},{5,4},{6,7},{7,6},{8,9},{9,8},{10,11... | collective-permute-start | bytes 983048 | tf_op jit(solution)/shard_map/ppermute | solution.py:228
  143.2 16.8 %collective-permute-start.28 = (bf16[256,640]{1,0:T(8,128)(2,1)S(1)}, bf16[256,640]{1,0:T(8,128)(2,1)S(1)}, u32[]{:S(2)}, u32[]{:S(2)}) collective-permute-start(bf16[256,640]{1,0:T(8,128)(2,1)S(1)} %add_convert_fusion.2), channel_id=1, source_target_pairs={{0,4},{1,5},{2,6},{3,7},{4,0},{5,1},{6,2},{7,3},{8,12},{9,13},{10,... | collective-permute-start | bytes 983048 | tf_op jit(solution)/shard_map/ppermute | solution.py:233
  146.2 18.1 %collective-permute-start.22 = (bf16[512,640]{1,0:T(8,128)(2,1)S(1)}, bf16[512,640]{1,0:T(8,128)(2,1)S(1)}, u32[]{:S(2)}, u32[]{:S(2)}) collective-permute-start(bf16[512,640]{1,0:T(8,128)(2,1)S(1)} %get-tuple-element.76), channel_id=1, source_target_pairs={{0,1},{1,0},{2,3},{3,2},{4,5},{5,4},{6,7},{7,6},{8,9},{9,8},{10,11... | collective-permute-start | bytes 1966088 | tf_op jit(solution)/shard_map/ppermute | solution.py:228
  159.9 35.9 %collective-permute-start.30 = (bf16[512,640]{1,0:T(8,128)(2,1)S(1)}, bf16[512,640]{1,0:T(8,128)(2,1)S(1)}, u32[]{:S(2)}, u32[]{:S(2)}) collective-permute-start(bf16[512,640]{1,0:T(8,128)(2,1)S(1)} %get-tuple-element.88), channel_id=1, source_target_pairs={{0,1},{1,0},{2,3},{3,2},{4,5},{5,4},{6,7},{7,6},{8,9},{9,8},{10,11... | collective-permute-start | bytes 1966088 | tf_op jit(solution)/shard_map/ppermute | solution.py:228
  164.2 30.4 %collective-permute-start.26 = (bf16[256,640]{1,0:T(8,128)(2,1)S(1)}, bf16[256,640]{1,0:T(8,128)(2,1)S(1)}, u32[]{:S(2)}, u32[]{:S(2)}) collective-permute-start(bf16[256,640]{1,0:T(8,128)(2,1)S(1)} %add_convert_fusion.3), channel_id=1, source_target_pairs={{0,4},{1,5},{2,6},{3,7},{4,0},{5,1},{6,2},{7,3},{8,12},{9,13},{10,... | collective-permute-start | bytes 983048 | tf_op jit(solution)/shard_map/ppermute | solution.py:233
  164.5 48.5 %collective-permute-start.29 = (bf16[512,640]{1,0:T(8,128)(2,1)S(1)}, bf16[512,640]{1,0:T(8,128)(2,1)S(1)}, u32[]{:S(2)}, u32[]{:S(2)}) collective-permute-start(bf16[512,640]{1,0:T(8,128)(2,1)S(1)} %add_convert_fusion.1), channel_id=1, source_target_pairs={{0,2},{1,3},{2,4},{3,5},{4,6},{5,7},{6,0},{7,1},{8,10},{9,11},{10,... | collective-permute-start | bytes 1966088 | tf_op jit(solution)/shard_map/ppermute | solution.py:233
  194.5 18.4 %collective-permute-start.27 = (bf16[512,640]{1,0:T(8,128)(2,1)S(1)}, bf16[512,640]{1,0:T(8,128)(2,1)S(1)}, u32[]{:S(2)}, u32[]{:S(2)}) collective-permute-start(bf16[512,640]{1,0:T(8,128)(2,1)S(1)} %fusion.5), channel_id=1, source_target_pairs={{0,1},{1,0},{2,3},{3,2},{4,5},{5,4},{6,7},{7,6},{8,9},{9,8},{10,11... | collective-permute-start | bytes 1966088 | tf_op jit(solution)/shard_map/ppermute | solution.py:228
  196.0 17.0 %collective-permute-start.31 = (bf16[512,640]{1,0:T(8,128)(2,1)S(1)}, bf16[512,640]{1,0:T(8,128)(2,1)S(1)}, u32[]{:S(2)}, u32[]{:S(2)}) collective-permute-start(bf16[512,640]{1,0:T(8,128)(2,1)S(1)} %add_convert_fusion), channel_id=1, source_target_pairs={{0,6},{1,7},{2,0},{3,1},{4,2},{5,3},{6,4},{7,5},{8,14},{9,15},{10,... | collective-permute-start | bytes 1966088 | tf_op jit(solution)/shard_map/ppermute | solution.py:233
  196.0 15.2 %collective-permute-start.32 = (f32[256]{0:T(256)S(1)}, f32[256]{0:T(256)S(1)}, u32[]{:S(2)}, u32[]{:S(2)}) collective-permute-start(f32[256]{0:T(256)S(1)} %add.45), channel_id=1, source_target_pairs={{0,1},{1,0},{2,3},{3,2},{4,5},{5,4},{6,7},{7,6},{8,9},{9,8},{10,11... | collective-permute-start | bytes 3080 | tf_op jit(solution)/shard_map/ppermute | solution.py:228
  (10 other events, 75.4 us)

commit v3 on v2

--- a/solution.py
+++ b/solution.py
@@ -129,11 +129,11 @@
     )(choice, in_hbm(normed), *[block for blocks in choices for block in blocks], *before)
 
 
-def late_kernel(
-    counts, choice_ref, student_ref, teacher_ref, part_s_ref, part_t_ref, gain_s_ref, gain_t_ref, *refs
-):
-    (same, *choices), (grad_ref, stats_ref, w_s, w_t, sems_s, sems_t) = split(refs, counts)
-    step, head, features = pl.program_id(0), gain_s_ref.shape[1], part_s_ref.shape[1]
+def late_kernel(counts, choice_ref, student_ref, teacher_ref, part_s_ref, part_t_ref, gain_s_ref, gain_t_ref, *refs):
+    (same, *choices), refs = split(refs, counts)
+    keep_of_ref, give_of_ref, grad_ref, stats_ref, keep_ref, give_ref, w_s, w_t, sems_s, sems_t = refs
+    step = pl.program_id(0)
+    head, features = gain_s_ref.shape[1], part_s_ref.shape[1]
 
     @pl.when(step == 0)
     def _():
@@ -146,7 +146,8 @@
     keys_t = part_t_ref[...] + jnp.dot(teacher_ref[...], w_t[...], preferred_element_type=jnp.float32)
     gain_s, gain_t = gain_s_ref[...], gain_t_ref[...]
     gain_sum, loss_sum = 0.0, 0.0
-    for at in range(0, keys_s.shape[1], head):
+    tokens = pl.ds(pl.multiple_of(step * keys_s.shape[0], 256), keys_s.shape[0])
+    for at in range(0, features, head):
         heads, taught = keys_s[:, at : at + head], keys_t[:, at : at + head]
         inverse = lax.rsqrt(jnp.mean(heads * heads, axis=-1, keepdims=True) + EPS)
         inverse_t = lax.rsqrt(jnp.mean(taught * taught, axis=-1, keepdims=True) + EPS)
@@ -155,7 +156,7 @@
         weighted = upstream * gain_s
         inner = jnp.sum(weighted * heads, axis=-1, keepdims=True)
         grad = weighted * inverse - heads * (inverse * inverse * inverse * inner / head)
-        grad_ref[:, at : at + head] = grad.astype(jnp.bfloat16)
+        grad_ref[tokens, at : at + head] = grad.astype(jnp.bfloat16)
         gain_sum = gain_sum + jnp.sum(upstream * heads * inverse, axis=0, keepdims=True)
         loss_sum = loss_sum + jnp.sum(differ * differ, axis=0, keepdims=True)
     stats = jnp.concatenate([gain_sum, loss_sum, jnp.zeros((6, head), jnp.float32)], axis=0)
@@ -168,20 +169,35 @@
     def _():
         stats_ref[...] += stats
 
-
-def late_keys(choice, student, teacher, part_s, part_t, gain_s, gain_t, same, choices):
+    @pl.when(step == pl.num_programs(0) - 1)
+    def _():
+        for block_ref, out_ref in ((give_of_ref, give_ref), (keep_of_ref, keep_ref)):
+            out_ref[...] = lax.dot_general(
+                grad_ref[...], block_ref[...], (((0,), (0,)), ((), ())), preferred_element_type=jnp.float32
+            ).astype(out_ref.dtype)
+
+
+def late_keys(choice, student, teacher, part_s, part_t, gain_s, gain_t, same, choices, rows, far):
     counts, (tokens, wide), head = [len(same)] + [len(blocks) for blocks in choices], part_s.shape, gain_s.shape[1]
     depth = sum(block.shape[0] for block in same)
     last = student.shape[1] // depth - 1
     token_block = pl.BlockSpec((KEY_TOKENS, depth), lambda i: (i, last))
     keys = pl.BlockSpec((KEY_TOKENS, wide), lambda i: (i, 0))
     gain = pl.BlockSpec((1, head), lambda i: (0, 0))
+    far_blocks = [pl.BlockSpec((tokens, rows), lambda i, at=at: (0, at)) for at in far]
+    outs = [
+        jax.ShapeDtypeStruct((tokens, wide), jnp.bfloat16),
+        jax.ShapeDtypeStruct((8, head), jnp.float32),
+        jax.ShapeDtypeStruct((wide, rows), jnp.float32),
+        jax.ShapeDtypeStruct((wide, rows), jnp.bfloat16),
+    ]
+    student, teacher = in_hbm(student), in_hbm(teacher)
     return pl.pallas_call(
         functools.partial(late_kernel, counts),
         grid=(tokens // KEY_TOKENS,),
-        in_specs=[SMEM, token_block, token_block, keys, keys, gain, gain] + [ANY] * sum(counts),
-        out_specs=[keys, pl.BlockSpec((8, head), lambda i: (0, 0))],
-        out_shape=[jax.ShapeDtypeStruct((tokens, wide), jnp.bfloat16), jax.ShapeDtypeStruct((8, head), jnp.float32)],
+        in_specs=[SMEM, token_block, token_block, keys, keys, gain, gain] + [ANY] * sum(counts) + far_blocks,
+        out_specs=[pl.BlockSpec(out.shape, lambda i: (0, 0)) for out in outs],
+        out_shape=outs,
         scratch_shapes=[pltpu.VMEM((depth, wide), jnp.bfloat16)] * 2
         + [pltpu.SemaphoreType.DMA((count,)) for count in (counts[0], max(counts[1:]))],
         compiler_params=pltpu.CompilerParams(vmem_limit_bytes=VMEM_LIMIT),
@@ -189,14 +205,16 @@
         name="late_keys",
     )(
         choice,
-        in_hbm(student),
-        in_hbm(teacher),
+        student,
+        teacher,
         part_s,
         part_t,
         gain_s,
         gain_t,
         *same,
         *[block for blocks in choices for block in blocks],
+        student,
+        student,
     )
 
 
@@ -264,6 +282,9 @@
     other[0, 0] = swap(own, "mp", 2)
     other[0, 1] = swap(same[0, 1], "mp", 2)
     same[far, 0] = fetch(after(own, same[near[0], 0]), far)
+    flags = [teacher == own_index ^ 2, teacher == own_index ^ 1, partner[own_index ^ 1] == own_index]
+    choice, across, offer = [jnp.where(flag, 0, 1).astype(jnp.int32).reshape(1) for flag in flags]
+    place, choice, across, offer = phase(place, choice, across, offer)
     student = normed_input(place, hidden_in[0], gain_in.astype(jnp.float32), order, rows)
     gains_own = jnp.concatenate([gain_in, key_gain], axis=1)
     gains_beside = swap(gains_own, "mp", 2)
@@ -272,18 +293,16 @@
     )
     gains_same = jnp.concatenate([gains_own, gains_beside], axis=0)
     gains_cross = swap(gains_same, "mp", 1)
-    is_beside = teacher == own_index ^ 2
     gains_teacher = jnp.where(
-        is_beside, gains_same[1:], jnp.where(teacher == own_index ^ 1, gains_cross[:1], gains_cross[1:])
+        choice == 0, gains_same[1:], jnp.where(across == 0, gains_cross[:1], gains_cross[1:])
     ).astype(jnp.float32)
-    choice = jnp.where(is_beside, 0, 1).astype(jnp.int32).reshape(1)
-    offer = jnp.where(partner[own_index ^ 1] == own_index, 0, 1).astype(jnp.int32).reshape(1)
     normed = normed_input(place, after(hidden_in[0], student), gains_teacher[:, :width], order, rows)
 
     for step, block in zip(near, moved):
         same[step, 0] = block
         other[step, 0] = swap(block, "mp", 2)
         same[step, 1] = swap(block, "fsdp", 1)
+    same[far, 1] = fetch(after(same[0, 1], other[near[0], 0], same[near[0], 1]), far)
 
     arrived = phase(
         same[far, 0],
@@ -294,33 +313,20 @@
     same[far, 0], normed = arrived[:2]
     for i, step in enumerate(near):
         same[step, 1], other[step, 0] = arrived[2 + i], arrived[2 + len(near) + i]
-
-    def cross(mine, beside, *wait):
-        return swap(pack(after(offer, *wait), mine, beside), "mp", 1)
-
-    first, second, end = order[: 2 + len(near)], order[2 + len(near) : -2], near[-1]
-    half = rows // 2
-    lead = after(same[0, 1], same[end, 1])
     other[far, 0] = swap(same[far, 0], "mp", 2)
-    for step in near[:-1]:
-        other[step, 1] = swap(other[step, 0], "fsdp", 1)
-    upper = fetch(lead[:half], far)
+    for i, step in enumerate(near):
+        other[step, 1] = swap(other[step, 0], "fsdp", 1) if i % 2 == 0 else swap(same[step, 1], "mp", 2)
+
+    def cross(keys, *wait):
+        return swap(pack(after(offer, *wait), [same[key] for key in keys], [other[key] for key in keys]), "mp", 1)
+
+    first, second, third = order[: 2 + len(near)], order[2 + len(near) : -2], order[-2:]
     part_s = early_keys(choice, student, [[same[key] for key in first + second]], 0)
-    crossed = cross([same[key] for key in first], [other[key] for key in first])
-    arrived = phase(lead, other[far, 0], upper, part_s, crossed, *[other[step, 1] for step in near[:-1]])
-    lead, other[far, 0], upper, part_s, crossed = arrived[:5]
-    for step, block in zip(near[:-1], arrived[5:]):
-        other[step, 1] = block
-
-    lower = fetch(lead[half:], far)
-    other[end, 1] = swap(after(same[end, 1], upper), "mp", 2)
-    other[far, 1] = swap(other[far, 0], "fsdp", 1)
-    part_t = early_keys(choice, normed, [[other[key] for key in first], [crossed]], 0)
-    mine, beside = [same[end, 1], upper, lower], [other[end, 1], other[far, 1]]
-    last = cross(mine, beside, part_t)
-    crossed = cross([same[key] for key in second], [other[key] for key in second])
-    part_t = early_keys(choice, normed, [[other[key] for key in second], [crossed]], len(first) * rows, part_t)
-    grad_keys, stats = late_keys(
+    other[far, 1] = swap(after(other[far, 0], part_s), "fsdp", 1)
+    part_t = early_keys(choice, normed, [[other[key] for key in first], [cross(first)]], 0)
+    crossed = cross(third, part_t)
+    part_t = early_keys(choice, normed, [[other[key] for key in second], [cross(second)]], len(first) * rows, part_t)
+    grad_keys, stats, keep_far, give_far = late_keys(
         choice,
         student,
         normed,
@@ -328,26 +334,28 @@
         part_t,
         key_gain.astype(jnp.float32),
         gains_teacher[:, width:],
-        mine,
-        [beside, [last]],
-    )
+        [same[key] for key in third],
+        [[other[key] for key in third], [crossed]],
+        rows,
+        [order.index((far, pair)) for pair in range(2)],
+    )
+
+    wide = features // 2
 
     def grads(keys, dtype, *wait):
         return grad_blocks(after(grad_keys, *wait), student, rows, [order.index(key) for key in keys], dtype)
 
-    wide = features // 2
-    give_far = grads([(far, 1)], jnp.bfloat16)
-    given = [swap(give_far[0, at : at + wide], "fsdp", 1) for at in (0, wide)]
-    keep_far = grads([(far, 0)], jnp.float32, given[0])
     sums = jnp.concatenate([stats[0], jnp.full((head,), jnp.sum(stats[1]))])
-    bit = 2
+    bit, first_step = 2, None
     while bit < lax.axis_size("fsdp"):
         sums = sums + swap(sums, "fsdp", bit)
+        first_step = sums if first_step is None else first_step
         bit *= 2
-    pieces = grads([(step, 1) for step in near], jnp.bfloat16, keep_far)
+    given = [swap(give_far[:wide], "fsdp", 1), swap(after(give_far[wide:], first_step), "fsdp", 1)]
+    pieces = grads([(step, 1) for step in near], jnp.bfloat16, given[0])
     keep = grads([(step, 0) for step in near], jnp.float32, pieces)
     ends = grads([(0, 0), (0, 1)], jnp.float32, keep)
-    kept = [keep_far[0, at : at + wide] for at in (0, wide)] + [keep[i] for i in range(len(near))]
+    kept = [keep_far[i * wide : (i + 1) * wide] for i in range(2)] + [keep[i] for i in range(len(near))]
     arrived = []
     for at, step in enumerate([far, far] + near):
         if at >= 2:
@@ -355,7 +363,7 @@
             given.append(swap(after(pieces[at - 2], ready), "fsdp", 1))
         mine, block = phase(kept[at], given[at])
         summed = (mine + block.astype(jnp.float32)).astype(jnp.bfloat16)
-        arrived.append(fetch(after(summed, sums if at < 2 else arrived[at - 2]), -step))
+        arrived.append(fetch(after(summed, [summed, sums, *arrived][at]), -step))
     last = swap(after(ends[1].astype(jnp.bfloat16), given[2], arrived[1]), "fsdp", 1)
     sums = sums + swap(after(sums, given[-1]), "fsdp", 1)
     total = ends[0] + last.astype(jnp.float32) + jnp.concatenate(arrived[:2], axis=0).astype(jnp.float32)

time: 217 us -> 199 us (0.917)
  waiting for transfers between devices: 109 us -> 93 us
  starting transfers between devices: 31 us -> 38.1 us
  Pallas kernels: 59.2 us -> 53.1 us
  local copies, waits for them, and re-layouts: 8.06 us -> 4.97 us
    ppermute x9 -> x8, waiting for transfers between devices: 75 us -> 50 us  [fetch(): lax.ppermute(value, 'fsdp', [(i, (i - 2 * step) % size) for i in range(si...]
    ppermute x24, waiting for transfers between devices: 34.2 us -> 42.9 us  [swap(): lax.ppermute(value, axis, [(i, i ^ bit) for i in range(lax.axis_size(axis...]
    pallas_call x5 -> x3, Pallas kernels: 12.6 us -> 8.62 us  [grad_blocks(): pl.pallas_call(grad_kernel, grid=(count,), in_specs=[pl.BlockSpec((tokens...]
    ppermute x9 -> x8, starting transfers between devices: 8.59 us -> 12.5 us  [fetch(): lax.ppermute(value, 'fsdp', [(i, (i - 2 * step) % size) for i in range(si...]
    ppermute x24, starting transfers between devices: 22.4 us -> 25.6 us  [swap(): lax.ppermute(value, axis, [(i, i ^ bit) for i in range(lax.axis_size(axis...]
    unnamed x19 -> x3, local copies, waits for them, and re-layouts: 4.5 us -> 1.47 us
    pallas_call x3, Pallas kernels: 4.18 us -> 1.7 us  [pack(): pl.pallas_call(functools.partial(pack_kernel, counts), in_specs=[SMEM] +...]
  transfers between devices with their start and end apart: 33 -> 32, of which waited for: 11 -> 15; matrix products, arithmetic and copies ran while one was open for 3% -> 3% of each run, Pallas kernels for 22% -> 22%
where the time goes in v3:
time: 199 us; the launch traced here: 198 us
  waiting for transfers between devices  93 us (47%)
  Pallas kernels  53.1 us (27%)
  starting transfers between devices  38.1 us (19%)
  local copies, waits for them, and re-layouts  4.97 us (2%)
  between operations  4.68 us (2%)
  other arithmetic  3.78 us (2%)
    ppermute x8, waiting for transfers between devices, fetch(): lax.ppermute(value, 'fsdp', [(i, (i - 2 * step) % size) for i in range(si...  50 us
    ppermute x24, waiting for transfers between devices, swap(): lax.ppermute(value, axis, [(i, i ^ bit) for i in range(lax.axis_size(axis...  42.9 us
    ppermute x24, starting transfers between devices, swap(): lax.ppermute(value, axis, [(i, i ^ bit) for i in range(lax.axis_size(axis...  25.6 us
    pallas_call x2, Pallas kernels, normed_input(): pl.pallas_call(functools.partial(norm_kernel, order, rows), grid=(tokens...  19.1 us
    pallas_call x3, Pallas kernels, early_keys(): pl.pallas_call(functools.partial(early_kernel, counts, bool(before)), gri...  15.6 us
    ppermute x8, starting transfers between devices, fetch(): lax.ppermute(value, 'fsdp', [(i, (i - 2 * step) % size) for i in range(si...  12.5 us
    pallas_call x3, Pallas kernels, grad_blocks(): pl.pallas_call(grad_kernel, grid=(count,), in_specs=[pl.BlockSpec((tokens...  8.62 us
    pallas_call x1, Pallas kernels, late_keys(): pl.pallas_call(functools.partial(late_kernel, counts), grid=(tokens // KE...  8.1 us
  transfers between devices with their start and end apart: 32, of which 15 were waited for; matrix products, arithmetic and copies ran while one was open for 3% of the time, Pallas kernels for 22%

profile of v3, /device:TPU:0, one launch (start us, length us, event | category | flops | bytes accessed | tf_op | source)
XLA Modules:
  0.0 197.7 jit_solution(1901206067471519468)
XLA Ops:
  0.6 3.0 %collective-permute-start.2 = (bf16[640,512]{1,0:T(8,128)(2,1)}, bf16[640,512]{1,0:T(8,128)(2,1)S(1)}, u32[]{:S(2)}, u32[]{:S(2)}) collective-permute-start(bf16[640,512]{1,0:T(8,128)(2,1)} %bitcast.40), channel_id=1, source_target_pairs={{0,1},{1,0},{2,3},{3,2},{4,5},{5,4},{6,7},{7,6},{8,9},{9,8},{10,11... | collective-permute-start | bytes 1966088 | tf_op jit(solution)/shard_map/ppermute | solution.py:246
  3.7 3.6 %collective-permute-start.4 = (bf16[640,512]{1,0:T(8,128)(2,1)}, bf16[640,512]{1,0:T(8,128)(2,1)S(1)}, u32[]{:S(2)}, u32[]{:S(2)}) collective-permute-start(bf16[640,512]{1,0:T(8,128)(2,1)} %bitcast.41), channel_id=1, source_target_pairs={{0,6},{1,7},{2,0},{3,1},{4,2},{5,3},{6,4},{7,5},{8,14},{9,15},{10,... | collective-permute-start | bytes 1966088 | tf_op jit(solution)/shard_map/ppermute | solution.py:251
  7.3 1.5 collective-permute-start.1
  8.8 9.8 %collective-permute-done.2.refs_1_ = bf16[640,512]{1,0:T(8,128)(2,1)S(1)} collective-permute-done((bf16[640,512]{1,0:T(8,128)(2,1)}, bf16[640,512]{1,0:T(8,128)(2,1)S(1)}, u32[]{:S(2)}, u32[]{:S(2)}) %collective-permute-start.2) | collective-permute-done | bytes 655392 | tf_op jit(solution)/shard_map/ppermute | solution.py:246
  18.6 1.7 collective-permute-start.3
  25.5 9.6 %norm_input.2.normed_ref.student_ref.refs_5_.refs_6_ = bf16[768,5120]{1,0:T(8,128)(2,1)} custom-call(s32[1]{0:T(128)} %bitcast.place_ref, bf16[768,5120]{1,0:T(8,128)(2,1)} %bitcast.47, f32[1,5120]{1,0:T(1,128)S(1)} %get-tuple-element.103.gain_ref), custom_call_target="tpu_custom_call" | custom-call | flops 1 | bytes 1 | tf_op jit(solution)/shard_map/norm_input/pallas_call | solution.py:33
  35.1 2.8 %collective-permute-done = bf16[1,5248]{1,0:T(2,128)(2,1)S(1)} collective-permute-done((bf16[1,5248]{1,0:T(2,128)(2,1)S(1)}, bf16[1,5248]{1,0:T(2,128)(2,1)S(1)}, u32[]{:S(2)}, u32[]{:S(2)}) %collective-permute-start) | collective-permute-done | bytes 10528 | tf_op jit(solution)/shard_map/ppermute | solution.py:246
  39.7 1.5 collective-permute-start.8
  42.4 9.5 %norm_input.3.normed_ref.teacher_ref = bf16[768,5120]{1,0:T(8,128)(2,1)} custom-call(s32[1]{0:T(128)} %bitcast.place_ref, bf16[768,5120]{1,0:T(8,128)(2,1)} %bitcast.48, f32[1,5120]{1,0:T(1,128)S(1)} %slice.75.gain_ref), custom_call_target="tpu_custom_call" | custom-call | flops 1 | bytes 1 | tf_op jit(solution)/shard_map/norm_input/pallas_call | solution.py:33
  51.9 17.5 %collective-permute-done.6.refs_5_.refs_1_ = bf16[640,512]{1,0:T(8,128)(2,1)S(1)} collective-permute-done((bf16[640,512]{1,0:T(8,128)(2,1)S(1)}, bf16[640,512]{1,0:T(8,128)(2,1)S(1)}, u32[]{:S(2)}, u32[]{:S(2)}) %collective-permute-start.6) | collective-permute-done | bytes 655392 | tf_op jit(solution)/shard_map/ppermute | solution.py:251
  73.3 1.9 collective-permute-start.16
  75.2 1.5 collective-permute-start.17
  76.6 6.7 %early_keys.3.part_s_ref = f32[768,512]{1,0:T(8,128)S(1)} custom-call(s32[1]{0:T(128)} %bitcast.2.choice_ref, bf16[768,5120]{1,0:T(8,128)(2,1)} %norm_input.2.normed_ref.student_ref.refs_5_.refs_6_, bf16[640,512]{1,0:T(8,128)(2,1)S(1)} %bitcast.46, bf16[640,512]{1,0:T(8,128)(2,1)S(1)} %collective-permute-done.2.refs_1_, ...), custom_call_target="tpu_custom_call" | custom-call | flops 1 | bytes 1 | tf_op jit(solution)/shard_map/early_keys/pallas_call | solution.py:117
  83.4 5.6 %collective-permute-done.13.refs_3_.refs_1_ = bf16[640,512]{1,0:T(8,128)(2,1)S(1)} collective-permute-done((bf16[640,512]{1,0:T(8,128)(2,1)S(1)}, bf16[640,512]{1,0:T(8,128)(2,1)S(1)}, u32[]{:S(2)}, u32[]{:S(2)}) %collective-permute-start.13) | collective-permute-done | bytes 655392 | tf_op jit(solution)/shard_map/ppermute | solution.py:246
  90.8 5.2 %early_keys.4.refs_3_ = f32[768,512]{1,0:T(8,128)S(1)} custom-call(s32[1]{0:T(128)} %bitcast.2.choice_ref, bf16[768,5120]{1,0:T(8,128)(2,1)} %norm_input.3.normed_ref.teacher_ref, bf16[640,512]{1,0:T(8,128)(2,1)S(1)} %collective-permute-done.1.refs_4_.refs_0_, bf16[640,512]{1,0:T(8,128)(2,1)S(1)} %collective-permute-done.3.refs_5_.refs_1_, ...), custom_call_target="tpu_custom_call" | custom-call | flops 1 | bytes 1 | tf_op jit(solution)/shard_map/early_keys/pallas_call | solution.py:117
  96.0 8.7 %collective-permute-done.16.refs_1_ = bf16[640,512]{1,0:T(8,128)(2,1)S(1)} collective-permute-done((bf16[640,512]{1,0:T(8,128)(2,1)S(1)}, bf16[640,512]{1,0:T(8,128)(2,1)S(1)}, u32[]{:S(2)}, u32[]{:S(2)}) %collective-permute-start.16) | collective-permute-done | bytes 655392 | tf_op jit(solution)/shard_map/ppermute | solution.py:251
  105.4 3.7 %early_keys.5.part_t_ref = f32[768,512]{1,0:T(8,128)S(1)} custom-call(s32[1]{0:T(128)} %bitcast.2.choice_ref, bf16[768,5120]{1,0:T(8,128)(2,1)} %norm_input.3.normed_ref.teacher_ref, bf16[640,512]{1,0:T(8,128)(2,1)S(1)} %collective-permute-done.12.refs_2_.refs_0_, bf16[640,512]{1,0:T(8,128)(2,1)S(1)} %collective-permute-done.13.refs_3_.refs_1_, ...), custom_call_target="tpu_custom_call" | custom-call | flops 1 | bytes 1 | tf_op jit(solution)/shard_map/early_keys/pallas_call | solution.py:117
  109.0 8.1 %late_keys.1 = (bf16[768,512]{1,0:T(8,128)(2,1)S(1)}, f32[8,128]{1,0:T(8,128)S(1)}, f32[512,640]{1,0:T(8,128)S(1)}, bf16[512,640]{1,0:T(8,128)(2,1)S(1)}) custom-call(s32[1]{0:T(128)} %bitcast.2.choice_ref, bf16[768,5120]{1,0:T(8,128)(2,1)} %norm_input.2.normed_ref.student_ref.refs_5_.refs_6_, bf16[768,5120]{1,0:T(8,128)(2,1)} %norm_input.3.normed_ref.teacher_ref, ...), custom_call_target="tpu_custom_call" | custom-call | flops 1 | bytes 1 | tf_op jit(solution)/shard_map/late_keys/pallas_call | solution.py:195
  119.9 1.6 collective-permute-start.20
  122.7 2.7 %collective-permute-start.24 = (f32[256]{0:T(256)S(1)}, f32[256]{0:T(256)S(1)}, u32[]{:S(2)}, u32[]{:S(2)}) collective-permute-start(f32[256]{0:T(256)S(1)} %pad_add_fusion), channel_id=1, source_target_pairs={{0,4},{1,5},{2,6},{3,7},{4,0},{5,1},{6,2},{7,3},{8,12},{9,13},{10,... | collective-permute-start | bytes 3080 | tf_op jit(solution)/shard_map/ppermute | solution.py:246
  127.2 3.3 %collective-permute-done.20 = bf16[256,640]{1,0:T(8,128)(2,1)S(1)} collective-permute-done((bf16[256,640]{1,0:T(8,128)(2,1)S(1)}, bf16[256,640]{1,0:T(8,128)(2,1)S(1)}, u32[]{:S(2)}, u32[]{:S(2)}) %collective-permute-start.20) | collective-permute-done | bytes 327712 | tf_op jit(solution)/shard_map/ppermute | solution.py:246
  131.9 2.9 %grad_blocks.3 = bf16[2,512,640]{2,1,0:T(8,128)(2,1)S(1)} custom-call(bf16[768,512]{1,0:T(8,128)(2,1)S(1)} %get-tuple-element.72.grad_ref, bf16[768,5120]{1,0:T(8,128)(2,1)} %norm_input.2.normed_ref.student_ref.refs_5_.refs_6_), custom_call_target="tpu_custom_call" | custom-call | flops 1 | bytes 1 | tf_op jit(solution)/shard_map/grad_blocks/pallas_call | solution.py:230
  135.5 2.9 %grad_blocks.4 = f32[2,512,640]{2,1,0:T(8,128)S(1)} custom-call(bf16[768,512]{1,0:T(8,128)(2,1)S(1)} %get-tuple-element.72.grad_ref, bf16[768,5120]{1,0:T(8,128)(2,1)} %norm_input.2.normed_ref.student_ref.refs_5_.refs_6_), custom_call_target="tpu_custom_call" | custom-call | flops 1 | bytes 1 | tf_op jit(solution)/shard_map/grad_blocks/pallas_call | solution.py:230
  138.4 2.9 %grad_blocks.5 = f32[2,512,640]{2,1,0:T(8,128)S(1)} custom-call(bf16[768,512]{1,0:T(8,128)(2,1)S(1)} %get-tuple-element.72.grad_ref, bf16[768,5120]{1,0:T(8,128)(2,1)} %norm_input.2.normed_ref.student_ref.refs_5_.refs_6_), custom_call_target="tpu_custom_call" | custom-call | flops 1 | bytes 1 | tf_op jit(solution)/shard_map/grad_blocks/pallas_call | solution.py:230
  141.4 2.7 %collective-permute-start.25 = (bf16[256,640]{1,0:T(8,128)(2,1)S(1)}, bf16[256,640]{1,0:T(8,128)(2,1)S(1)}, u32[]{:S(2)}, u32[]{:S(2)}) collective-permute-start(bf16[256,640]{1,0:T(8,128)(2,1)S(1)} %add_convert_fusion.3), channel_id=1, source_target_pairs={{0,4},{1,5},{2,6},{3,7},{4,0},{5,1},{6,2},{7,3},{8,12},{9,13},{10,... | collective-permute-start | bytes 983048 | tf_op jit(solution)/shard_map/ppermute | solution.py:251
  144.1 10.0 %collective-permute-done.27 = bf16[256,640]{1,0:T(8,128)(2,1)S(1)} collective-permute-done((bf16[256,640]{1,0:T(8,128)(2,1)S(1)}, bf16[256,640]{1,0:T(8,128)(2,1)S(1)}, u32[]{:S(2)}, u32[]{:S(2)}) %collective-permute-start.27) | collective-permute-done | bytes 327712 | tf_op jit(solution)/shard_map/ppermute | solution.py:251
  155.6 5.3 %collective-permute-done.25 = bf16[256,640]{1,0:T(8,128)(2,1)S(1)} collective-permute-done((bf16[256,640]{1,0:T(8,128)(2,1)S(1)}, bf16[256,640]{1,0:T(8,128)(2,1)S(1)}, u32[]{:S(2)}, u32[]{:S(2)}) %collective-permute-start.25) | collective-permute-done | bytes 327712 | tf_op jit(solution)/shard_map/ppermute | solution.py:251
  162.5 9.2 %collective-permute-done.29 = bf16[512,640]{1,0:T(8,128)(2,1)S(1)} collective-permute-done((bf16[512,640]{1,0:T(8,128)(2,1)S(1)}, bf16[512,640]{1,0:T(8,128)(2,1)S(1)}, u32[]{:S(2)}, u32[]{:S(2)}) %collective-permute-start.29) | collective-permute-done | bytes 655392 | tf_op jit(solution)/shard_map/ppermute | solution.py:246
  171.8 2.7 %collective-permute-start.30 = (bf16[512,640]{1,0:T(8,128)(2,1)S(1)}, bf16[512,640]{1,0:T(8,128)(2,1)S(1)}, u32[]{:S(2)}, u32[]{:S(2)}) collective-permute-start(bf16[512,640]{1,0:T(8,128)(2,1)S(1)} %add_convert_fusion), channel_id=1, source_target_pairs={{0,6},{1,7},{2,0},{3,1},{4,2},{5,3},{6,4},{7,5},{8,14},{9,15},{10,... | collective-permute-start | bytes 1966088 | tf_op jit(solution)/shard_map/ppermute | solution.py:251
  175.0 9.4 %collective-permute-done.31 = f32[256]{0:T(256)S(1)} collective-permute-done((f32[256]{0:T(256)S(1)}, f32[256]{0:T(256)S(1)}, u32[]{:S(2)}, u32[]{:S(2)}) %collective-permute-start.31) | collective-permute-done | bytes 1056 | tf_op jit(solution)/shard_map/ppermute | solution.py:246
  186.2 8.6 %collective-permute-done.30 = bf16[512,640]{1,0:T(8,128)(2,1)S(1)} collective-permute-done((bf16[512,640]{1,0:T(8,128)(2,1)S(1)}, bf16[512,640]{1,0:T(8,128)(2,1)S(1)}, u32[]{:S(2)}, u32[]{:S(2)}) %collective-permute-start.30) | collective-permute-done | bytes 655392 | tf_op jit(solution)/shard_map/ppermute | solution.py:251
  195.1 1.5 copy.8
  (71 shorter events, 25.6 us)
Async XLA Ops:
  0.6 18.0 %collective-permute-start.2 = (bf16[640,512]{1,0:T(8,128)(2,1)}, bf16[640,512]{1,0:T(8,128)(2,1)S(1)}, u32[]{:S(2)}, u32[]{:S(2)}) collective-permute-start(bf16[640,512]{1,0:T(8,128)(2,1)} %bitcast.40), channel_id=1, source_target_pairs={{0,1},{1,0},{2,3},{3,2},{4,5},{5,4},{6,7},{7,6},{8,9},{9,8},{10,11... | collective-permute-start | bytes 1966088 | tf_op jit(solution)/shard_map/ppermute | solution.py:246
  3.7 34.2 %collective-permute-start.4 = (bf16[640,512]{1,0:T(8,128)(2,1)}, bf16[640,512]{1,0:T(8,128)(2,1)S(1)}, u32[]{:S(2)}, u32[]{:S(2)}) collective-permute-start(bf16[640,512]{1,0:T(8,128)(2,1)} %bitcast.41), channel_id=1, source_target_pairs={{0,6},{1,7},{2,0},{3,1},{4,2},{5,3},{6,4},{7,5},{8,14},{9,15},{10,... | collective-permute-start | bytes 1966088 | tf_op jit(solution)/shard_map/ppermute | solution.py:251
  7.3 30.6 %collective-permute-start.1 = (bf16[640,512]{1,0:T(8,128)(2,1)}, bf16[640,512]{1,0:T(8,128)(2,1)S(1)}, u32[]{:S(2)}, u32[]{:S(2)}) collective-permute-start(bf16[640,512]{1,0:T(8,128)(2,1)} %bitcast.42), channel_id=1, source_target_pairs={{0,16},{8,24},{16,0},{24,8},{1,17},{9,25},{17,1},{25,9},{2,18},{10... | collective-permute-start | bytes 1966088 | tf_op jit(solution)/shard_map/ppermute | solution.py:246
  8.8 29.1 %collective-permute-start.5 = (bf16[640,512]{1,0:T(8,128)(2,1)}, bf16[640,512]{1,0:T(8,128)(2,1)S(1)}, u32[]{:S(2)}, u32[]{:S(2)}) collective-permute-start(bf16[640,512]{1,0:T(8,128)(2,1)} %bitcast.43), channel_id=1, source_target_pairs={{0,2},{1,3},{2,4},{3,5},{4,6},{5,7},{6,0},{7,1},{8,10},{9,11},{10,... | collective-permute-start | bytes 1966088 | tf_op jit(solution)/shard_map/ppermute | solution.py:251
  18.6 19.3 %collective-permute-start.3 = (bf16[640,512]{1,0:T(8,128)(2,1)S(1)}, bf16[640,512]{1,0:T(8,128)(2,1)S(1)}, u32[]{:S(2)}, u32[]{:S(2)}) collective-permute-start(bf16[640,512]{1,0:T(8,128)(2,1)S(1)} %collective-permute-done.2.refs_1_), channel_id=1, source_target_pairs={{0,16},{8,24},{16,0},{24,8},{1,17},{9,25},{17,1},{25,9},{2,18},{10... | collective-permute-start | bytes 1966088 | tf_op jit(solution)/shard_map/ppermute | solution.py:246
  21.9 16.0 %collective-permute-start = (bf16[1,5248]{1,0:T(2,128)(2,1)S(1)}, bf16[1,5248]{1,0:T(2,128)(2,1)S(1)}, u32[]{:S(2)}, u32[]{:S(2)}) collective-permute-start(bf16[1,5248]{1,0:T(2,128)(2,1)S(1)} %get-tuple-element.107), channel_id=1, source_target_pairs={{0,16},{8,24},{16,0},{24,8},{1,17},{9,25},{17,1},{25,9},{2,18},{10... | collective-permute-start | bytes 31496 | tf_op jit(solution)/shard_map/ppermute | solution.py:246
  38.0 3.8 %collective-permute-start.7 = (bf16[2,5248]{1,0:T(2,128)(2,1)S(1)}, bf16[2,5248]{1,0:T(2,128)(2,1)S(1)}, u32[]{:S(2)}, u32[]{:S(2)}) collective-permute-start(bf16[2,5248]{1,0:T(2,128)(2,1)S(1)} %pad_maximum_fusion), channel_id=1, source_target_pairs={{0,8},{8,0},{16,24},{24,16},{1,9},{9,1},{17,25},{25,17},{2,10},{10... | collective-permute-start | bytes 62984 | tf_op jit(solution)/shard_map/ppermute | solution.py:246
  38.1 31.4 %collective-permute-start.6 = (bf16[640,512]{1,0:T(8,128)(2,1)S(1)}, bf16[640,512]{1,0:T(8,128)(2,1)S(1)}, u32[]{:S(2)}, u32[]{:S(2)}) collective-permute-start(bf16[640,512]{1,0:T(8,128)(2,1)S(1)} %bitcast.44), channel_id=1, source_target_pairs={{0,4},{1,5},{2,6},{3,7},{4,0},{5,1},{6,2},{7,3},{8,12},{9,13},{10,... | collective-permute-start | bytes 1966088 | tf_op jit(solution)/shard_map/ppermute | solution.py:251
  38.3 31.1 %collective-permute-start.10 = (bf16[640,512]{1,0:T(8,128)(2,1)S(1)}, bf16[640,512]{1,0:T(8,128)(2,1)S(1)}, u32[]{:S(2)}, u32[]{:S(2)}) collective-permute-start(bf16[640,512]{1,0:T(8,128)(2,1)S(1)} %collective-permute-done.4.refs_2_), channel_id=1, source_target_pairs={{0,16},{8,24},{16,0},{24,8},{1,17},{9,25},{17,1},{25,9},{2,18},{10... | collective-permute-start | bytes 1966088 | tf_op jit(solution)/shard_map/ppermute | solution.py:246
  39.7 29.7 %collective-permute-start.8 = (bf16[640,512]{1,0:T(8,128)(2,1)S(1)}, bf16[640,512]{1,0:T(8,128)(2,1)S(1)}, u32[]{:S(2)}, u32[]{:S(2)}) collective-permute-start(bf16[640,512]{1,0:T(8,128)(2,1)S(1)} %collective-permute-done.4.refs_2_), channel_id=1, source_target_pairs={{0,1},{1,0},{2,3},{3,2},{4,5},{5,4},{6,7},{7,6},{8,9},{9,8},{10,11... | collective-permute-start | bytes 1966088 | tf_op jit(solution)/shard_map/ppermute | solution.py:246
  41.2 28.3 %collective-permute-start.11 = (bf16[640,512]{1,0:T(8,128)(2,1)S(1)}, bf16[640,512]{1,0:T(8,128)(2,1)S(1)}, u32[]{:S(2)}, u32[]{:S(2)}) collective-permute-start(bf16[640,512]{1,0:T(8,128)(2,1)S(1)} %collective-permute-done.5.refs_3_), channel_id=1, source_target_pairs={{0,16},{8,24},{16,0},{24,8},{1,17},{9,25},{17,1},{25,9},{2,18},{10... | collective-permute-start | bytes 1966088 | tf_op jit(solution)/shard_map/ppermute | solution.py:246
  41.7 28.7 %collective-permute-start.9 = (bf16[640,512]{1,0:T(8,128)(2,1)S(1)}, bf16[640,512]{1,0:T(8,128)(2,1)S(1)}, u32[]{:S(2)}, u32[]{:S(2)}) collective-permute-start(bf16[640,512]{1,0:T(8,128)(2,1)S(1)} %collective-permute-done.5.refs_3_), channel_id=1, source_target_pairs={{0,1},{1,0},{2,3},{3,2},{4,5},{5,4},{6,7},{7,6},{8,9},{9,8},{10,11... | collective-permute-start | bytes 1966088 | tf_op jit(solution)/shard_map/ppermute | solution.py:246
  71.3 19.5 %collective-permute-start.15 = (bf16[2560,512]{1,0:T(8,128)(2,1)S(1)}, bf16[2560,512]{1,0:T(8,128)(2,1)S(1)}, u32[]{:S(2)}, u32[]{:S(2)}) collective-permute-start(bf16[2560,512]{1,0:T(8,128)(2,1)S(1)} %pack_blocks.4), channel_id=1, source_target_pairs={{0,8},{8,0},{16,24},{24,16},{1,9},{9,1},{17,25},{25,17},{2,10},{10... | collective-permute-start | bytes 7864328 | tf_op jit(solution)/shard_map/ppermute | solution.py:246
  71.4 17.6 %collective-permute-start.13 = (bf16[640,512]{1,0:T(8,128)(2,1)S(1)}, bf16[640,512]{1,0:T(8,128)(2,1)S(1)}, u32[]{:S(2)}, u32[]{:S(2)}) collective-permute-start(bf16[640,512]{1,0:T(8,128)(2,1)S(1)} %collective-permute-done.6.refs_5_.refs_1_), channel_id=1, source_target_pairs={{0,16},{8,24},{16,0},{24,8},{1,17},{9,25},{17,1},{25,9},{2,18},{10... | collective-permute-start | bytes 1966088 | tf_op jit(solution)/shard_map/ppermute | solution.py:246
  72.0 18.3 %collective-permute-start.12 = (bf16[640,512]{1,0:T(8,128)(2,1)S(1)}, bf16[640,512]{1,0:T(8,128)(2,1)S(1)}, u32[]{:S(2)}, u32[]{:S(2)}) collective-permute-start(bf16[640,512]{1,0:T(8,128)(2,1)S(1)} %collective-permute-done.10.refs_6_.refs_2_), channel_id=1, source_target_pairs={{0,1},{1,0},{2,3},{3,2},{4,5},{5,4},{6,7},{7,6},{8,9},{9,8},{10,11... | collective-permute-start | bytes 1966088 | tf_op jit(solution)/shard_map/ppermute | solution.py:246
  73.3 31.5 %collective-permute-start.16 = (bf16[640,512]{1,0:T(8,128)(2,1)S(1)}, bf16[640,512]{1,0:T(8,128)(2,1)S(1)}, u32[]{:S(2)}, u32[]{:S(2)}) collective-permute-start(bf16[640,512]{1,0:T(8,128)(2,1)S(1)} %collective-permute-done.2.refs_1_), channel_id=1, source_target_pairs={{0,4},{1,5},{2,6},{3,7},{4,0},{5,1},{6,2},{7,3},{8,12},{9,13},{10,... | collective-permute-start | bytes 1966088 | tf_op jit(solution)/shard_map/ppermute | solution.py:251
  75.2 29.6 %collective-permute-start.17 = (bf16[640,512]{1,0:T(8,128)(2,1)S(1)}, bf16[640,512]{1,0:T(8,128)(2,1)S(1)}, u32[]{:S(2)}, u32[]{:S(2)}) collective-permute-start(bf16[640,512]{1,0:T(8,128)(2,1)S(1)} %collective-permute-done.9.refs_0_), channel_id=1, source_target_pairs={{0,16},{8,24},{16,0},{24,8},{1,17},{9,25},{17,1},{25,9},{2,18},{10... | collective-permute-start | bytes 1966088 | tf_op jit(solution)/shard_map/ppermute | solution.py:246
  89.0 15.8 %collective-permute-start.18 = (bf16[640,512]{1,0:T(8,128)(2,1)S(1)}, bf16[640,512]{1,0:T(8,128)(2,1)S(1)}, u32[]{:S(2)}, u32[]{:S(2)}) collective-permute-start(bf16[640,512]{1,0:T(8,128)(2,1)S(1)} %collective-permute-done.13.refs_3_.refs_1_), channel_id=1, source_target_pairs={{0,1},{1,0},{2,3},{3,2},{4,5},{5,4},{6,7},{7,6},{8,9},{9,8},{10,11... | collective-permute-start | bytes 1966088 | tf_op jit(solution)/shard_map/ppermute | solution.py:246
  90.7 14.6 %collective-permute-start.14 = (bf16[1280,512]{1,0:T(8,128)(2,1)S(1)}, bf16[1280,512]{1,0:T(8,128)(2,1)S(1)}, u32[]{:S(2)}, u32[]{:S(2)}) collective-permute-start(bf16[1280,512]{1,0:T(8,128)(2,1)S(1)} %pack_blocks.3), channel_id=1, source_target_pairs={{0,8},{8,0},{16,24},{24,16},{1,9},{9,1},{17,25},{25,17},{2,10},{10... | collective-permute-start | bytes 3932168 | tf_op jit(solution)/shard_map/ppermute | solution.py:246
  105.3 3.8 %collective-permute-start.19 = (bf16[1280,512]{1,0:T(8,128)(2,1)S(1)}, bf16[1280,512]{1,0:T(8,128)(2,1)S(1)}, u32[]{:S(2)}, u32[]{:S(2)}) collective-permute-start(bf16[1280,512]{1,0:T(8,128)(2,1)S(1)} %pack_blocks.5), channel_id=1, source_target_pairs={{0,8},{8,0},{16,24},{24,16},{1,9},{9,1},{17,25},{25,17},{2,10},{10... | collective-permute-start | bytes 3932168 | tf_op jit(solution)/shard_map/ppermute | solution.py:246
  118.4 3.6 %collective-permute-start.22 = (f32[256]{0:T(256)S(1)}, f32[256]{0:T(256)S(1)}, u32[]{:S(2)}, u32[]{:S(2)}) collective-permute-start(f32[256]{0:T(256)S(1)} %concatenate.14), channel_id=1, source_target_pairs={{0,2},{1,3},{2,0},{3,1},{4,6},{5,7},{6,4},{7,5},{8,10},{9,11},{10,... | collective-permute-start | bytes 3080 | tf_op jit(solution)/shard_map/ppermute | solution.py:246
  119.9 10.6 %collective-permute-start.20 = (bf16[256,640]{1,0:T(8,128)(2,1)S(1)}, bf16[256,640]{1,0:T(8,128)(2,1)S(1)}, u32[]{:S(2)}, u32[]{:S(2)}) collective-permute-start(bf16[256,640]{1,0:T(8,128)(2,1)S(1)} %get-tuple-element.101), channel_id=1, source_target_pairs={{0,1},{1,0},{2,3},{3,2},{4,5},{5,4},{6,7},{7,6},{8,9},{9,8},{10,11... | collective-permute-start | bytes 983048 | tf_op jit(solution)/shard_map/ppermute | solution.py:246
  122.7 4.5 %collective-permute-start.24 = (f32[256]{0:T(256)S(1)}, f32[256]{0:T(256)S(1)}, u32[]{:S(2)}, u32[]{:S(2)}) collective-permute-start(f32[256]{0:T(256)S(1)} %pad_add_fusion), channel_id=1, source_target_pairs={{0,4},{1,5},{2,6},{3,7},{4,0},{5,1},{6,2},{7,3},{8,12},{9,13},{10,... | collective-permute-start | bytes 3080 | tf_op jit(solution)/shard_map/ppermute | solution.py:246
  125.5 15.8 %collective-permute-start.23 = (bf16[256,640]{1,0:T(8,128)(2,1)S(1)}, bf16[256,640]{1,0:T(8,128)(2,1)S(1)}, u32[]{:S(2)}, u32[]{:S(2)}) collective-permute-start(bf16[256,640]{1,0:T(8,128)(2,1)S(1)} %get-tuple-element.76), channel_id=1, source_target_pairs={{0,1},{1,0},{2,3},{3,2},{4,5},{5,4},{6,7},{7,6},{8,9},{9,8},{10,11... | collective-permute-start | bytes 983048 | tf_op jit(solution)/shard_map/ppermute | solution.py:246
  130.6 23.5 %collective-permute-start.27 = (bf16[256,640]{1,0:T(8,128)(2,1)S(1)}, bf16[256,640]{1,0:T(8,128)(2,1)S(1)}, u32[]{:S(2)}, u32[]{:S(2)}) collective-permute-start(bf16[256,640]{1,0:T(8,128)(2,1)S(1)} %add_convert_fusion.2), channel_id=1, source_target_pairs={{0,4},{1,5},{2,6},{3,7},{4,0},{5,1},{6,2},{7,3},{8,12},{9,13},{10,... | collective-permute-start | bytes 983048 | tf_op jit(solution)/shard_map/ppermute | solution.py:251
  134.9 25.9 %collective-permute-start.21 = (bf16[512,640]{1,0:T(8,128)(2,1)S(1)}, bf16[512,640]{1,0:T(8,128)(2,1)S(1)}, u32[]{:S(2)}, u32[]{:S(2)}) collective-permute-start(bf16[512,640]{1,0:T(8,128)(2,1)S(1)} %get-tuple-element.73), channel_id=1, source_target_pairs={{0,1},{1,0},{2,3},{3,2},{4,5},{5,4},{6,7},{7,6},{8,9},{9,8},{10,11... | collective-permute-start | bytes 1966088 | tf_op jit(solution)/shard_map/ppermute | solution.py:246
  141.4 19.5 %collective-permute-start.25 = (bf16[256,640]{1,0:T(8,128)(2,1)S(1)}, bf16[256,640]{1,0:T(8,128)(2,1)S(1)}, u32[]{:S(2)}, u32[]{:S(2)}) collective-permute-start(bf16[256,640]{1,0:T(8,128)(2,1)S(1)} %add_convert_fusion.3), channel_id=1, source_target_pairs={{0,4},{1,5},{2,6},{3,7},{4,0},{5,1},{6,2},{7,3},{8,12},{9,13},{10,... | collective-permute-start | bytes 983048 | tf_op jit(solution)/shard_map/ppermute | solution.py:251
  154.0 17.6 %collective-permute-start.29 = (bf16[512,640]{1,0:T(8,128)(2,1)S(1)}, bf16[512,640]{1,0:T(8,128)(2,1)S(1)}, u32[]{:S(2)}, u32[]{:S(2)}) collective-permute-start(bf16[512,640]{1,0:T(8,128)(2,1)S(1)} %get-tuple-element.86), channel_id=1, source_target_pairs={{0,1},{1,0},{2,3},{3,2},{4,5},{5,4},{6,7},{7,6},{8,9},{9,8},{10,11... | collective-permute-start | bytes 1966088 | tf_op jit(solution)/shard_map/ppermute | solution.py:246
  160.8 25.3 %collective-permute-start.26 = (bf16[512,640]{1,0:T(8,128)(2,1)S(1)}, bf16[512,640]{1,0:T(8,128)(2,1)S(1)}, u32[]{:S(2)}, u32[]{:S(2)}) collective-permute-start(bf16[512,640]{1,0:T(8,128)(2,1)S(1)} %fusion.5), channel_id=1, source_target_pairs={{0,1},{1,0},{2,3},{3,2},{4,5},{5,4},{6,7},{7,6},{8,9},{9,8},{10,11... | collective-permute-start | bytes 1966088 | tf_op jit(solution)/shard_map/ppermute | solution.py:246
  162.4 23.7 %collective-permute-start.28 = (bf16[512,640]{1,0:T(8,128)(2,1)S(1)}, bf16[512,640]{1,0:T(8,128)(2,1)S(1)}, u32[]{:S(2)}, u32[]{:S(2)}) collective-permute-start(bf16[512,640]{1,0:T(8,128)(2,1)S(1)} %add_convert_fusion.1), channel_id=1, source_target_pairs={{0,2},{1,3},{2,4},{3,5},{4,6},{5,7},{6,0},{7,1},{8,10},{9,11},{10,... | collective-permute-start | bytes 1966088 | tf_op jit(solution)/shard_map/ppermute | solution.py:251
  171.8 22.9 %collective-permute-start.30 = (bf16[512,640]{1,0:T(8,128)(2,1)S(1)}, bf16[512,640]{1,0:T(8,128)(2,1)S(1)}, u32[]{:S(2)}, u32[]{:S(2)}) collective-permute-start(bf16[512,640]{1,0:T(8,128)(2,1)S(1)} %add_convert_fusion), channel_id=1, source_target_pairs={{0,6},{1,7},{2,0},{3,1},{4,2},{5,3},{6,4},{7,5},{8,14},{9,15},{10,... | collective-permute-start | bytes 1966088 | tf_op jit(solution)/shard_map/ppermute | solution.py:251
  174.6 9.9 %collective-permute-start.31 = (f32[256]{0:T(256)S(1)}, f32[256]{0:T(256)S(1)}, u32[]{:S(2)}, u32[]{:S(2)}) collective-permute-start(f32[256]{0:T(256)S(1)} %add.45), channel_id=1, source_target_pairs={{0,1},{1,0},{2,3},{3,2},{4,5},{5,4},{6,7},{7,6},{8,9},{9,8},{10,11... | collective-permute-start | bytes 3080 | tf_op jit(solution)/shard_map/ppermute | solution.py:246
  (1 other events, 12.6 us)

commit v4 on v3

--- a/solution.py
+++ b/solution.py
@@ -10,7 +10,7 @@
 EPS = 1e-06
 NORM_TOKENS = 128
 KEY_TOKENS = 256
-VMEM_LIMIT = 24 * 1024 * 1024
+VMEM_LIMIT = 16 * 1024 * 1024
 SHORT = pl.CostEstimate(flops=1, bytes_accessed=1, transcendentals=0)
 ANY = pl.BlockSpec(memory_space=pl.ANY)
 SMEM = pl.BlockSpec(memory_space=pltpu.SMEM)
@@ -131,7 +131,7 @@
 
 def late_kernel(counts, choice_ref, student_ref, teacher_ref, part_s_ref, part_t_ref, gain_s_ref, gain_t_ref, *refs):
     (same, *choices), refs = split(refs, counts)
-    keep_of_ref, give_of_ref, grad_ref, stats_ref, keep_ref, give_ref, w_s, w_t, sems_s, sems_t = refs
+    give_of_ref, grad_ref, stats_ref, give_ref, w_s, w_t, sems_s, sems_t = refs
     step = pl.program_id(0)
     head, features = gain_s_ref.shape[1], part_s_ref.shape[1]
 
@@ -171,31 +171,29 @@
 
     @pl.when(step == pl.num_programs(0) - 1)
     def _():
-        for block_ref, out_ref in ((give_of_ref, give_ref), (keep_of_ref, keep_ref)):
-            out_ref[...] = lax.dot_general(
-                grad_ref[...], block_ref[...], (((0,), (0,)), ((), ())), preferred_element_type=jnp.float32
-            ).astype(out_ref.dtype)
-
-
-def late_keys(choice, student, teacher, part_s, part_t, gain_s, gain_t, same, choices, rows, far):
+        give_ref[...] = lax.dot_general(
+            grad_ref[...], give_of_ref[...], (((0,), (0,)), ((), ())), preferred_element_type=jnp.float32
+        ).astype(give_ref.dtype)
+
+
+def late_keys(choice, student, teacher, part_s, part_t, gain_s, gain_t, same, choices, rows, give):
     counts, (tokens, wide), head = [len(same)] + [len(blocks) for blocks in choices], part_s.shape, gain_s.shape[1]
     depth = sum(block.shape[0] for block in same)
     last = student.shape[1] // depth - 1
     token_block = pl.BlockSpec((KEY_TOKENS, depth), lambda i: (i, last))
     keys = pl.BlockSpec((KEY_TOKENS, wide), lambda i: (i, 0))
     gain = pl.BlockSpec((1, head), lambda i: (0, 0))
-    far_blocks = [pl.BlockSpec((tokens, rows), lambda i, at=at: (0, at)) for at in far]
     outs = [
         jax.ShapeDtypeStruct((tokens, wide), jnp.bfloat16),
         jax.ShapeDtypeStruct((8, head), jnp.float32),
-        jax.ShapeDtypeStruct((wide, rows), jnp.float32),
         jax.ShapeDtypeStruct((wide, rows), jnp.bfloat16),
     ]
     student, teacher = in_hbm(student), in_hbm(teacher)
     return pl.pallas_call(
         functools.partial(late_kernel, counts),
         grid=(tokens // KEY_TOKENS,),
-        in_specs=[SMEM, token_block, token_block, keys, keys, gain, gain] + [ANY] * sum(counts) + far_blocks,
+        in_specs=[SMEM, token_block, token_block, keys, keys, gain, gain] + [ANY] * sum(counts)
+        + [pl.BlockSpec((tokens, rows), lambda i: (0, give))],
         out_specs=[pl.BlockSpec(out.shape, lambda i: (0, 0)) for out in outs],
         out_shape=outs,
         scratch_shapes=[pltpu.VMEM((depth, wide), jnp.bfloat16)] * 2
@@ -214,7 +212,6 @@
         *same,
         *[block for blocks in choices for block in blocks],
         student,
-        student,
     )
 
 
@@ -326,7 +323,7 @@
     part_t = early_keys(choice, normed, [[other[key] for key in first], [cross(first)]], 0)
     crossed = cross(third, part_t)
     part_t = early_keys(choice, normed, [[other[key] for key in second], [cross(second)]], len(first) * rows, part_t)
-    grad_keys, stats, keep_far, give_far = late_keys(
+    grad_keys, sums, give_far = late_keys(
         choice,
         student,
         normed,
@@ -337,7 +334,7 @@
         [same[key] for key in third],
         [[other[key] for key in third], [crossed]],
         rows,
-        [order.index((far, pair)) for pair in range(2)],
+        order.index((far, 1)),
     )
 
     wide = features // 2
@@ -345,34 +342,33 @@
     def grads(keys, dtype, *wait):
         return grad_blocks(after(grad_keys, *wait), student, rows, [order.index(key) for key in keys], dtype)
 
-    sums = jnp.concatenate([stats[0], jnp.full((head,), jnp.sum(stats[1]))])
-    bit, first_step = 2, None
+    keep_far = grads([(far, 0)], jnp.float32, give_far)
+    halves = [slice(0, wide), slice(wide, features)]
+    given = [swap(give_far[halves[0]], "fsdp", 1), swap(after(give_far[halves[1]], keep_far), "fsdp", 1)]
+    bit = 2
     while bit < lax.axis_size("fsdp"):
         sums = sums + swap(sums, "fsdp", bit)
-        first_step = sums if first_step is None else first_step
         bit *= 2
-    given = [swap(give_far[:wide], "fsdp", 1), swap(after(give_far[wide:], first_step), "fsdp", 1)]
     pieces = grads([(step, 1) for step in near], jnp.bfloat16, given[0])
     keep = grads([(step, 0) for step in near], jnp.float32, pieces)
     ends = grads([(0, 0), (0, 1)], jnp.float32, keep)
-    kept = [keep_far[i * wide : (i + 1) * wide] for i in range(2)] + [keep[i] for i in range(len(near))]
+    kept = [keep_far[0, half] for half in halves] + [keep[i] for i in range(len(near))]
     arrived = []
     for at, step in enumerate([far, far] + near):
         if at >= 2:
-            ready = given[0] if at == 2 else arrived[at - 3]
-            given.append(swap(after(pieces[at - 2], ready), "fsdp", 1))
+            given.append(swap(after(pieces[at - 2], [given[0], arrived[0]][at - 2]), "fsdp", 1))
         mine, block = phase(kept[at], given[at])
         summed = (mine + block.astype(jnp.float32)).astype(jnp.bfloat16)
         arrived.append(fetch(after(summed, [summed, sums, *arrived][at]), -step))
     last = swap(after(ends[1].astype(jnp.bfloat16), given[2], arrived[1]), "fsdp", 1)
-    sums = sums + swap(after(sums, given[-1]), "fsdp", 1)
+    sums = sums + swap(after(sums, given[3]), "fsdp", 1)
     total = ends[0] + last.astype(jnp.float32) + jnp.concatenate(arrived[:2], axis=0).astype(jnp.float32)
     for block in arrived[2:]:
         total = total + block.astype(jnp.float32)
 
     tokens_all = tok_rows * lax.axis_size("fsdp")
-    distill_loss = (sums[head] / (tokens_all * features)).reshape(1)
-    return (total.T[None], sums[None, :head], distill_loss)
+    distill_loss = (jnp.sum(sums[1]) / (tokens_all * features)).reshape(1)
+    return (total.T[None], sums[:1], distill_loss)
 
 
 def norm_input(hidden, gain):

time: 199 us -> 199 us (level)
  waiting for transfers between devices: 93 us -> 87 us
  other arithmetic: 3.78 us -> 7.8 us
  starting transfers between devices: 38.1 us -> 40.2 us
    ppermute x24, waiting for transfers between devices: 42.9 us -> 38.1 us  [swap(): lax.ppermute(value, axis, [(i, i ^ bit) for i in range(lax.axis_size(axis...]
    broadcast_in_dim x1, other arithmetic: 0.37 us -> 2.94 us  [local(): return (total.T[None], sums[:1], distill_loss)]
    pallas_call x3 -> x4, Pallas kernels: 8.62 us -> 10.6 us  [grad_blocks(): pl.pallas_call(grad_kernel, grid=(count,), in_specs=[pl.BlockSpec((tokens...]
  transfers between devices with their start and end apart: 32 -> 32, of which waited for: 15 -> 15; matrix products, arithmetic and copies ran while one was open for 3% -> 4% of each run, Pallas kernels for 22% -> 23%
where the time goes in v4:
time: 199 us; the launch traced here: 198 us
  waiting for transfers between devices  87 us (44%)
  Pallas kernels  53 us (27%)
  starting transfers between devices  40.2 us (20%)
  other arithmetic  7.8 us (4%)
  local copies, waits for them, and re-layouts  5.47 us (3%)
  between operations  4.66 us (2%)
    ppermute x8, waiting for transfers between devices, fetch(): lax.ppermute(value, 'fsdp', [(i, (i - 2 * step) % size) for i in range(si...  48.9 us
    ppermute x24, waiting for transfers between devices, swap(): lax.ppermute(value, axis, [(i, i ^ bit) for i in range(lax.axis_size(axis...  38.1 us
    ppermute x24, starting transfers between devices, swap(): lax.ppermute(value, axis, [(i, i ^ bit) for i in range(lax.axis_size(axis...  25.8 us
    pallas_call x2, Pallas kernels, normed_input(): pl.pallas_call(functools.partial(norm_kernel, order, rows), grid=(tokens...  19.1 us
    pallas_call x3, Pallas kernels, early_keys(): pl.pallas_call(functools.partial(early_kernel, counts, bool(before)), gri...  14.6 us
    ppermute x8, starting transfers between devices, fetch(): lax.ppermute(value, 'fsdp', [(i, (i - 2 * step) % size) for i in range(si...  14.3 us
    pallas_call x4, Pallas kernels, grad_blocks(): pl.pallas_call(grad_kernel, grid=(count,), in_specs=[pl.BlockSpec((tokens...  10.6 us
    pallas_call x1, Pallas kernels, late_keys(): pl.pallas_call(functools.partial(late_kernel, counts), grid=(tokens // KE...  6.99 us
  transfers between devices with their start and end apart: 32, of which 15 were waited for; matrix products, arithmetic and copies ran while one was open for 4% of the time, Pallas kernels for 23%

profile of v4, /device:TPU:0, one launch (start us, length us, event | category | flops | bytes accessed | tf_op | source)
XLA Modules:
  0.0 198.1 jit_solution(8409570653485260695)
XLA Ops:
  0.6 3.0 %collective-permute-start.2 = (bf16[640,512]{1,0:T(8,128)(2,1)}, bf16[640,512]{1,0:T(8,128)(2,1)S(1)}, u32[]{:S(2)}, u32[]{:S(2)}) collective-permute-start(bf16[640,512]{1,0:T(8,128)(2,1)} %bitcast.41), channel_id=1, source_target_pairs={{0,1},{1,0},{2,3},{3,2},{4,5},{5,4},{6,7},{7,6},{8,9},{9,8},{10,11... | collective-permute-start | bytes 1966088 | tf_op jit(solution)/shard_map/ppermute | solution.py:243
  3.7 3.6 %collective-permute-start.4 = (bf16[640,512]{1,0:T(8,128)(2,1)}, bf16[640,512]{1,0:T(8,128)(2,1)S(1)}, u32[]{:S(2)}, u32[]{:S(2)}) collective-permute-start(bf16[640,512]{1,0:T(8,128)(2,1)} %bitcast.42), channel_id=1, source_target_pairs={{0,6},{1,7},{2,0},{3,1},{4,2},{5,3},{6,4},{7,5},{8,14},{9,15},{10,... | collective-permute-start | bytes 1966088 | tf_op jit(solution)/shard_map/ppermute | solution.py:248
  8.8 9.8 %collective-permute-done.2.refs_1_ = bf16[640,512]{1,0:T(8,128)(2,1)S(1)} collective-permute-done((bf16[640,512]{1,0:T(8,128)(2,1)}, bf16[640,512]{1,0:T(8,128)(2,1)S(1)}, u32[]{:S(2)}, u32[]{:S(2)}) %collective-permute-start.2) | collective-permute-done | bytes 655392 | tf_op jit(solution)/shard_map/ppermute | solution.py:243
  18.6 1.7 collective-permute-start.3
  25.5 9.6 %norm_input.2.normed_ref.student_ref.refs_5_ = bf16[768,5120]{1,0:T(8,128)(2,1)} custom-call(s32[1]{0:T(128)} %bitcast.place_ref, bf16[768,5120]{1,0:T(8,128)(2,1)} %bitcast.48, f32[1,5120]{1,0:T(1,128)S(1)} %get-tuple-element.103.gain_ref), custom_call_target="tpu_custom_call" | custom-call | flops 1 | bytes 1 | tf_op jit(solution)/shard_map/norm_input/pallas_call | solution.py:33
  35.1 2.8 %collective-permute-done = bf16[1,5248]{1,0:T(2,128)(2,1)S(1)} collective-permute-done((bf16[1,5248]{1,0:T(2,128)(2,1)S(1)}, bf16[1,5248]{1,0:T(2,128)(2,1)S(1)}, u32[]{:S(2)}, u32[]{:S(2)}) %collective-permute-start) | collective-permute-done | bytes 10528 | tf_op jit(solution)/shard_map/ppermute | solution.py:243
  42.4 9.5 %norm_input.3.normed_ref.teacher_ref = bf16[768,5120]{1,0:T(8,128)(2,1)} custom-call(s32[1]{0:T(128)} %bitcast.place_ref, bf16[768,5120]{1,0:T(8,128)(2,1)} %bitcast.49, f32[1,5120]{1,0:T(1,128)S(1)} %slice.67.gain_ref), custom_call_target="tpu_custom_call" | custom-call | flops 1 | bytes 1 | tf_op jit(solution)/shard_map/norm_input/pallas_call | solution.py:33
  51.9 17.5 %collective-permute-done.6.refs_5_.refs_1_ = bf16[640,512]{1,0:T(8,128)(2,1)S(1)} collective-permute-done((bf16[640,512]{1,0:T(8,128)(2,1)S(1)}, bf16[640,512]{1,0:T(8,128)(2,1)S(1)}, u32[]{:S(2)}, u32[]{:S(2)}) %collective-permute-start.6) | collective-permute-done | bytes 655392 | tf_op jit(solution)/shard_map/ppermute | solution.py:248
  73.3 1.9 collective-permute-start.16
  76.6 6.7 %early_keys.3.part_s_ref = f32[768,512]{1,0:T(8,128)S(1)} custom-call(s32[1]{0:T(128)} %bitcast.2.choice_ref, bf16[768,5120]{1,0:T(8,128)(2,1)} %norm_input.2.normed_ref.student_ref.refs_5_, bf16[640,512]{1,0:T(8,128)(2,1)S(1)} %bitcast.47, bf16[640,512]{1,0:T(8,128)(2,1)S(1)} %collective-permute-done.2.refs_1_, ...), custom_call_target="tpu_custom_call" | custom-call | flops 1 | bytes 1 | tf_op jit(solution)/shard_map/early_keys/pallas_call | solution.py:117
  83.4 5.6 %collective-permute-done.13.refs_3_.refs_1_ = bf16[640,512]{1,0:T(8,128)(2,1)S(1)} collective-permute-done((bf16[640,512]{1,0:T(8,128)(2,1)S(1)}, bf16[640,512]{1,0:T(8,128)(2,1)S(1)}, u32[]{:S(2)}, u32[]{:S(2)}) %collective-permute-start.13) | collective-permute-done | bytes 655392 | tf_op jit(solution)/shard_map/ppermute | solution.py:243
  90.8 4.6 %early_keys.4.refs_3_ = f32[768,512]{1,0:T(8,128)S(1)} custom-call(s32[1]{0:T(128)} %bitcast.2.choice_ref, bf16[768,5120]{1,0:T(8,128)(2,1)} %norm_input.3.normed_ref.teacher_ref, bf16[640,512]{1,0:T(8,128)(2,1)S(1)} %collective-permute-done.1.refs_4_.refs_0_, bf16[640,512]{1,0:T(8,128)(2,1)S(1)} %collective-permute-done.3.refs_5_.refs_1_, ...), custom_call_target="tpu_custom_call" | custom-call | flops 1 | bytes 1 | tf_op jit(solution)/shard_map/early_keys/pallas_call | solution.py:117
  95.4 9.4 %collective-permute-done.16.refs_1_ = bf16[640,512]{1,0:T(8,128)(2,1)S(1)} collective-permute-done((bf16[640,512]{1,0:T(8,128)(2,1)S(1)}, bf16[640,512]{1,0:T(8,128)(2,1)S(1)}, u32[]{:S(2)}, u32[]{:S(2)}) %collective-permute-start.16) | collective-permute-done | bytes 655392 | tf_op jit(solution)/shard_map/ppermute | solution.py:248
  105.4 3.3 %early_keys.5.part_t_ref = f32[768,512]{1,0:T(8,128)S(1)} custom-call(s32[1]{0:T(128)} %bitcast.2.choice_ref, bf16[768,5120]{1,0:T(8,128)(2,1)} %norm_input.3.normed_ref.teacher_ref, bf16[640,512]{1,0:T(8,128)(2,1)S(1)} %collective-permute-done.12.refs_2_.refs_0_, bf16[640,512]{1,0:T(8,128)(2,1)S(1)} %collective-permute-done.13.refs_3_.refs_1_, ...), custom_call_target="tpu_custom_call" | custom-call | flops 1 | bytes 1 | tf_op jit(solution)/shard_map/early_keys/pallas_call | solution.py:117
  108.7 7.0 %late_keys.1 = (bf16[768,512]{1,0:T(8,128)(2,1)S(1)}, f32[8,128]{1,0:T(8,128)S(1)}, bf16[512,640]{1,0:T(8,128)(2,1)S(1)}) custom-call(s32[1]{0:T(128)} %bitcast.2.choice_ref, bf16[768,5120]{1,0:T(8,128)(2,1)} %norm_input.2.normed_ref.student_ref.refs_5_, bf16[768,5120]{1,0:T(8,128)(2,1)} %norm_input.3.normed_ref.teacher_ref, ...), custom_call_target="tpu_custom_call" | custom-call | flops 1 | bytes 1 | tf_op jit(solution)/shard_map/late_keys/pallas_call | solution.py:192
  117.1 1.6 collective-permute-start.23
  118.7 2.0 %grad_blocks.7 = f32[1,512,640]{2,1,0:T(8,128)S(1)} custom-call(bf16[768,512]{1,0:T(8,128)(2,1)S(1)} %get-tuple-element.74.grad_ref, bf16[768,5120]{1,0:T(8,128)(2,1)} %norm_input.2.normed_ref.student_ref.refs_5_), custom_call_target="tpu_custom_call" | custom-call | flops 1 | bytes 1 | tf_op jit(solution)/shard_map/grad_blocks/pallas_call | solution.py:227
  120.8 1.9 collective-permute-start.24
  122.7 1.6 collective-permute-start.22
  126.4 2.7 %collective-permute-start.27 = (bf16[256,640]{1,0:T(8,128)(2,1)S(1)}, bf16[256,640]{1,0:T(8,128)(2,1)}, u32[]{:S(2)}, u32[]{:S(2)}) collective-permute-start(bf16[256,640]{1,0:T(8,128)(2,1)S(1)} %add_convert_fusion.2), channel_id=1, source_target_pairs={{0,4},{1,5},{2,6},{3,7},{4,0},{5,1},{6,2},{7,3},{8,12},{9,13},{10,... | collective-permute-start | bytes 983048 | tf_op jit(solution)/shard_map/ppermute | solution.py:248
  129.1 2.9 %grad_blocks.4 = bf16[2,512,640]{2,1,0:T(8,128)(2,1)S(1)} custom-call(bf16[768,512]{1,0:T(8,128)(2,1)S(1)} %get-tuple-element.74.grad_ref, bf16[768,5120]{1,0:T(8,128)(2,1)} %norm_input.2.normed_ref.student_ref.refs_5_), custom_call_target="tpu_custom_call" | custom-call | flops 1 | bytes 1 | tf_op jit(solution)/shard_map/grad_blocks/pallas_call | solution.py:227
  133.0 3.1 %collective-permute-start.25 = (bf16[256,640]{1,0:T(8,128)(2,1)S(1)}, bf16[256,640]{1,0:T(8,128)(2,1)}, u32[]{:S(2)}, u32[]{:S(2)}) collective-permute-start(bf16[256,640]{1,0:T(8,128)(2,1)S(1)} %add_convert_fusion.3), channel_id=1, source_target_pairs={{0,4},{1,5},{2,6},{3,7},{4,0},{5,1},{6,2},{7,3},{8,12},{9,13},{10,... | collective-permute-start | bytes 983048 | tf_op jit(solution)/shard_map/ppermute | solution.py:248
  136.2 2.8 %grad_blocks.5 = f32[2,512,640]{2,1,0:T(8,128)S(1)} custom-call(bf16[768,512]{1,0:T(8,128)(2,1)S(1)} %get-tuple-element.74.grad_ref, bf16[768,5120]{1,0:T(8,128)(2,1)} %norm_input.2.normed_ref.student_ref.refs_5_), custom_call_target="tpu_custom_call" | custom-call | flops 1 | bytes 1 | tf_op jit(solution)/shard_map/grad_blocks/pallas_call | solution.py:227
  139.0 2.9 %grad_blocks.6 = f32[2,512,640]{2,1,0:T(8,128)S(1)} custom-call(bf16[768,512]{1,0:T(8,128)(2,1)S(1)} %get-tuple-element.74.grad_ref, bf16[768,5120]{1,0:T(8,128)(2,1)} %norm_input.2.normed_ref.student_ref.refs_5_), custom_call_target="tpu_custom_call" | custom-call | flops 1 | bytes 1 | tf_op jit(solution)/shard_map/grad_blocks/pallas_call | solution.py:227
  141.9 9.5 %collective-permute-done.27 = bf16[256,640]{1,0:T(8,128)(2,1)} collective-permute-done((bf16[256,640]{1,0:T(8,128)(2,1)S(1)}, bf16[256,640]{1,0:T(8,128)(2,1)}, u32[]{:S(2)}, u32[]{:S(2)}) %collective-permute-start.27) | collective-permute-done | bytes 327712 | tf_op jit(solution)/shard_map/ppermute | solution.py:248
  154.0 3.5 %collective-permute-done.25 = bf16[256,640]{1,0:T(8,128)(2,1)} collective-permute-done((bf16[256,640]{1,0:T(8,128)(2,1)S(1)}, bf16[256,640]{1,0:T(8,128)(2,1)}, u32[]{:S(2)}, u32[]{:S(2)}) %collective-permute-start.25) | collective-permute-done | bytes 327712 | tf_op jit(solution)/shard_map/ppermute | solution.py:248
  159.7 9.3 %collective-permute-done.29 = bf16[512,640]{1,0:T(8,128)(2,1)S(1)} collective-permute-done((bf16[512,640]{1,0:T(8,128)(2,1)S(1)}, bf16[512,640]{1,0:T(8,128)(2,1)S(1)}, u32[]{:S(2)}, u32[]{:S(2)}) %collective-permute-start.29) | collective-permute-done | bytes 655392 | tf_op jit(solution)/shard_map/ppermute | solution.py:243
  170.0 2.7 %collective-permute-start.30 = (bf16[512,640]{1,0:T(8,128)(2,1)}, bf16[512,640]{1,0:T(8,128)(2,1)}, u32[]{:S(2)}, u32[]{:S(2)}) collective-permute-start(bf16[512,640]{1,0:T(8,128)(2,1)} %add_convert_fusion), channel_id=1, source_target_pairs={{0,6},{1,7},{2,0},{3,1},{4,2},{5,3},{6,4},{7,5},{8,14},{9,15},{10,... | collective-permute-start | bytes 1966088 | tf_op jit(solution)/shard_map/ppermute | solution.py:248
  173.3 7.1 %collective-permute-done.31 = f32[8,128]{1,0:T(8,128)S(1)} collective-permute-done((f32[8,128]{1,0:T(8,128)S(1)}, f32[8,128]{1,0:T(8,128)S(1)}, u32[]{:S(2)}, u32[]{:S(2)}) %collective-permute-start.31) | collective-permute-done | bytes 4128 | tf_op jit(solution)/shard_map/ppermute | solution.py:243
  182.1 9.1 %collective-permute-done.30 = bf16[512,640]{1,0:T(8,128)(2,1)} collective-permute-done((bf16[512,640]{1,0:T(8,128)(2,1)}, bf16[512,640]{1,0:T(8,128)(2,1)}, u32[]{:S(2)}, u32[]{:S(2)}) %collective-permute-start.30) | collective-permute-done | bytes 655392 | tf_op jit(solution)/shard_map/ppermute | solution.py:248
  191.3 2.9 %fusion.4 = f32[1,640,512]{1,2,0:T(8,128)} fusion(f32[2,512,640]{2,1,0:T(8,128)S(1)} %grad_blocks.6, bf16[512,640]{1,0:T(8,128)(2,1)} %collective-permute-done.30, bf16[512,640]{1,0:T(8,128)(2,1)} %collective-permute-done.28, bf16[512,640]{1,0:T(8,128)(2,1)S(1)} %collective-permute-done.26, bf16[256,640]{1,0:T(8,128)(2,1)} %collective-permute-done.25, ...), kind=kLoop, calls=%fused_computation.8 | loop fusion | flops 3604480 | bytes 5242880 | tf_op jit(solution)/shard_map/broadcast_in_dim | solution.py:371
  194.2 2.8 %copy.8 = f32[1,640,512]{2,1,0:T(8,128)} copy(f32[1,640,512]{1,2,0:T(8,128)} %fusion.4) | data formatting | bytes 2621440
  (69 shorter events, 29.0 us)
Async XLA Ops:
  0.6 18.0 %collective-permute-start.2 = (bf16[640,512]{1,0:T(8,128)(2,1)}, bf16[640,512]{1,0:T(8,128)(2,1)S(1)}, u32[]{:S(2)}, u32[]{:S(2)}) collective-permute-start(bf16[640,512]{1,0:T(8,128)(2,1)} %bitcast.41), channel_id=1, source_target_pairs={{0,1},{1,0},{2,3},{3,2},{4,5},{5,4},{6,7},{7,6},{8,9},{9,8},{10,11... | collective-permute-start | bytes 1966088 | tf_op jit(solution)/shard_map/ppermute | solution.py:243
  3.7 34.2 %collective-permute-start.4 = (bf16[640,512]{1,0:T(8,128)(2,1)}, bf16[640,512]{1,0:T(8,128)(2,1)S(1)}, u32[]{:S(2)}, u32[]{:S(2)}) collective-permute-start(bf16[640,512]{1,0:T(8,128)(2,1)} %bitcast.42), channel_id=1, source_target_pairs={{0,6},{1,7},{2,0},{3,1},{4,2},{5,3},{6,4},{7,5},{8,14},{9,15},{10,... | collective-permute-start | bytes 1966088 | tf_op jit(solution)/shard_map/ppermute | solution.py:248
  7.3 30.6 %collective-permute-start.1 = (bf16[640,512]{1,0:T(8,128)(2,1)}, bf16[640,512]{1,0:T(8,128)(2,1)S(1)}, u32[]{:S(2)}, u32[]{:S(2)}) collective-permute-start(bf16[640,512]{1,0:T(8,128)(2,1)} %bitcast.43), channel_id=1, source_target_pairs={{0,16},{8,24},{16,0},{24,8},{1,17},{9,25},{17,1},{25,9},{2,18},{10... | collective-permute-start | bytes 1966088 | tf_op jit(solution)/shard_map/ppermute | solution.py:243
  8.8 29.1 %collective-permute-start.5 = (bf16[640,512]{1,0:T(8,128)(2,1)}, bf16[640,512]{1,0:T(8,128)(2,1)S(1)}, u32[]{:S(2)}, u32[]{:S(2)}) collective-permute-start(bf16[640,512]{1,0:T(8,128)(2,1)} %bitcast.44), channel_id=1, source_target_pairs={{0,2},{1,3},{2,4},{3,5},{4,6},{5,7},{6,0},{7,1},{8,10},{9,11},{10,... | collective-permute-start | bytes 1966088 | tf_op jit(solution)/shard_map/ppermute | solution.py:248
  18.6 19.3 %collective-permute-start.3 = (bf16[640,512]{1,0:T(8,128)(2,1)S(1)}, bf16[640,512]{1,0:T(8,128)(2,1)S(1)}, u32[]{:S(2)}, u32[]{:S(2)}) collective-permute-start(bf16[640,512]{1,0:T(8,128)(2,1)S(1)} %collective-permute-done.2.refs_1_), channel_id=1, source_target_pairs={{0,16},{8,24},{16,0},{24,8},{1,17},{9,25},{17,1},{25,9},{2,18},{10... | collective-permute-start | bytes 1966088 | tf_op jit(solution)/shard_map/ppermute | solution.py:243
  21.9 16.0 %collective-permute-start = (bf16[1,5248]{1,0:T(2,128)(2,1)S(1)}, bf16[1,5248]{1,0:T(2,128)(2,1)S(1)}, u32[]{:S(2)}, u32[]{:S(2)}) collective-permute-start(bf16[1,5248]{1,0:T(2,128)(2,1)S(1)} %get-tuple-element.107), channel_id=1, source_target_pairs={{0,16},{8,24},{16,0},{24,8},{1,17},{9,25},{17,1},{25,9},{2,18},{10... | collective-permute-start | bytes 31496 | tf_op jit(solution)/shard_map/ppermute | solution.py:243
  38.0 3.8 %collective-permute-start.7 = (bf16[2,5248]{1,0:T(2,128)(2,1)S(1)}, bf16[2,5248]{1,0:T(2,128)(2,1)S(1)}, u32[]{:S(2)}, u32[]{:S(2)}) collective-permute-start(bf16[2,5248]{1,0:T(2,128)(2,1)S(1)} %pad_maximum_fusion), channel_id=1, source_target_pairs={{0,8},{8,0},{16,24},{24,16},{1,9},{9,1},{17,25},{25,17},{2,10},{10... | collective-permute-start | bytes 62984 | tf_op jit(solution)/shard_map/ppermute | solution.py:243
  38.1 31.4 %collective-permute-start.6 = (bf16[640,512]{1,0:T(8,128)(2,1)S(1)}, bf16[640,512]{1,0:T(8,128)(2,1)S(1)}, u32[]{:S(2)}, u32[]{:S(2)}) collective-permute-start(bf16[640,512]{1,0:T(8,128)(2,1)S(1)} %bitcast.45), channel_id=1, source_target_pairs={{0,4},{1,5},{2,6},{3,7},{4,0},{5,1},{6,2},{7,3},{8,12},{9,13},{10,... | collective-permute-start | bytes 1966088 | tf_op jit(solution)/shard_map/ppermute | solution.py:248
  38.3 31.1 %collective-permute-start.10 = (bf16[640,512]{1,0:T(8,128)(2,1)S(1)}, bf16[640,512]{1,0:T(8,128)(2,1)S(1)}, u32[]{:S(2)}, u32[]{:S(2)}) collective-permute-start(bf16[640,512]{1,0:T(8,128)(2,1)S(1)} %collective-permute-done.4.refs_2_), channel_id=1, source_target_pairs={{0,16},{8,24},{16,0},{24,8},{1,17},{9,25},{17,1},{25,9},{2,18},{10... | collective-permute-start | bytes 1966088 | tf_op jit(solution)/shard_map/ppermute | solution.py:243
  39.7 29.7 %collective-permute-start.8 = (bf16[640,512]{1,0:T(8,128)(2,1)S(1)}, bf16[640,512]{1,0:T(8,128)(2,1)S(1)}, u32[]{:S(2)}, u32[]{:S(2)}) collective-permute-start(bf16[640,512]{1,0:T(8,128)(2,1)S(1)} %collective-permute-done.4.refs_2_), channel_id=1, source_target_pairs={{0,1},{1,0},{2,3},{3,2},{4,5},{5,4},{6,7},{7,6},{8,9},{9,8},{10,11... | collective-permute-start | bytes 1966088 | tf_op jit(solution)/shard_map/ppermute | solution.py:243
  41.2 28.2 %collective-permute-start.11 = (bf16[640,512]{1,0:T(8,128)(2,1)S(1)}, bf16[640,512]{1,0:T(8,128)(2,1)S(1)}, u32[]{:S(2)}, u32[]{:S(2)}) collective-permute-start(bf16[640,512]{1,0:T(8,128)(2,1)S(1)} %collective-permute-done.5.refs_3_), channel_id=1, source_target_pairs={{0,16},{8,24},{16,0},{24,8},{1,17},{9,25},{17,1},{25,9},{2,18},{10... | collective-permute-start | bytes 1966088 | tf_op jit(solution)/shard_map/ppermute | solution.py:243
  41.7 28.7 %collective-permute-start.9 = (bf16[640,512]{1,0:T(8,128)(2,1)S(1)}, bf16[640,512]{1,0:T(8,128)(2,1)S(1)}, u32[]{:S(2)}, u32[]{:S(2)}) collective-permute-start(bf16[640,512]{1,0:T(8,128)(2,1)S(1)} %collective-permute-done.5.refs_3_), channel_id=1, source_target_pairs={{0,1},{1,0},{2,3},{3,2},{4,5},{5,4},{6,7},{7,6},{8,9},{9,8},{10,11... | collective-permute-start | bytes 1966088 | tf_op jit(solution)/shard_map/ppermute | solution.py:243
  71.3 19.5 %collective-permute-start.15 = (bf16[2560,512]{1,0:T(8,128)(2,1)S(1)}, bf16[2560,512]{1,0:T(8,128)(2,1)S(1)}, u32[]{:S(2)}, u32[]{:S(2)}) collective-permute-start(bf16[2560,512]{1,0:T(8,128)(2,1)S(1)} %pack_blocks.4), channel_id=1, source_target_pairs={{0,8},{8,0},{16,24},{24,16},{1,9},{9,1},{17,25},{25,17},{2,10},{10... | collective-permute-start | bytes 7864328 | tf_op jit(solution)/shard_map/ppermute | solution.py:243
  71.4 17.6 %collective-permute-start.13 = (bf16[640,512]{1,0:T(8,128)(2,1)S(1)}, bf16[640,512]{1,0:T(8,128)(2,1)S(1)}, u32[]{:S(2)}, u32[]{:S(2)}) collective-permute-start(bf16[640,512]{1,0:T(8,128)(2,1)S(1)} %collective-permute-done.6.refs_5_.refs_1_), channel_id=1, source_target_pairs={{0,16},{8,24},{16,0},{24,8},{1,17},{9,25},{17,1},{25,9},{2,18},{10... | collective-permute-start | bytes 1966088 | tf_op jit(solution)/shard_map/ppermute | solution.py:243
  72.0 18.3 %collective-permute-start.12 = (bf16[640,512]{1,0:T(8,128)(2,1)S(1)}, bf16[640,512]{1,0:T(8,128)(2,1)S(1)}, u32[]{:S(2)}, u32[]{:S(2)}) collective-permute-start(bf16[640,512]{1,0:T(8,128)(2,1)S(1)} %collective-permute-done.10.refs_6_.refs_2_), channel_id=1, source_target_pairs={{0,1},{1,0},{2,3},{3,2},{4,5},{5,4},{6,7},{7,6},{8,9},{9,8},{10,11... | collective-permute-start | bytes 1966088 | tf_op jit(solution)/shard_map/ppermute | solution.py:243
  73.3 31.5 %collective-permute-start.16 = (bf16[640,512]{1,0:T(8,128)(2,1)S(1)}, bf16[640,512]{1,0:T(8,128)(2,1)S(1)}, u32[]{:S(2)}, u32[]{:S(2)}) collective-permute-start(bf16[640,512]{1,0:T(8,128)(2,1)S(1)} %collective-permute-done.2.refs_1_), channel_id=1, source_target_pairs={{0,4},{1,5},{2,6},{3,7},{4,0},{5,1},{6,2},{7,3},{8,12},{9,13},{10,... | collective-permute-start | bytes 1966088 | tf_op jit(solution)/shard_map/ppermute | solution.py:248
  75.1 29.6 %collective-permute-start.17 = (bf16[640,512]{1,0:T(8,128)(2,1)S(1)}, bf16[640,512]{1,0:T(8,128)(2,1)S(1)}, u32[]{:S(2)}, u32[]{:S(2)}) collective-permute-start(bf16[640,512]{1,0:T(8,128)(2,1)S(1)} %collective-permute-done.9.refs_0_), channel_id=1, source_target_pairs={{0,16},{8,24},{16,0},{24,8},{1,17},{9,25},{17,1},{25,9},{2,18},{10... | collective-permute-start | bytes 1966088 | tf_op jit(solution)/shard_map/ppermute | solution.py:243
  89.0 15.8 %collective-permute-start.18 = (bf16[640,512]{1,0:T(8,128)(2,1)S(1)}, bf16[640,512]{1,0:T(8,128)(2,1)S(1)}, u32[]{:S(2)}, u32[]{:S(2)}) collective-permute-start(bf16[640,512]{1,0:T(8,128)(2,1)S(1)} %collective-permute-done.13.refs_3_.refs_1_), channel_id=1, source_target_pairs={{0,1},{1,0},{2,3},{3,2},{4,5},{5,4},{6,7},{7,6},{8,9},{9,8},{10,11... | collective-permute-start | bytes 1966088 | tf_op jit(solution)/shard_map/ppermute | solution.py:243
  90.7 14.6 %collective-permute-start.14 = (bf16[1280,512]{1,0:T(8,128)(2,1)S(1)}, bf16[1280,512]{1,0:T(8,128)(2,1)S(1)}, u32[]{:S(2)}, u32[]{:S(2)}) collective-permute-start(bf16[1280,512]{1,0:T(8,128)(2,1)S(1)} %pack_blocks.3), channel_id=1, source_target_pairs={{0,8},{8,0},{16,24},{24,16},{1,9},{9,1},{17,25},{25,17},{2,10},{10... | collective-permute-start | bytes 3932168 | tf_op jit(solution)/shard_map/ppermute | solution.py:243
  105.3 3.4 %collective-permute-start.19 = (bf16[1280,512]{1,0:T(8,128)(2,1)S(1)}, bf16[1280,512]{1,0:T(8,128)(2,1)S(1)}, u32[]{:S(2)}, u32[]{:S(2)}) collective-permute-start(bf16[1280,512]{1,0:T(8,128)(2,1)S(1)} %pack_blocks.5), channel_id=1, source_target_pairs={{0,8},{8,0},{16,24},{24,16},{1,9},{9,1},{17,25},{25,17},{2,10},{10... | collective-permute-start | bytes 3932168 | tf_op jit(solution)/shard_map/ppermute | solution.py:243
  115.8 10.6 %collective-permute-start.20 = (bf16[256,640]{1,0:T(8,128)(2,1)S(1)}, bf16[256,640]{1,0:T(8,128)(2,1)S(1)}, u32[]{:S(2)}, u32[]{:S(2)}) collective-permute-start(bf16[256,640]{1,0:T(8,128)(2,1)S(1)} %get-tuple-element.101), channel_id=1, source_target_pairs={{0,1},{1,0},{2,3},{3,2},{4,5},{5,4},{6,7},{7,6},{8,9},{9,8},{10,11... | collective-permute-start | bytes 983048 | tf_op jit(solution)/shard_map/ppermute | solution.py:243
  117.1 3.6 %collective-permute-start.23 = (f32[8,128]{1,0:T(8,128)S(1)}, f32[8,128]{1,0:T(8,128)S(1)}, u32[]{:S(2)}, u32[]{:S(2)}) collective-permute-start(f32[8,128]{1,0:T(8,128)S(1)} %get-tuple-element.78), channel_id=1, source_target_pairs={{0,2},{1,3},{2,0},{3,1},{4,6},{5,7},{6,4},{7,5},{8,10},{9,11},{10,... | collective-permute-start | bytes 12296 | tf_op jit(solution)/shard_map/ppermute | solution.py:243
  120.8 4.6 %collective-permute-start.24 = (f32[8,128]{1,0:T(8,128)S(1)}, f32[8,128]{1,0:T(8,128)S(1)}, u32[]{:S(2)}, u32[]{:S(2)}) collective-permute-start(f32[8,128]{1,0:T(8,128)S(1)} %add.42), channel_id=1, source_target_pairs={{0,4},{1,5},{2,6},{3,7},{4,0},{5,1},{6,2},{7,3},{8,12},{9,13},{10,... | collective-permute-start | bytes 12296 | tf_op jit(solution)/shard_map/ppermute | solution.py:243
  122.7 10.2 %collective-permute-start.22 = (bf16[256,640]{1,0:T(8,128)(2,1)S(1)}, bf16[256,640]{1,0:T(8,128)(2,1)S(1)}, u32[]{:S(2)}, u32[]{:S(2)}) collective-permute-start(bf16[256,640]{1,0:T(8,128)(2,1)S(1)} %get-tuple-element.75), channel_id=1, source_target_pairs={{0,1},{1,0},{2,3},{3,2},{4,5},{5,4},{6,7},{7,6},{8,9},{9,8},{10,11... | collective-permute-start | bytes 983048 | tf_op jit(solution)/shard_map/ppermute | solution.py:243
  126.4 24.9 %collective-permute-start.27 = (bf16[256,640]{1,0:T(8,128)(2,1)S(1)}, bf16[256,640]{1,0:T(8,128)(2,1)}, u32[]{:S(2)}, u32[]{:S(2)}) collective-permute-start(bf16[256,640]{1,0:T(8,128)(2,1)S(1)} %add_convert_fusion.2), channel_id=1, source_target_pairs={{0,4},{1,5},{2,6},{3,7},{4,0},{5,1},{6,2},{7,3},{8,12},{9,13},{10,... | collective-permute-start | bytes 983048 | tf_op jit(solution)/shard_map/ppermute | solution.py:248
  132.1 25.3 %collective-permute-start.21 = (bf16[512,640]{1,0:T(8,128)(2,1)S(1)}, bf16[512,640]{1,0:T(8,128)(2,1)S(1)}, u32[]{:S(2)}, u32[]{:S(2)}) collective-permute-start(bf16[512,640]{1,0:T(8,128)(2,1)S(1)} %get-tuple-element.73), channel_id=1, source_target_pairs={{0,1},{1,0},{2,3},{3,2},{4,5},{5,4},{6,7},{7,6},{8,9},{9,8},{10,11... | collective-permute-start | bytes 1966088 | tf_op jit(solution)/shard_map/ppermute | solution.py:243
  133.0 24.4 %collective-permute-start.25 = (bf16[256,640]{1,0:T(8,128)(2,1)S(1)}, bf16[256,640]{1,0:T(8,128)(2,1)}, u32[]{:S(2)}, u32[]{:S(2)}) collective-permute-start(bf16[256,640]{1,0:T(8,128)(2,1)S(1)} %add_convert_fusion.3), channel_id=1, source_target_pairs={{0,4},{1,5},{2,6},{3,7},{4,0},{5,1},{6,2},{7,3},{8,12},{9,13},{10,... | collective-permute-start | bytes 983048 | tf_op jit(solution)/shard_map/ppermute | solution.py:248
  151.4 17.7 %collective-permute-start.29 = (bf16[512,640]{1,0:T(8,128)(2,1)S(1)}, bf16[512,640]{1,0:T(8,128)(2,1)S(1)}, u32[]{:S(2)}, u32[]{:S(2)}) collective-permute-start(bf16[512,640]{1,0:T(8,128)(2,1)S(1)} %get-tuple-element.86), channel_id=1, source_target_pairs={{0,1},{1,0},{2,3},{3,2},{4,5},{5,4},{6,7},{7,6},{8,9},{9,8},{10,11... | collective-permute-start | bytes 1966088 | tf_op jit(solution)/shard_map/ppermute | solution.py:243
  157.4 24.7 %collective-permute-start.26 = (bf16[512,640]{1,0:T(8,128)(2,1)}, bf16[512,640]{1,0:T(8,128)(2,1)S(1)}, u32[]{:S(2)}, u32[]{:S(2)}) collective-permute-start(bf16[512,640]{1,0:T(8,128)(2,1)} %fusion.5), channel_id=1, source_target_pairs={{0,1},{1,0},{2,3},{3,2},{4,5},{5,4},{6,7},{7,6},{8,9},{9,8},{10,11... | collective-permute-start | bytes 1966088 | tf_op jit(solution)/shard_map/ppermute | solution.py:243
  159.7 22.4 %collective-permute-start.28 = (bf16[512,640]{1,0:T(8,128)(2,1)}, bf16[512,640]{1,0:T(8,128)(2,1)}, u32[]{:S(2)}, u32[]{:S(2)}) collective-permute-start(bf16[512,640]{1,0:T(8,128)(2,1)} %add_convert_fusion.1), channel_id=1, source_target_pairs={{0,2},{1,3},{2,4},{3,5},{4,6},{5,7},{6,0},{7,1},{8,10},{9,11},{10,... | collective-permute-start | bytes 1966088 | tf_op jit(solution)/shard_map/ppermute | solution.py:248
  170.0 21.3 %collective-permute-start.30 = (bf16[512,640]{1,0:T(8,128)(2,1)}, bf16[512,640]{1,0:T(8,128)(2,1)}, u32[]{:S(2)}, u32[]{:S(2)}) collective-permute-start(bf16[512,640]{1,0:T(8,128)(2,1)} %add_convert_fusion), channel_id=1, source_target_pairs={{0,6},{1,7},{2,0},{3,1},{4,2},{5,3},{6,4},{7,5},{8,14},{9,15},{10,... | collective-permute-start | bytes 1966088 | tf_op jit(solution)/shard_map/ppermute | solution.py:248
  172.7 7.6 %collective-permute-start.31 = (f32[8,128]{1,0:T(8,128)S(1)}, f32[8,128]{1,0:T(8,128)S(1)}, u32[]{:S(2)}, u32[]{:S(2)}) collective-permute-start(f32[8,128]{1,0:T(8,128)S(1)} %add.43), channel_id=1, source_target_pairs={{0,1},{1,0},{2,3},{3,2},{4,5},{5,4},{6,7},{7,6},{8,9},{9,8},{10,11... | collective-permute-start | bytes 12296 | tf_op jit(solution)/shard_map/ppermute | solution.py:243
  (1 other events, 12.6 us)

commit v5 on v4

--- a/solution.py
+++ b/solution.py
@@ -239,6 +239,30 @@
     )(grad_keys, in_hbm(student))
 
 
+def finish_kernel(ends_ref, last_ref, far_ref, far_rest_ref, *refs):
+    *near_refs, out_ref = refs
+    far = jnp.concatenate([far_ref[...].astype(jnp.float32), far_rest_ref[...].astype(jnp.float32)], axis=0)
+    total = ends_ref[0] + last_ref[...].astype(jnp.float32) + far
+    for near_ref in near_refs:
+        total = total + near_ref[...].astype(jnp.float32)
+    out_ref[...] = total.T
+
+
+def finish(ends, last, arrived):
+    wide, rows = last.shape
+    blocks = [pl.BlockSpec((array.shape[0], 128), lambda i: (0, i)) for array in (last, *arrived)]
+    return pl.pallas_call(
+        finish_kernel,
+        grid=(rows // 128,),
+        in_specs=[pl.BlockSpec((1, wide, 128), lambda i: (0, 0, i))] + blocks,
+        out_specs=pl.BlockSpec((128, wide), lambda i: (i, 0)),
+        out_shape=jax.ShapeDtypeStruct((rows, wide), jnp.float32),
+        compiler_params=pltpu.CompilerParams(vmem_limit_bytes=VMEM_LIMIT),
+        cost_estimate=SHORT,
+        name="finish",
+    )(ends, last, *arrived)
+
+
 def swap(value, axis, bit):
     return lax.ppermute(value, axis, [(i, i ^ bit) for i in range(lax.axis_size(axis))])
 
@@ -337,18 +361,19 @@
         order.index((far, 1)),
     )
 
-    wide = features // 2
 
     def grads(keys, dtype, *wait):
         return grad_blocks(after(grad_keys, *wait), student, rows, [order.index(key) for key in keys], dtype)
 
-    keep_far = grads([(far, 0)], jnp.float32, give_far)
-    halves = [slice(0, wide), slice(wide, features)]
-    given = [swap(give_far[halves[0]], "fsdp", 1), swap(after(give_far[halves[1]], keep_far), "fsdp", 1)]
-    bit = 2
+    halves = [slice(0, features // 4), slice(features // 4, features)]
+    given = [swap(give_far[halves[0]], "fsdp", 1)]
+    steps, bit = [], 2
     while bit < lax.axis_size("fsdp"):
         sums = sums + swap(sums, "fsdp", bit)
+        steps.append(sums)
         bit *= 2
+    keep_far = grads([(far, 0)], jnp.float32, steps[0])
+    given.append(swap(after(give_far[halves[1]], keep_far), "fsdp", 1))
     pieces = grads([(step, 1) for step in near], jnp.bfloat16, given[0])
     keep = grads([(step, 0) for step in near], jnp.float32, pieces)
     ends = grads([(0, 0), (0, 1)], jnp.float32, keep)
@@ -362,13 +387,11 @@
         arrived.append(fetch(after(summed, [summed, sums, *arrived][at]), -step))
     last = swap(after(ends[1].astype(jnp.bfloat16), given[2], arrived[1]), "fsdp", 1)
     sums = sums + swap(after(sums, given[3]), "fsdp", 1)
-    total = ends[0] + last.astype(jnp.float32) + jnp.concatenate(arrived[:2], axis=0).astype(jnp.float32)
-    for block in arrived[2:]:
-        total = total + block.astype(jnp.float32)
+    total = finish(ends, last, arrived)
 
     tokens_all = tok_rows * lax.axis_size("fsdp")
     distill_loss = (jnp.sum(sums[1]) / (tokens_all * features)).reshape(1)
-    return (total.T[None], sums[:1], distill_loss)
+    return (total[None], sums[:1], distill_loss)
 
 
 def norm_input(hidden, gain):

time: 199 us -> 203 us (1.020)
  waiting for transfers between devices: 87 us -> 97.1 us
  starting transfers between devices: 40.2 us -> 33.8 us
  Pallas kernels: 53 us -> 57.3 us
  other arithmetic: 7.8 us -> 4.89 us
    ppermute x24, waiting for transfers between devices: 38.1 us -> 58.4 us  [swap(): lax.ppermute(value, axis, [(i, i ^ bit) for i in range(lax.axis_size(axis...]
    ppermute x8, waiting for transfers between devices: 48.9 us -> 38.7 us  [fetch(): lax.ppermute(value, 'fsdp', [(i, (i - 2 * step) % size) for i in range(si...]
    ppermute x8, starting transfers between devices: 14.3 us -> 8.15 us  [fetch(): lax.ppermute(value, 'fsdp', [(i, (i - 2 * step) % size) for i in range(si...]
    pallas_call x0 -> x1, Pallas kernels: none -> 4.33 us  [finish(): pl.pallas_call(finish_kernel, grid=(rows // 128,), in_specs=[pl.BlockSpec...]
    broadcast_in_dim x1 -> x0, other arithmetic: 2.94 us -> none  [local(): return (total.T[None], sums[:1], distill_loss)]
  transfers between devices with their start and end apart: 32 -> 32, of which waited for: 15 -> 13; matrix products, arithmetic and copies ran while one was open for 4% -> 4% of each run, Pallas kernels for 23% -> 22%
where the time goes in v5:
time: 203 us; the launch traced here: 202 us
  waiting for transfers between devices  97.1 us (48%)
  Pallas kernels  57.3 us (28%)
  starting transfers between devices  33.8 us (17%)
  other arithmetic  4.89 us (2%)
  between operations  4.7 us (2%)
  local copies, waits for them, and re-layouts  4.48 us (2%)
    ppermute x24, waiting for transfers between devices, swap(): lax.ppermute(value, axis, [(i, i ^ bit) for i in range(lax.axis_size(axis...  58.4 us
    ppermute x8, waiting for transfers between devices, fetch(): lax.ppermute(value, 'fsdp', [(i, (i - 2 * step) % size) for i in range(si...  38.7 us
    ppermute x24, starting transfers between devices, swap(): lax.ppermute(value, axis, [(i, i ^ bit) for i in range(lax.axis_size(axis...  25.6 us
    pallas_call x2, Pallas kernels, normed_input(): pl.pallas_call(functools.partial(norm_kernel, order, rows), grid=(tokens...  19.1 us
    pallas_call x3, Pallas kernels, early_keys(): pl.pallas_call(functools.partial(early_kernel, counts, bool(before)), gri...  14.6 us
    pallas_call x4, Pallas kernels, grad_blocks(): pl.pallas_call(grad_kernel, grid=(count,), in_specs=[pl.BlockSpec((tokens...  10.6 us
    ppermute x8, starting transfers between devices, fetch(): lax.ppermute(value, 'fsdp', [(i, (i - 2 * step) % size) for i in range(si...  8.15 us
    pallas_call x1, Pallas kernels, late_keys(): pl.pallas_call(functools.partial(late_kernel, counts), grid=(tokens // KE...  6.91 us
  transfers between devices with their start and end apart: 32, of which 13 were waited for; matrix products, arithmetic and copies ran while one was open for 4% of the time, Pallas kernels for 22%

profile of v5, /device:TPU:0, one launch (start us, length us, event | category | flops | bytes accessed | tf_op | source)
XLA Modules:
  0.0 202.3 jit_solution(5390896240472679757)
XLA Ops:
  0.6 3.0 %collective-permute-start.2 = (bf16[640,512]{1,0:T(8,128)(2,1)}, bf16[640,512]{1,0:T(8,128)(2,1)S(1)}, u32[]{:S(2)}, u32[]{:S(2)}) collective-permute-start(bf16[640,512]{1,0:T(8,128)(2,1)} %bitcast.26), channel_id=1, source_target_pairs={{0,1},{1,0},{2,3},{3,2},{4,5},{5,4},{6,7},{7,6},{8,9},{9,8},{10,11... | collective-permute-start | bytes 1966088 | tf_op jit(solution)/shard_map/ppermute | solution.py:267
  3.7 3.6 %collective-permute-start.4 = (bf16[640,512]{1,0:T(8,128)(2,1)}, bf16[640,512]{1,0:T(8,128)(2,1)S(1)}, u32[]{:S(2)}, u32[]{:S(2)}) collective-permute-start(bf16[640,512]{1,0:T(8,128)(2,1)} %bitcast.27), channel_id=1, source_target_pairs={{0,6},{1,7},{2,0},{3,1},{4,2},{5,3},{6,4},{7,5},{8,14},{9,15},{10,... | collective-permute-start | bytes 1966088 | tf_op jit(solution)/shard_map/ppermute | solution.py:272
  7.3 1.5 collective-permute-start.1
  8.8 9.8 %collective-permute-done.2.refs_1_ = bf16[640,512]{1,0:T(8,128)(2,1)S(1)} collective-permute-done((bf16[640,512]{1,0:T(8,128)(2,1)}, bf16[640,512]{1,0:T(8,128)(2,1)S(1)}, u32[]{:S(2)}, u32[]{:S(2)}) %collective-permute-start.2) | collective-permute-done | bytes 655392 | tf_op jit(solution)/shard_map/ppermute | solution.py:267
  18.6 1.7 collective-permute-start.3
  25.5 9.6 %norm_input.2.normed_ref.student_ref.refs_5_ = bf16[768,5120]{1,0:T(8,128)(2,1)} custom-call(s32[1]{0:T(128)} %bitcast.place_ref, bf16[768,5120]{1,0:T(8,128)(2,1)} %bitcast.33, f32[1,5120]{1,0:T(1,128)S(1)} %get-tuple-element.96.gain_ref), custom_call_target="tpu_custom_call" | custom-call | flops 1 | bytes 1 | tf_op jit(solution)/shard_map/norm_input/pallas_call | solution.py:33
  35.1 2.8 %collective-permute-done = bf16[1,5248]{1,0:T(2,128)(2,1)S(1)} collective-permute-done((bf16[1,5248]{1,0:T(2,128)(2,1)S(1)}, bf16[1,5248]{1,0:T(2,128)(2,1)S(1)}, u32[]{:S(2)}, u32[]{:S(2)}) %collective-permute-start) | collective-permute-done | bytes 10528 | tf_op jit(solution)/shard_map/ppermute | solution.py:267
  39.7 1.5 collective-permute-start.8
  42.4 9.5 %norm_input.3.normed_ref.teacher_ref = bf16[768,5120]{1,0:T(8,128)(2,1)} custom-call(s32[1]{0:T(128)} %bitcast.place_ref, bf16[768,5120]{1,0:T(8,128)(2,1)} %bitcast.34, f32[1,5120]{1,0:T(1,128)S(1)} %slice.63.gain_ref), custom_call_target="tpu_custom_call" | custom-call | flops 1 | bytes 1 | tf_op jit(solution)/shard_map/norm_input/pallas_call | solution.py:33
  51.9 17.5 %collective-permute-done.6.refs_5_.refs_1_ = bf16[640,512]{1,0:T(8,128)(2,1)S(1)} collective-permute-done((bf16[640,512]{1,0:T(8,128)(2,1)S(1)}, bf16[640,512]{1,0:T(8,128)(2,1)S(1)}, u32[]{:S(2)}, u32[]{:S(2)}) %collective-permute-start.6) | collective-permute-done | bytes 655392 | tf_op jit(solution)/shard_map/ppermute | solution.py:272
  73.3 1.9 collective-permute-start.16
  75.2 1.5 collective-permute-start.17
  76.6 6.7 %early_keys.3.part_s_ref = f32[768,512]{1,0:T(8,128)S(1)} custom-call(s32[1]{0:T(128)} %bitcast.2.choice_ref, bf16[768,5120]{1,0:T(8,128)(2,1)} %norm_input.2.normed_ref.student_ref.refs_5_, bf16[640,512]{1,0:T(8,128)(2,1)S(1)} %bitcast.32, bf16[640,512]{1,0:T(8,128)(2,1)S(1)} %collective-permute-done.2.refs_1_, ...), custom_call_target="tpu_custom_call" | custom-call | flops 1 | bytes 1 | tf_op jit(solution)/shard_map/early_keys/pallas_call | solution.py:117
  83.4 5.6 %collective-permute-done.13.refs_3_.refs_1_ = bf16[640,512]{1,0:T(8,128)(2,1)S(1)} collective-permute-done((bf16[640,512]{1,0:T(8,128)(2,1)S(1)}, bf16[640,512]{1,0:T(8,128)(2,1)S(1)}, u32[]{:S(2)}, u32[]{:S(2)}) %collective-permute-start.13) | collective-permute-done | bytes 655392 | tf_op jit(solution)/shard_map/ppermute | solution.py:267
  90.8 4.6 %early_keys.4.refs_3_ = f32[768,512]{1,0:T(8,128)S(1)} custom-call(s32[1]{0:T(128)} %bitcast.2.choice_ref, bf16[768,5120]{1,0:T(8,128)(2,1)} %norm_input.3.normed_ref.teacher_ref, bf16[640,512]{1,0:T(8,128)(2,1)S(1)} %collective-permute-done.1.refs_4_.refs_0_, bf16[640,512]{1,0:T(8,128)(2,1)S(1)} %collective-permute-done.3.refs_5_.refs_1_, ...), custom_call_target="tpu_custom_call" | custom-call | flops 1 | bytes 1 | tf_op jit(solution)/shard_map/early_keys/pallas_call | solution.py:117
  95.4 9.4 %collective-permute-done.16.refs_1_ = bf16[640,512]{1,0:T(8,128)(2,1)S(1)} collective-permute-done((bf16[640,512]{1,0:T(8,128)(2,1)S(1)}, bf16[640,512]{1,0:T(8,128)(2,1)S(1)}, u32[]{:S(2)}, u32[]{:S(2)}) %collective-permute-start.16) | collective-permute-done | bytes 655392 | tf_op jit(solution)/shard_map/ppermute | solution.py:272
  105.4 3.3 %early_keys.5.part_t_ref = f32[768,512]{1,0:T(8,128)S(1)} custom-call(s32[1]{0:T(128)} %bitcast.2.choice_ref, bf16[768,5120]{1,0:T(8,128)(2,1)} %norm_input.3.normed_ref.teacher_ref, bf16[640,512]{1,0:T(8,128)(2,1)S(1)} %collective-permute-done.12.refs_2_.refs_0_, bf16[640,512]{1,0:T(8,128)(2,1)S(1)} %collective-permute-done.13.refs_3_.refs_1_, ...), custom_call_target="tpu_custom_call" | custom-call | flops 1 | bytes 1 | tf_op jit(solution)/shard_map/early_keys/pallas_call | solution.py:117
  108.7 6.9 %late_keys.1 = (bf16[768,512]{1,0:T(8,128)(2,1)S(1)}, f32[8,128]{1,0:T(8,128)S(1)}, bf16[512,640]{1,0:T(8,128)(2,1)S(1)}) custom-call(s32[1]{0:T(128)} %bitcast.2.choice_ref, bf16[768,5120]{1,0:T(8,128)(2,1)} %norm_input.2.normed_ref.student_ref.refs_5_, bf16[768,5120]{1,0:T(8,128)(2,1)} %norm_input.3.normed_ref.teacher_ref, ...), custom_call_target="tpu_custom_call" | custom-call | flops 1 | bytes 1 | tf_op jit(solution)/shard_map/late_keys/pallas_call | solution.py:192
  115.6 1.4 collective-permute-start.22
  117.1 1.6 collective-permute-start.20
  119.3 2.7 %collective-permute-start.24 = (f32[8,128]{1,0:T(8,128)S(1)}, f32[8,128]{1,0:T(8,128)S(1)}, u32[]{:S(2)}, u32[]{:S(2)}) collective-permute-start(f32[8,128]{1,0:T(8,128)S(1)} %add.29), channel_id=1, source_target_pairs={{0,4},{1,5},{2,6},{3,7},{4,0},{5,1},{6,2},{7,3},{8,12},{9,13},{10,... | collective-permute-start | bytes 12296 | tf_op jit(solution)/shard_map/ppermute | solution.py:267
  122.0 2.0 grad_blocks.7
  124.7 2.9 %grad_blocks.4 = bf16[2,512,640]{2,1,0:T(8,128)(2,1)S(1)} custom-call(bf16[768,512]{1,0:T(8,128)(2,1)S(1)} %get-tuple-element.75.grad_ref, bf16[768,5120]{1,0:T(8,128)(2,1)} %norm_input.2.normed_ref.student_ref.refs_5_), custom_call_target="tpu_custom_call" | custom-call | flops 1 | bytes 1 | tf_op jit(solution)/shard_map/grad_blocks/pallas_call | solution.py:227
  127.7 1.9 collective-permute-start.27
  129.6 2.9 %grad_blocks.5 = f32[2,512,640]{2,1,0:T(8,128)S(1)} custom-call(bf16[768,512]{1,0:T(8,128)(2,1)S(1)} %get-tuple-element.75.grad_ref, bf16[768,5120]{1,0:T(8,128)(2,1)} %norm_input.2.normed_ref.student_ref.refs_5_), custom_call_target="tpu_custom_call" | custom-call | flops 1 | bytes 1 | tf_op jit(solution)/shard_map/grad_blocks/pallas_call | solution.py:227
  133.2 2.9 %grad_blocks.6.ends_ref = f32[2,512,640]{2,1,0:T(8,128)S(1)} custom-call(bf16[768,512]{1,0:T(8,128)(2,1)S(1)} %get-tuple-element.75.grad_ref, bf16[768,5120]{1,0:T(8,128)(2,1)} %norm_input.2.normed_ref.student_ref.refs_5_), custom_call_target="tpu_custom_call" | custom-call | flops 1 | bytes 1 | tf_op jit(solution)/shard_map/grad_blocks/pallas_call | solution.py:227
  139.9 12.5 %collective-permute-done.21 = bf16[512,640]{1,0:T(8,128)(2,1)S(1)} collective-permute-done((bf16[512,640]{1,0:T(8,128)(2,1)S(1)}, bf16[512,640]{1,0:T(8,128)(2,1)S(1)}, u32[]{:S(2)}, u32[]{:S(2)}) %collective-permute-start.21) | collective-permute-done | bytes 655392 | tf_op jit(solution)/shard_map/ppermute | solution.py:267
  153.3 11.1 %collective-permute-done.29 = bf16[512,640]{1,0:T(8,128)(2,1)S(1)} collective-permute-done((bf16[512,640]{1,0:T(8,128)(2,1)S(1)}, bf16[512,640]{1,0:T(8,128)(2,1)S(1)}, u32[]{:S(2)}, u32[]{:S(2)}) %collective-permute-start.29) | collective-permute-done | bytes 655392 | tf_op jit(solution)/shard_map/ppermute | solution.py:267
  165.4 10.8 %collective-permute-done.25.far_rest_ref = bf16[384,640]{1,0:T(8,128)(2,1)S(1)} collective-permute-done((bf16[384,640]{1,0:T(8,128)(2,1)S(1)}, bf16[384,640]{1,0:T(8,128)(2,1)S(1)}, u32[]{:S(2)}, u32[]{:S(2)}) %collective-permute-start.25) | collective-permute-done | bytes 491552 | tf_op jit(solution)/shard_map/ppermute | solution.py:272
  177.0 1.5 collective-permute-start.26
  179.0 15.0 %collective-permute-done.31 = f32[8,128]{1,0:T(8,128)S(1)} collective-permute-done((f32[8,128]{1,0:T(8,128)S(1)}, f32[8,128]{1,0:T(8,128)S(1)}, u32[]{:S(2)}, u32[]{:S(2)}) %collective-permute-start.31) | collective-permute-done | bytes 4128 | tf_op jit(solution)/shard_map/ppermute | solution.py:267
  196.8 4.3 %finish.1 = f32[640,512]{1,0:T(8,128)} custom-call(f32[2,512,640]{2,1,0:T(8,128)S(1)} %grad_blocks.6.ends_ref, bf16[512,640]{1,0:T(8,128)(2,1)} %collective-permute-done.26.last_ref, bf16[128,640]{1,0:T(8,128)(2,1)S(1)} %collective-permute-done.27.far_ref, bf16[384,640]{1,0:T(8,128)(2,1)S(1)} %copy-done.2, ...), custom_call_target="tpu_custom_call" | custom-call | flops 1 | bytes 1 | tf_op jit(solution)/shard_map/finish/pallas_call | solution.py:254
  (74 shorter events, 23.9 us)
Async XLA Ops:
  0.6 18.0 %collective-permute-start.2 = (bf16[640,512]{1,0:T(8,128)(2,1)}, bf16[640,512]{1,0:T(8,128)(2,1)S(1)}, u32[]{:S(2)}, u32[]{:S(2)}) collective-permute-start(bf16[640,512]{1,0:T(8,128)(2,1)} %bitcast.26), channel_id=1, source_target_pairs={{0,1},{1,0},{2,3},{3,2},{4,5},{5,4},{6,7},{7,6},{8,9},{9,8},{10,11... | collective-permute-start | bytes 1966088 | tf_op jit(solution)/shard_map/ppermute | solution.py:267
  3.7 34.2 %collective-permute-start.4 = (bf16[640,512]{1,0:T(8,128)(2,1)}, bf16[640,512]{1,0:T(8,128)(2,1)S(1)}, u32[]{:S(2)}, u32[]{:S(2)}) collective-permute-start(bf16[640,512]{1,0:T(8,128)(2,1)} %bitcast.27), channel_id=1, source_target_pairs={{0,6},{1,7},{2,0},{3,1},{4,2},{5,3},{6,4},{7,5},{8,14},{9,15},{10,... | collective-permute-start | bytes 1966088 | tf_op jit(solution)/shard_map/ppermute | solution.py:272
  7.3 30.6 %collective-permute-start.1 = (bf16[640,512]{1,0:T(8,128)(2,1)}, bf16[640,512]{1,0:T(8,128)(2,1)S(1)}, u32[]{:S(2)}, u32[]{:S(2)}) collective-permute-start(bf16[640,512]{1,0:T(8,128)(2,1)} %bitcast.28), channel_id=1, source_target_pairs={{0,16},{8,24},{16,0},{24,8},{1,17},{9,25},{17,1},{25,9},{2,18},{10... | collective-permute-start | bytes 1966088 | tf_op jit(solution)/shard_map/ppermute | solution.py:267
  8.8 29.1 %collective-permute-start.5 = (bf16[640,512]{1,0:T(8,128)(2,1)}, bf16[640,512]{1,0:T(8,128)(2,1)S(1)}, u32[]{:S(2)}, u32[]{:S(2)}) collective-permute-start(bf16[640,512]{1,0:T(8,128)(2,1)} %bitcast.29), channel_id=1, source_target_pairs={{0,2},{1,3},{2,4},{3,5},{4,6},{5,7},{6,0},{7,1},{8,10},{9,11},{10,... | collective-permute-start | bytes 1966088 | tf_op jit(solution)/shard_map/ppermute | solution.py:272
  18.6 19.3 %collective-permute-start.3 = (bf16[640,512]{1,0:T(8,128)(2,1)S(1)}, bf16[640,512]{1,0:T(8,128)(2,1)S(1)}, u32[]{:S(2)}, u32[]{:S(2)}) collective-permute-start(bf16[640,512]{1,0:T(8,128)(2,1)S(1)} %collective-permute-done.2.refs_1_), channel_id=1, source_target_pairs={{0,16},{8,24},{16,0},{24,8},{1,17},{9,25},{17,1},{25,9},{2,18},{10... | collective-permute-start | bytes 1966088 | tf_op jit(solution)/shard_map/ppermute | solution.py:267
  21.9 16.0 %collective-permute-start = (bf16[1,5248]{1,0:T(2,128)(2,1)S(1)}, bf16[1,5248]{1,0:T(2,128)(2,1)S(1)}, u32[]{:S(2)}, u32[]{:S(2)}) collective-permute-start(bf16[1,5248]{1,0:T(2,128)(2,1)S(1)} %get-tuple-element.100), channel_id=1, source_target_pairs={{0,16},{8,24},{16,0},{24,8},{1,17},{9,25},{17,1},{25,9},{2,18},{10... | collective-permute-start | bytes 31496 | tf_op jit(solution)/shard_map/ppermute | solution.py:267
  38.0 3.8 %collective-permute-start.7 = (bf16[2,5248]{1,0:T(2,128)(2,1)S(1)}, bf16[2,5248]{1,0:T(2,128)(2,1)S(1)}, u32[]{:S(2)}, u32[]{:S(2)}) collective-permute-start(bf16[2,5248]{1,0:T(2,128)(2,1)S(1)} %pad_maximum_fusion), channel_id=1, source_target_pairs={{0,8},{8,0},{16,24},{24,16},{1,9},{9,1},{17,25},{25,17},{2,10},{10... | collective-permute-start | bytes 62984 | tf_op jit(solution)/shard_map/ppermute | solution.py:267
  38.1 31.4 %collective-permute-start.6 = (bf16[640,512]{1,0:T(8,128)(2,1)S(1)}, bf16[640,512]{1,0:T(8,128)(2,1)S(1)}, u32[]{:S(2)}, u32[]{:S(2)}) collective-permute-start(bf16[640,512]{1,0:T(8,128)(2,1)S(1)} %bitcast.30), channel_id=1, source_target_pairs={{0,4},{1,5},{2,6},{3,7},{4,0},{5,1},{6,2},{7,3},{8,12},{9,13},{10,... | collective-permute-start | bytes 1966088 | tf_op jit(solution)/shard_map/ppermute | solution.py:272
  38.3 31.1 %collective-permute-start.10 = (bf16[640,512]{1,0:T(8,128)(2,1)S(1)}, bf16[640,512]{1,0:T(8,128)(2,1)S(1)}, u32[]{:S(2)}, u32[]{:S(2)}) collective-permute-start(bf16[640,512]{1,0:T(8,128)(2,1)S(1)} %collective-permute-done.4.refs_2_), channel_id=1, source_target_pairs={{0,16},{8,24},{16,0},{24,8},{1,17},{9,25},{17,1},{25,9},{2,18},{10... | collective-permute-start | bytes 1966088 | tf_op jit(solution)/shard_map/ppermute | solution.py:267
  39.7 29.7 %collective-permute-start.8 = (bf16[640,512]{1,0:T(8,128)(2,1)S(1)}, bf16[640,512]{1,0:T(8,128)(2,1)S(1)}, u32[]{:S(2)}, u32[]{:S(2)}) collective-permute-start(bf16[640,512]{1,0:T(8,128)(2,1)S(1)} %collective-permute-done.4.refs_2_), channel_id=1, source_target_pairs={{0,1},{1,0},{2,3},{3,2},{4,5},{5,4},{6,7},{7,6},{8,9},{9,8},{10,11... | collective-permute-start | bytes 1966088 | tf_op jit(solution)/shard_map/ppermute | solution.py:267
  41.2 28.3 %collective-permute-start.11 = (bf16[640,512]{1,0:T(8,128)(2,1)S(1)}, bf16[640,512]{1,0:T(8,128)(2,1)S(1)}, u32[]{:S(2)}, u32[]{:S(2)}) collective-permute-start(bf16[640,512]{1,0:T(8,128)(2,1)S(1)} %collective-permute-done.5.refs_3_), channel_id=1, source_target_pairs={{0,16},{8,24},{16,0},{24,8},{1,17},{9,25},{17,1},{25,9},{2,18},{10... | collective-permute-start | bytes 1966088 | tf_op jit(solution)/shard_map/ppermute | solution.py:267
  41.7 28.7 %collective-permute-start.9 = (bf16[640,512]{1,0:T(8,128)(2,1)S(1)}, bf16[640,512]{1,0:T(8,128)(2,1)S(1)}, u32[]{:S(2)}, u32[]{:S(2)}) collective-permute-start(bf16[640,512]{1,0:T(8,128)(2,1)S(1)} %collective-permute-done.5.refs_3_), channel_id=1, source_target_pairs={{0,1},{1,0},{2,3},{3,2},{4,5},{5,4},{6,7},{7,6},{8,9},{9,8},{10,11... | collective-permute-start | bytes 1966088 | tf_op jit(solution)/shard_map/ppermute | solution.py:267
  71.3 19.5 %collective-permute-start.15 = (bf16[2560,512]{1,0:T(8,128)(2,1)S(1)}, bf16[2560,512]{1,0:T(8,128)(2,1)S(1)}, u32[]{:S(2)}, u32[]{:S(2)}) collective-permute-start(bf16[2560,512]{1,0:T(8,128)(2,1)S(1)} %pack_blocks.4), channel_id=1, source_target_pairs={{0,8},{8,0},{16,24},{24,16},{1,9},{9,1},{17,25},{25,17},{2,10},{10... | collective-permute-start | bytes 7864328 | tf_op jit(solution)/shard_map/ppermute | solution.py:267
  71.4 17.6 %collective-permute-start.13 = (bf16[640,512]{1,0:T(8,128)(2,1)S(1)}, bf16[640,512]{1,0:T(8,128)(2,1)S(1)}, u32[]{:S(2)}, u32[]{:S(2)}) collective-permute-start(bf16[640,512]{1,0:T(8,128)(2,1)S(1)} %collective-permute-done.6.refs_5_.refs_1_), channel_id=1, source_target_pairs={{0,16},{8,24},{16,0},{24,8},{1,17},{9,25},{17,1},{25,9},{2,18},{10... | collective-permute-start | bytes 1966088 | tf_op jit(solution)/shard_map/ppermute | solution.py:267
  72.0 18.3 %collective-permute-start.12 = (bf16[640,512]{1,0:T(8,128)(2,1)S(1)}, bf16[640,512]{1,0:T(8,128)(2,1)S(1)}, u32[]{:S(2)}, u32[]{:S(2)}) collective-permute-start(bf16[640,512]{1,0:T(8,128)(2,1)S(1)} %collective-permute-done.10.refs_6_.refs_2_), channel_id=1, source_target_pairs={{0,1},{1,0},{2,3},{3,2},{4,5},{5,4},{6,7},{7,6},{8,9},{9,8},{10,11... | collective-permute-start | bytes 1966088 | tf_op jit(solution)/shard_map/ppermute | solution.py:267
  73.3 31.5 %collective-permute-start.16 = (bf16[640,512]{1,0:T(8,128)(2,1)S(1)}, bf16[640,512]{1,0:T(8,128)(2,1)S(1)}, u32[]{:S(2)}, u32[]{:S(2)}) collective-permute-start(bf16[640,512]{1,0:T(8,128)(2,1)S(1)} %collective-permute-done.2.refs_1_), channel_id=1, source_target_pairs={{0,4},{1,5},{2,6},{3,7},{4,0},{5,1},{6,2},{7,3},{8,12},{9,13},{10,... | collective-permute-start | bytes 1966088 | tf_op jit(solution)/shard_map/ppermute | solution.py:272
  75.2 29.6 %collective-permute-start.17 = (bf16[640,512]{1,0:T(8,128)(2,1)S(1)}, bf16[640,512]{1,0:T(8,128)(2,1)S(1)}, u32[]{:S(2)}, u32[]{:S(2)}) collective-permute-start(bf16[640,512]{1,0:T(8,128)(2,1)S(1)} %collective-permute-done.9.refs_0_), channel_id=1, source_target_pairs={{0,16},{8,24},{16,0},{24,8},{1,17},{9,25},{17,1},{25,9},{2,18},{10... | collective-permute-start | bytes 1966088 | tf_op jit(solution)/shard_map/ppermute | solution.py:267
  89.0 15.8 %collective-permute-start.18 = (bf16[640,512]{1,0:T(8,128)(2,1)S(1)}, bf16[640,512]{1,0:T(8,128)(2,1)S(1)}, u32[]{:S(2)}, u32[]{:S(2)}) collective-permute-start(bf16[640,512]{1,0:T(8,128)(2,1)S(1)} %collective-permute-done.13.refs_3_.refs_1_), channel_id=1, source_target_pairs={{0,1},{1,0},{2,3},{3,2},{4,5},{5,4},{6,7},{7,6},{8,9},{9,8},{10,11... | collective-permute-start | bytes 1966088 | tf_op jit(solution)/shard_map/ppermute | solution.py:267
  90.7 14.6 %collective-permute-start.14 = (bf16[1280,512]{1,0:T(8,128)(2,1)S(1)}, bf16[1280,512]{1,0:T(8,128)(2,1)S(1)}, u32[]{:S(2)}, u32[]{:S(2)}) collective-permute-start(bf16[1280,512]{1,0:T(8,128)(2,1)S(1)} %pack_blocks.3), channel_id=1, source_target_pairs={{0,8},{8,0},{16,24},{24,16},{1,9},{9,1},{17,25},{25,17},{2,10},{10... | collective-permute-start | bytes 3932168 | tf_op jit(solution)/shard_map/ppermute | solution.py:267
  105.3 3.4 %collective-permute-start.19 = (bf16[1280,512]{1,0:T(8,128)(2,1)S(1)}, bf16[1280,512]{1,0:T(8,128)(2,1)S(1)}, u32[]{:S(2)}, u32[]{:S(2)}) collective-permute-start(bf16[1280,512]{1,0:T(8,128)(2,1)S(1)} %pack_blocks.5), channel_id=1, source_target_pairs={{0,8},{8,0},{16,24},{24,16},{1,9},{9,1},{17,25},{25,17},{2,10},{10... | collective-permute-start | bytes 3932168 | tf_op jit(solution)/shard_map/ppermute | solution.py:267
  115.6 3.7 %collective-permute-start.22 = (f32[8,128]{1,0:T(8,128)S(1)}, f32[8,128]{1,0:T(8,128)S(1)}, u32[]{:S(2)}, u32[]{:S(2)}) collective-permute-start(f32[8,128]{1,0:T(8,128)S(1)} %get-tuple-element.74), channel_id=1, source_target_pairs={{0,2},{1,3},{2,0},{3,1},{4,6},{5,7},{6,4},{7,5},{8,10},{9,11},{10,... | collective-permute-start | bytes 12296 | tf_op jit(solution)/shard_map/ppermute | solution.py:267
  117.1 7.6 %collective-permute-start.20 = (bf16[128,640]{1,0:T(8,128)(2,1)S(1)}, bf16[128,640]{1,0:T(8,128)(2,1)S(1)}, u32[]{:S(2)}, u32[]{:S(2)}) collective-permute-start(bf16[128,640]{1,0:T(8,128)(2,1)S(1)} %slice.50), channel_id=1, source_target_pairs={{0,1},{1,0},{2,3},{3,2},{4,5},{5,4},{6,7},{7,6},{8,9},{9,8},{10,11... | collective-permute-start | bytes 491528 | tf_op jit(solution)/shard_map/ppermute | solution.py:267
  119.3 5.4 %collective-permute-start.24 = (f32[8,128]{1,0:T(8,128)S(1)}, f32[8,128]{1,0:T(8,128)S(1)}, u32[]{:S(2)}, u32[]{:S(2)}) collective-permute-start(f32[8,128]{1,0:T(8,128)S(1)} %add.29), channel_id=1, source_target_pairs={{0,4},{1,5},{2,6},{3,7},{4,0},{5,1},{6,2},{7,3},{8,12},{9,13},{10,... | collective-permute-start | bytes 12296 | tf_op jit(solution)/shard_map/ppermute | solution.py:267
  124.1 15.1 %collective-permute-start.23 = (bf16[384,640]{1,0:T(8,128)(2,1)S(1)}, bf16[384,640]{1,0:T(8,128)(2,1)S(1)}, u32[]{:S(2)}, u32[]{:S(2)}) collective-permute-start(bf16[384,640]{1,0:T(8,128)(2,1)S(1)} %slice.54), channel_id=1, source_target_pairs={{0,1},{1,0},{2,3},{3,2},{4,5},{5,4},{6,7},{7,6},{8,9},{9,8},{10,11... | collective-permute-start | bytes 1474568 | tf_op jit(solution)/shard_map/ppermute | solution.py:267
  127.7 9.3 %collective-permute-start.27 = (bf16[128,640]{1,0:T(8,128)(2,1)S(1)}, bf16[128,640]{1,0:T(8,128)(2,1)S(1)}, u32[]{:S(2)}, u32[]{:S(2)}) collective-permute-start(bf16[128,640]{1,0:T(8,128)(2,1)S(1)} %add_convert_fusion.3), channel_id=1, source_target_pairs={{0,4},{1,5},{2,6},{3,7},{4,0},{5,1},{6,2},{7,3},{8,12},{9,13},{10,... | collective-permute-start | bytes 491528 | tf_op jit(solution)/shard_map/ppermute | solution.py:272
  132.5 19.9 %collective-permute-start.21 = (bf16[512,640]{1,0:T(8,128)(2,1)S(1)}, bf16[512,640]{1,0:T(8,128)(2,1)S(1)}, u32[]{:S(2)}, u32[]{:S(2)}) collective-permute-start(bf16[512,640]{1,0:T(8,128)(2,1)S(1)} %get-tuple-element.73), channel_id=1, source_target_pairs={{0,1},{1,0},{2,3},{3,2},{4,5},{5,4},{6,7},{7,6},{8,9},{9,8},{10,11... | collective-permute-start | bytes 1966088 | tf_op jit(solution)/shard_map/ppermute | solution.py:267
  137.1 27.3 %collective-permute-start.29 = (bf16[512,640]{1,0:T(8,128)(2,1)S(1)}, bf16[512,640]{1,0:T(8,128)(2,1)S(1)}, u32[]{:S(2)}, u32[]{:S(2)}) collective-permute-start(bf16[512,640]{1,0:T(8,128)(2,1)S(1)} %get-tuple-element.86), channel_id=1, source_target_pairs={{0,1},{1,0},{2,3},{3,2},{4,5},{5,4},{6,7},{7,6},{8,9},{9,8},{10,11... | collective-permute-start | bytes 1966088 | tf_op jit(solution)/shard_map/ppermute | solution.py:267
  139.3 36.9 %collective-permute-start.25 = (bf16[384,640]{1,0:T(8,128)(2,1)S(1)}, bf16[384,640]{1,0:T(8,128)(2,1)S(1)}, u32[]{:S(2)}, u32[]{:S(2)}) collective-permute-start(bf16[384,640]{1,0:T(8,128)(2,1)S(1)} %add_convert_fusion.2), channel_id=1, source_target_pairs={{0,4},{1,5},{2,6},{3,7},{4,0},{5,1},{6,2},{7,3},{8,12},{9,13},{10,... | collective-permute-start | bytes 1474568 | tf_op jit(solution)/shard_map/ppermute | solution.py:272
  153.3 42.4 %collective-permute-start.28 = (bf16[512,640]{1,0:T(8,128)(2,1)}, bf16[512,640]{1,0:T(8,128)(2,1)S(1)}, u32[]{:S(2)}, u32[]{:S(2)}) collective-permute-start(bf16[512,640]{1,0:T(8,128)(2,1)} %add_convert_fusion.1), channel_id=1, source_target_pairs={{0,2},{1,3},{2,4},{3,5},{4,6},{5,7},{6,0},{7,1},{8,10},{9,11},{10,... | collective-permute-start | bytes 1966088 | tf_op jit(solution)/shard_map/ppermute | solution.py:272
  177.0 18.8 %collective-permute-start.30 = (bf16[512,640]{1,0:T(8,128)(2,1)}, bf16[512,640]{1,0:T(8,128)(2,1)}, u32[]{:S(2)}, u32[]{:S(2)}) collective-permute-start(bf16[512,640]{1,0:T(8,128)(2,1)} %add_convert_fusion), channel_id=1, source_target_pairs={{0,6},{1,7},{2,0},{3,1},{4,2},{5,3},{6,4},{7,5},{8,14},{9,15},{10,... | collective-permute-start | bytes 1966088 | tf_op jit(solution)/shard_map/ppermute | solution.py:272
  177.0 18.8 %collective-permute-start.26 = (bf16[512,640]{1,0:T(8,128)(2,1)}, bf16[512,640]{1,0:T(8,128)(2,1)}, u32[]{:S(2)}, u32[]{:S(2)}) collective-permute-start(bf16[512,640]{1,0:T(8,128)(2,1)} %fusion), channel_id=1, source_target_pairs={{0,1},{1,0},{2,3},{3,2},{4,5},{5,4},{6,7},{7,6},{8,9},{9,8},{10,11... | collective-permute-start | bytes 1966088 | tf_op jit(solution)/shard_map/ppermute | solution.py:267
  178.5 15.5 %collective-permute-start.31 = (f32[8,128]{1,0:T(8,128)S(1)}, f32[8,128]{1,0:T(8,128)S(1)}, u32[]{:S(2)}, u32[]{:S(2)}) collective-permute-start(f32[8,128]{1,0:T(8,128)S(1)} %add.31), channel_id=1, source_target_pairs={{0,1},{1,0},{2,3},{3,2},{4,5},{5,4},{6,7},{7,6},{8,9},{9,8},{10,11... | collective-permute-start | bytes 12296 | tf_op jit(solution)/shard_map/ppermute | solution.py:267
  (3 other events, 14.4 us)

commit v6 on v3

--- a/solution.py
+++ b/solution.py
@@ -159,7 +159,8 @@
         grad_ref[tokens, at : at + head] = grad.astype(jnp.bfloat16)
         gain_sum = gain_sum + jnp.sum(upstream * heads * inverse, axis=0, keepdims=True)
         loss_sum = loss_sum + jnp.sum(differ * differ, axis=0, keepdims=True)
-    stats = jnp.concatenate([gain_sum, loss_sum, jnp.zeros((6, head), jnp.float32)], axis=0)
+    loss_sum = jnp.broadcast_to(jnp.sum(loss_sum, axis=1, keepdims=True), gain_sum.shape)
+    stats = jnp.concatenate([gain_sum, loss_sum], axis=1)
 
     @pl.when(step == 0)
     def _():
@@ -187,7 +188,7 @@
     far_blocks = [pl.BlockSpec((tokens, rows), lambda i, at=at: (0, at)) for at in far]
     outs = [
         jax.ShapeDtypeStruct((tokens, wide), jnp.bfloat16),
-        jax.ShapeDtypeStruct((8, head), jnp.float32),
+        jax.ShapeDtypeStruct((1, 2 * head), jnp.float32),
         jax.ShapeDtypeStruct((wide, rows), jnp.float32),
         jax.ShapeDtypeStruct((wide, rows), jnp.bfloat16),
     ]
@@ -345,8 +346,7 @@
     def grads(keys, dtype, *wait):
         return grad_blocks(after(grad_keys, *wait), student, rows, [order.index(key) for key in keys], dtype)
 
-    sums = jnp.concatenate([stats[0], jnp.full((head,), jnp.sum(stats[1]))])
-    bit, first_step = 2, None
+    sums, bit, first_step = stats[0], 2, None
     while bit < lax.axis_size("fsdp"):
         sums = sums + swap(sums, "fsdp", bit)
         first_step = sums if first_step is None else first_step

time: 199 us -> 196 us (0.985)
  transfers between devices with their start and end apart: 32 -> 32, of which waited for: 15 -> 15; matrix products, arithmetic and copies ran while one was open for 3% -> 3% of each run, Pallas kernels for 22% -> 23%
where the time goes in v6:
time: 196 us; the launch traced here: 195 us
  waiting for transfers between devices  91.5 us (47%)
  Pallas kernels  53.2 us (27%)
  starting transfers between devices  38.3 us (20%)
  between operations  4.67 us (2%)
  local copies, waits for them, and re-layouts  4.32 us (2%)
  other arithmetic  2.53 us (1%)
    ppermute x8, waiting for transfers between devices, fetch(): lax.ppermute(value, 'fsdp', [(i, (i - 2 * step) % size) for i in range(si...  50.2 us
    ppermute x24, waiting for transfers between devices, swap(): lax.ppermute(value, axis, [(i, i ^ bit) for i in range(lax.axis_size(axis...  41.3 us
    ppermute x24, starting transfers between devices, swap(): lax.ppermute(value, axis, [(i, i ^ bit) for i in range(lax.axis_size(axis...  25.9 us
    pallas_call x2, Pallas kernels, normed_input(): pl.pallas_call(functools.partial(norm_kernel, order, rows), grid=(tokens...  19.1 us
    pallas_call x3, Pallas kernels, early_keys(): pl.pallas_call(functools.partial(early_kernel, counts, bool(before)), gri...  15.6 us
    ppermute x8, starting transfers between devices, fetch(): lax.ppermute(value, 'fsdp', [(i, (i - 2 * step) % size) for i in range(si...  12.4 us
    pallas_call x3, Pallas kernels, grad_blocks(): pl.pallas_call(grad_kernel, grid=(count,), in_specs=[pl.BlockSpec((tokens...  8.62 us
    pallas_call x1, Pallas kernels, late_keys(): pl.pallas_call(functools.partial(late_kernel, counts), grid=(tokens // KE...  8.19 us
  transfers between devices with their start and end apart: 32, of which 15 were waited for; matrix products, arithmetic and copies ran while one was open for 3% of the time, Pallas kernels for 23%

profile of v6, /device:TPU:0, one launch (start us, length us, event | category | flops | bytes accessed | tf_op | source)
XLA Modules:
  0.0 194.6 jit_solution(10141334137170693493)
XLA Ops:
  0.6 3.0 %collective-permute-start.2 = (bf16[640,512]{1,0:T(8,128)(2,1)}, bf16[640,512]{1,0:T(8,128)(2,1)S(1)}, u32[]{:S(2)}, u32[]{:S(2)}) collective-permute-start(bf16[640,512]{1,0:T(8,128)(2,1)} %bitcast.39), channel_id=1, source_target_pairs={{0,1},{1,0},{2,3},{3,2},{4,5},{5,4},{6,7},{7,6},{8,9},{9,8},{10,11... | collective-permute-start | bytes 1966088 | tf_op jit(solution)/shard_map/ppermute | solution.py:247
  3.7 3.6 %collective-permute-start.4 = (bf16[640,512]{1,0:T(8,128)(2,1)}, bf16[640,512]{1,0:T(8,128)(2,1)S(1)}, u32[]{:S(2)}, u32[]{:S(2)}) collective-permute-start(bf16[640,512]{1,0:T(8,128)(2,1)} %bitcast.40), channel_id=1, source_target_pairs={{0,6},{1,7},{2,0},{3,1},{4,2},{5,3},{6,4},{7,5},{8,14},{9,15},{10,... | collective-permute-start | bytes 1966088 | tf_op jit(solution)/shard_map/ppermute | solution.py:252
  7.3 1.5 collective-permute-start.1
  8.8 9.8 %collective-permute-done.2.refs_1_ = bf16[640,512]{1,0:T(8,128)(2,1)S(1)} collective-permute-done((bf16[640,512]{1,0:T(8,128)(2,1)}, bf16[640,512]{1,0:T(8,128)(2,1)S(1)}, u32[]{:S(2)}, u32[]{:S(2)}) %collective-permute-start.2) | collective-permute-done | bytes 655392 | tf_op jit(solution)/shard_map/ppermute | solution.py:247
  18.6 1.7 collective-permute-start.3
  25.5 9.6 %norm_input.2.normed_ref.student_ref.refs_5_.refs_6_ = bf16[768,5120]{1,0:T(8,128)(2,1)} custom-call(s32[1]{0:T(128)} %bitcast.place_ref, bf16[768,5120]{1,0:T(8,128)(2,1)} %bitcast.48, f32[1,5120]{1,0:T(1,128)S(1)} %get-tuple-element.103.gain_ref), custom_call_target="tpu_custom_call" | custom-call | flops 1 | bytes 1 | tf_op jit(solution)/shard_map/norm_input/pallas_call | solution.py:33
  35.1 2.8 %collective-permute-done = bf16[1,5248]{1,0:T(2,128)(2,1)S(1)} collective-permute-done((bf16[1,5248]{1,0:T(2,128)(2,1)S(1)}, bf16[1,5248]{1,0:T(2,128)(2,1)S(1)}, u32[]{:S(2)}, u32[]{:S(2)}) %collective-permute-start) | collective-permute-done | bytes 10528 | tf_op jit(solution)/shard_map/ppermute | solution.py:247
  42.4 9.5 %norm_input.3.normed_ref.teacher_ref = bf16[768,5120]{1,0:T(8,128)(2,1)} custom-call(s32[1]{0:T(128)} %bitcast.place_ref, bf16[768,5120]{1,0:T(8,128)(2,1)} %bitcast.49, f32[1,5120]{1,0:T(1,128)S(1)} %slice.67.gain_ref), custom_call_target="tpu_custom_call" | custom-call | flops 1 | bytes 1 | tf_op jit(solution)/shard_map/norm_input/pallas_call | solution.py:33
  52.0 17.5 %collective-permute-done.6.refs_5_.refs_1_ = bf16[640,512]{1,0:T(8,128)(2,1)S(1)} collective-permute-done((bf16[640,512]{1,0:T(8,128)(2,1)S(1)}, bf16[640,512]{1,0:T(8,128)(2,1)S(1)}, u32[]{:S(2)}, u32[]{:S(2)}) %collective-permute-start.6) | collective-permute-done | bytes 655392 | tf_op jit(solution)/shard_map/ppermute | solution.py:252
  73.3 1.9 collective-permute-start.16
  75.1 1.5 collective-permute-start.17
  76.6 6.7 %early_keys.3.part_s_ref = f32[768,512]{1,0:T(8,128)S(1)} custom-call(s32[1]{0:T(128)} %bitcast.2.choice_ref, bf16[768,5120]{1,0:T(8,128)(2,1)} %norm_input.2.normed_ref.student_ref.refs_5_.refs_6_, bf16[640,512]{1,0:T(8,128)(2,1)S(1)} %bitcast.45, bf16[640,512]{1,0:T(8,128)(2,1)S(1)} %collective-permute-done.2.refs_1_, ...), custom_call_target="tpu_custom_call" | custom-call | flops 1 | bytes 1 | tf_op jit(solution)/shard_map/early_keys/pallas_call | solution.py:117
  83.4 5.6 %collective-permute-done.13.refs_3_.refs_1_ = bf16[640,512]{1,0:T(8,128)(2,1)S(1)} collective-permute-done((bf16[640,512]{1,0:T(8,128)(2,1)S(1)}, bf16[640,512]{1,0:T(8,128)(2,1)S(1)}, u32[]{:S(2)}, u32[]{:S(2)}) %collective-permute-start.13) | collective-permute-done | bytes 655392 | tf_op jit(solution)/shard_map/ppermute | solution.py:247
  90.8 5.2 %early_keys.4.refs_3_ = f32[768,512]{1,0:T(8,128)S(1)} custom-call(s32[1]{0:T(128)} %bitcast.2.choice_ref, bf16[768,5120]{1,0:T(8,128)(2,1)} %norm_input.3.normed_ref.teacher_ref, bf16[640,512]{1,0:T(8,128)(2,1)S(1)} %collective-permute-done.1.refs_4_.refs_0_, bf16[640,512]{1,0:T(8,128)(2,1)S(1)} %collective-permute-done.3.refs_5_.refs_1_, ...), custom_call_target="tpu_custom_call" | custom-call | flops 1 | bytes 1 | tf_op jit(solution)/shard_map/early_keys/pallas_call | solution.py:117
  96.0 8.7 %collective-permute-done.16.refs_1_ = bf16[640,512]{1,0:T(8,128)(2,1)S(1)} collective-permute-done((bf16[640,512]{1,0:T(8,128)(2,1)S(1)}, bf16[640,512]{1,0:T(8,128)(2,1)S(1)}, u32[]{:S(2)}, u32[]{:S(2)}) %collective-permute-start.16) | collective-permute-done | bytes 655392 | tf_op jit(solution)/shard_map/ppermute | solution.py:252
  105.4 3.7 %early_keys.5.part_t_ref = f32[768,512]{1,0:T(8,128)S(1)} custom-call(s32[1]{0:T(128)} %bitcast.2.choice_ref, bf16[768,5120]{1,0:T(8,128)(2,1)} %norm_input.3.normed_ref.teacher_ref, bf16[640,512]{1,0:T(8,128)(2,1)S(1)} %collective-permute-done.12.refs_2_.refs_0_, bf16[640,512]{1,0:T(8,128)(2,1)S(1)} %collective-permute-done.13.refs_3_.refs_1_, ...), custom_call_target="tpu_custom_call" | custom-call | flops 1 | bytes 1 | tf_op jit(solution)/shard_map/early_keys/pallas_call | solution.py:117
  109.0 8.2 %late_keys.1 = (bf16[768,512]{1,0:T(8,128)(2,1)S(1)}, f32[1,256]{1,0:T(1,128)S(1)}, f32[512,640]{1,0:T(8,128)S(1)}, bf16[512,640]{1,0:T(8,128)(2,1)S(1)}) custom-call(s32[1]{0:T(128)} %bitcast.2.choice_ref, bf16[768,5120]{1,0:T(8,128)(2,1)} %norm_input.2.normed_ref.student_ref.refs_5_.refs_6_, bf16[768,5120]{1,0:T(8,128)(2,1)} %norm_input.3.normed_ref.teacher_ref, ...), custom_call_target="tpu_custom_call" | custom-call | flops 1 | bytes 1 | tf_op jit(solution)/shard_map/late_keys/pallas_call | solution.py:196
  118.7 1.6 collective-permute-start.22
  120.2 2.0 %collective-permute-done.22 = f32[256]{0:T(256)S(1)} collective-permute-done((f32[256]{0:T(256)S(1)}, f32[256]{0:T(256)S(1)}, u32[]{:S(2)}, u32[]{:S(2)}) %collective-permute-start.22) | collective-permute-done | bytes 1056 | tf_op jit(solution)/shard_map/ppermute | solution.py:247
  122.2 1.9 collective-permute-start.24
  124.2 1.6 collective-permute-start.23
  127.9 2.7 %collective-permute-start.27 = (bf16[256,640]{1,0:T(8,128)(2,1)S(1)}, bf16[256,640]{1,0:T(8,128)(2,1)S(1)}, u32[]{:S(2)}, u32[]{:S(2)}) collective-permute-start(bf16[256,640]{1,0:T(8,128)(2,1)S(1)} %add_convert_fusion.2), channel_id=1, source_target_pairs={{0,4},{1,5},{2,6},{3,7},{4,0},{5,1},{6,2},{7,3},{8,12},{9,13},{10,... | collective-permute-start | bytes 983048 | tf_op jit(solution)/shard_map/ppermute | solution.py:252
  130.7 2.9 %grad_blocks.3 = bf16[2,512,640]{2,1,0:T(8,128)(2,1)S(1)} custom-call(bf16[768,512]{1,0:T(8,128)(2,1)S(1)} %get-tuple-element.72.grad_ref, bf16[768,5120]{1,0:T(8,128)(2,1)} %norm_input.2.normed_ref.student_ref.refs_5_.refs_6_), custom_call_target="tpu_custom_call" | custom-call | flops 1 | bytes 1 | tf_op jit(solution)/shard_map/grad_blocks/pallas_call | solution.py:231
  134.2 2.9 %grad_blocks.4 = f32[2,512,640]{2,1,0:T(8,128)S(1)} custom-call(bf16[768,512]{1,0:T(8,128)(2,1)S(1)} %get-tuple-element.72.grad_ref, bf16[768,5120]{1,0:T(8,128)(2,1)} %norm_input.2.normed_ref.student_ref.refs_5_.refs_6_), custom_call_target="tpu_custom_call" | custom-call | flops 1 | bytes 1 | tf_op jit(solution)/shard_map/grad_blocks/pallas_call | solution.py:231
  137.1 2.9 %grad_blocks.5 = f32[2,512,640]{2,1,0:T(8,128)S(1)} custom-call(bf16[768,512]{1,0:T(8,128)(2,1)S(1)} %get-tuple-element.72.grad_ref, bf16[768,5120]{1,0:T(8,128)(2,1)} %norm_input.2.normed_ref.student_ref.refs_5_.refs_6_), custom_call_target="tpu_custom_call" | custom-call | flops 1 | bytes 1 | tf_op jit(solution)/shard_map/grad_blocks/pallas_call | solution.py:231
  141.2 11.6 %collective-permute-done.27 = bf16[256,640]{1,0:T(8,128)(2,1)S(1)} collective-permute-done((bf16[256,640]{1,0:T(8,128)(2,1)S(1)}, bf16[256,640]{1,0:T(8,128)(2,1)S(1)}, u32[]{:S(2)}, u32[]{:S(2)}) %collective-permute-start.27) | collective-permute-done | bytes 327712 | tf_op jit(solution)/shard_map/ppermute | solution.py:252
  152.8 1.5 collective-permute-start.29
  154.5 4.3 %collective-permute-done.25 = bf16[256,640]{1,0:T(8,128)(2,1)S(1)} collective-permute-done((bf16[256,640]{1,0:T(8,128)(2,1)S(1)}, bf16[256,640]{1,0:T(8,128)(2,1)S(1)}, u32[]{:S(2)}, u32[]{:S(2)}) %collective-permute-start.25) | collective-permute-done | bytes 327712 | tf_op jit(solution)/shard_map/ppermute | solution.py:252
  160.4 10.1 %collective-permute-done.29 = bf16[512,640]{1,0:T(8,128)(2,1)S(1)} collective-permute-done((bf16[512,640]{1,0:T(8,128)(2,1)S(1)}, bf16[512,640]{1,0:T(8,128)(2,1)S(1)}, u32[]{:S(2)}, u32[]{:S(2)}) %collective-permute-start.29) | collective-permute-done | bytes 655392 | tf_op jit(solution)/shard_map/ppermute | solution.py:247
  170.6 2.8 %collective-permute-start.30 = (bf16[512,640]{1,0:T(8,128)(2,1)S(1)}, bf16[512,640]{1,0:T(8,128)(2,1)S(1)}, u32[]{:S(2)}, u32[]{:S(2)}) collective-permute-start(bf16[512,640]{1,0:T(8,128)(2,1)S(1)} %add_convert_fusion), channel_id=1, source_target_pairs={{0,6},{1,7},{2,0},{3,1},{4,2},{5,3},{6,4},{7,5},{8,14},{9,15},{10,... | collective-permute-start | bytes 1966088 | tf_op jit(solution)/shard_map/ppermute | solution.py:252
  173.9 7.8 %collective-permute-done.31 = f32[256]{0:T(256)S(1)} collective-permute-done((f32[256]{0:T(256)S(1)}, f32[256]{0:T(256)S(1)}, u32[]{:S(2)}, u32[]{:S(2)}) %collective-permute-start.31) | collective-permute-done | bytes 1056 | tf_op jit(solution)/shard_map/ppermute | solution.py:247
  183.4 8.1 %collective-permute-done.30 = bf16[512,640]{1,0:T(8,128)(2,1)S(1)} collective-permute-done((bf16[512,640]{1,0:T(8,128)(2,1)S(1)}, bf16[512,640]{1,0:T(8,128)(2,1)S(1)}, u32[]{:S(2)}, u32[]{:S(2)}) %collective-permute-start.30) | collective-permute-done | bytes 655392 | tf_op jit(solution)/shard_map/ppermute | solution.py:252
  (69 shorter events, 24.8 us)
Async XLA Ops:
  0.6 18.0 %collective-permute-start.2 = (bf16[640,512]{1,0:T(8,128)(2,1)}, bf16[640,512]{1,0:T(8,128)(2,1)S(1)}, u32[]{:S(2)}, u32[]{:S(2)}) collective-permute-start(bf16[640,512]{1,0:T(8,128)(2,1)} %bitcast.39), channel_id=1, source_target_pairs={{0,1},{1,0},{2,3},{3,2},{4,5},{5,4},{6,7},{7,6},{8,9},{9,8},{10,11... | collective-permute-start | bytes 1966088 | tf_op jit(solution)/shard_map/ppermute | solution.py:247
  3.7 34.2 %collective-permute-start.4 = (bf16[640,512]{1,0:T(8,128)(2,1)}, bf16[640,512]{1,0:T(8,128)(2,1)S(1)}, u32[]{:S(2)}, u32[]{:S(2)}) collective-permute-start(bf16[640,512]{1,0:T(8,128)(2,1)} %bitcast.40), channel_id=1, source_target_pairs={{0,6},{1,7},{2,0},{3,1},{4,2},{5,3},{6,4},{7,5},{8,14},{9,15},{10,... | collective-permute-start | bytes 1966088 | tf_op jit(solution)/shard_map/ppermute | solution.py:252
  7.3 30.6 %collective-permute-start.1 = (bf16[640,512]{1,0:T(8,128)(2,1)}, bf16[640,512]{1,0:T(8,128)(2,1)S(1)}, u32[]{:S(2)}, u32[]{:S(2)}) collective-permute-start(bf16[640,512]{1,0:T(8,128)(2,1)} %bitcast.41), channel_id=1, source_target_pairs={{0,16},{8,24},{16,0},{24,8},{1,17},{9,25},{17,1},{25,9},{2,18},{10... | collective-permute-start | bytes 1966088 | tf_op jit(solution)/shard_map/ppermute | solution.py:247
  8.8 29.1 %collective-permute-start.5 = (bf16[640,512]{1,0:T(8,128)(2,1)}, bf16[640,512]{1,0:T(8,128)(2,1)S(1)}, u32[]{:S(2)}, u32[]{:S(2)}) collective-permute-start(bf16[640,512]{1,0:T(8,128)(2,1)} %bitcast.42), channel_id=1, source_target_pairs={{0,2},{1,3},{2,4},{3,5},{4,6},{5,7},{6,0},{7,1},{8,10},{9,11},{10,... | collective-permute-start | bytes 1966088 | tf_op jit(solution)/shard_map/ppermute | solution.py:252
  18.6 19.3 %collective-permute-start.3 = (bf16[640,512]{1,0:T(8,128)(2,1)S(1)}, bf16[640,512]{1,0:T(8,128)(2,1)S(1)}, u32[]{:S(2)}, u32[]{:S(2)}) collective-permute-start(bf16[640,512]{1,0:T(8,128)(2,1)S(1)} %collective-permute-done.2.refs_1_), channel_id=1, source_target_pairs={{0,16},{8,24},{16,0},{24,8},{1,17},{9,25},{17,1},{25,9},{2,18},{10... | collective-permute-start | bytes 1966088 | tf_op jit(solution)/shard_map/ppermute | solution.py:247
  21.9 16.0 %collective-permute-start = (bf16[1,5248]{1,0:T(2,128)(2,1)S(1)}, bf16[1,5248]{1,0:T(2,128)(2,1)S(1)}, u32[]{:S(2)}, u32[]{:S(2)}) collective-permute-start(bf16[1,5248]{1,0:T(2,128)(2,1)S(1)} %get-tuple-element.105), channel_id=1, source_target_pairs={{0,16},{8,24},{16,0},{24,8},{1,17},{9,25},{17,1},{25,9},{2,18},{10... | collective-permute-start | bytes 31496 | tf_op jit(solution)/shard_map/ppermute | solution.py:247
  38.0 3.8 %collective-permute-start.7 = (bf16[2,5248]{1,0:T(2,128)(2,1)S(1)}, bf16[2,5248]{1,0:T(2,128)(2,1)S(1)}, u32[]{:S(2)}, u32[]{:S(2)}) collective-permute-start(bf16[2,5248]{1,0:T(2,128)(2,1)S(1)} %pad_maximum_fusion), channel_id=1, source_target_pairs={{0,8},{8,0},{16,24},{24,16},{1,9},{9,1},{17,25},{25,17},{2,10},{10... | collective-permute-start | bytes 62984 | tf_op jit(solution)/shard_map/ppermute | solution.py:247
  38.1 31.4 %collective-permute-start.6 = (bf16[640,512]{1,0:T(8,128)(2,1)S(1)}, bf16[640,512]{1,0:T(8,128)(2,1)S(1)}, u32[]{:S(2)}, u32[]{:S(2)}) collective-permute-start(bf16[640,512]{1,0:T(8,128)(2,1)S(1)} %bitcast.43), channel_id=1, source_target_pairs={{0,4},{1,5},{2,6},{3,7},{4,0},{5,1},{6,2},{7,3},{8,12},{9,13},{10,... | collective-permute-start | bytes 1966088 | tf_op jit(solution)/shard_map/ppermute | solution.py:252
  38.3 31.1 %collective-permute-start.10 = (bf16[640,512]{1,0:T(8,128)(2,1)S(1)}, bf16[640,512]{1,0:T(8,128)(2,1)S(1)}, u32[]{:S(2)}, u32[]{:S(2)}) collective-permute-start(bf16[640,512]{1,0:T(8,128)(2,1)S(1)} %collective-permute-done.4.refs_2_), channel_id=1, source_target_pairs={{0,16},{8,24},{16,0},{24,8},{1,17},{9,25},{17,1},{25,9},{2,18},{10... | collective-permute-start | bytes 1966088 | tf_op jit(solution)/shard_map/ppermute | solution.py:247
  39.7 29.7 %collective-permute-start.8 = (bf16[640,512]{1,0:T(8,128)(2,1)S(1)}, bf16[640,512]{1,0:T(8,128)(2,1)S(1)}, u32[]{:S(2)}, u32[]{:S(2)}) collective-permute-start(bf16[640,512]{1,0:T(8,128)(2,1)S(1)} %collective-permute-done.4.refs_2_), channel_id=1, source_target_pairs={{0,1},{1,0},{2,3},{3,2},{4,5},{5,4},{6,7},{7,6},{8,9},{9,8},{10,11... | collective-permute-start | bytes 1966088 | tf_op jit(solution)/shard_map/ppermute | solution.py:247
  41.2 28.2 %collective-permute-start.11 = (bf16[640,512]{1,0:T(8,128)(2,1)S(1)}, bf16[640,512]{1,0:T(8,128)(2,1)S(1)}, u32[]{:S(2)}, u32[]{:S(2)}) collective-permute-start(bf16[640,512]{1,0:T(8,128)(2,1)S(1)} %collective-permute-done.5.refs_3_), channel_id=1, source_target_pairs={{0,16},{8,24},{16,0},{24,8},{1,17},{9,25},{17,1},{25,9},{2,18},{10... | collective-permute-start | bytes 1966088 | tf_op jit(solution)/shard_map/ppermute | solution.py:247
  41.7 28.7 %collective-permute-start.9 = (bf16[640,512]{1,0:T(8,128)(2,1)S(1)}, bf16[640,512]{1,0:T(8,128)(2,1)S(1)}, u32[]{:S(2)}, u32[]{:S(2)}) collective-permute-start(bf16[640,512]{1,0:T(8,128)(2,1)S(1)} %collective-permute-done.5.refs_3_), channel_id=1, source_target_pairs={{0,1},{1,0},{2,3},{3,2},{4,5},{5,4},{6,7},{7,6},{8,9},{9,8},{10,11... | collective-permute-start | bytes 1966088 | tf_op jit(solution)/shard_map/ppermute | solution.py:247
  71.3 19.5 %collective-permute-start.15 = (bf16[2560,512]{1,0:T(8,128)(2,1)S(1)}, bf16[2560,512]{1,0:T(8,128)(2,1)S(1)}, u32[]{:S(2)}, u32[]{:S(2)}) collective-permute-start(bf16[2560,512]{1,0:T(8,128)(2,1)S(1)} %pack_blocks.4), channel_id=1, source_target_pairs={{0,8},{8,0},{16,24},{24,16},{1,9},{9,1},{17,25},{25,17},{2,10},{10... | collective-permute-start | bytes 7864328 | tf_op jit(solution)/shard_map/ppermute | solution.py:247
  71.4 17.6 %collective-permute-start.13 = (bf16[640,512]{1,0:T(8,128)(2,1)S(1)}, bf16[640,512]{1,0:T(8,128)(2,1)S(1)}, u32[]{:S(2)}, u32[]{:S(2)}) collective-permute-start(bf16[640,512]{1,0:T(8,128)(2,1)S(1)} %collective-permute-done.6.refs_5_.refs_1_), channel_id=1, source_target_pairs={{0,16},{8,24},{16,0},{24,8},{1,17},{9,25},{17,1},{25,9},{2,18},{10... | collective-permute-start | bytes 1966088 | tf_op jit(solution)/shard_map/ppermute | solution.py:247
  72.0 18.3 %collective-permute-start.12 = (bf16[640,512]{1,0:T(8,128)(2,1)S(1)}, bf16[640,512]{1,0:T(8,128)(2,1)S(1)}, u32[]{:S(2)}, u32[]{:S(2)}) collective-permute-start(bf16[640,512]{1,0:T(8,128)(2,1)S(1)} %collective-permute-done.10.refs_6_.refs_2_), channel_id=1, source_target_pairs={{0,1},{1,0},{2,3},{3,2},{4,5},{5,4},{6,7},{7,6},{8,9},{9,8},{10,11... | collective-permute-start | bytes 1966088 | tf_op jit(solution)/shard_map/ppermute | solution.py:247
  73.3 31.5 %collective-permute-start.16 = (bf16[640,512]{1,0:T(8,128)(2,1)S(1)}, bf16[640,512]{1,0:T(8,128)(2,1)S(1)}, u32[]{:S(2)}, u32[]{:S(2)}) collective-permute-start(bf16[640,512]{1,0:T(8,128)(2,1)S(1)} %collective-permute-done.2.refs_1_), channel_id=1, source_target_pairs={{0,4},{1,5},{2,6},{3,7},{4,0},{5,1},{6,2},{7,3},{8,12},{9,13},{10,... | collective-permute-start | bytes 1966088 | tf_op jit(solution)/shard_map/ppermute | solution.py:252
  75.1 29.6 %collective-permute-start.17 = (bf16[640,512]{1,0:T(8,128)(2,1)S(1)}, bf16[640,512]{1,0:T(8,128)(2,1)S(1)}, u32[]{:S(2)}, u32[]{:S(2)}) collective-permute-start(bf16[640,512]{1,0:T(8,128)(2,1)S(1)} %collective-permute-done.9.refs_0_), channel_id=1, source_target_pairs={{0,16},{8,24},{16,0},{24,8},{1,17},{9,25},{17,1},{25,9},{2,18},{10... | collective-permute-start | bytes 1966088 | tf_op jit(solution)/shard_map/ppermute | solution.py:247
  89.0 15.8 %collective-permute-start.18 = (bf16[640,512]{1,0:T(8,128)(2,1)S(1)}, bf16[640,512]{1,0:T(8,128)(2,1)S(1)}, u32[]{:S(2)}, u32[]{:S(2)}) collective-permute-start(bf16[640,512]{1,0:T(8,128)(2,1)S(1)} %collective-permute-done.13.refs_3_.refs_1_), channel_id=1, source_target_pairs={{0,1},{1,0},{2,3},{3,2},{4,5},{5,4},{6,7},{7,6},{8,9},{9,8},{10,11... | collective-permute-start | bytes 1966088 | tf_op jit(solution)/shard_map/ppermute | solution.py:247
  90.7 14.6 %collective-permute-start.14 = (bf16[1280,512]{1,0:T(8,128)(2,1)S(1)}, bf16[1280,512]{1,0:T(8,128)(2,1)S(1)}, u32[]{:S(2)}, u32[]{:S(2)}) collective-permute-start(bf16[1280,512]{1,0:T(8,128)(2,1)S(1)} %pack_blocks.3), channel_id=1, source_target_pairs={{0,8},{8,0},{16,24},{24,16},{1,9},{9,1},{17,25},{25,17},{2,10},{10... | collective-permute-start | bytes 3932168 | tf_op jit(solution)/shard_map/ppermute | solution.py:247
  105.3 3.8 %collective-permute-start.19 = (bf16[1280,512]{1,0:T(8,128)(2,1)S(1)}, bf16[1280,512]{1,0:T(8,128)(2,1)S(1)}, u32[]{:S(2)}, u32[]{:S(2)}) collective-permute-start(bf16[1280,512]{1,0:T(8,128)(2,1)S(1)} %pack_blocks.5), channel_id=1, source_target_pairs={{0,8},{8,0},{16,24},{24,16},{1,9},{9,1},{17,25},{25,17},{2,10},{10... | collective-permute-start | bytes 3932168 | tf_op jit(solution)/shard_map/ppermute | solution.py:247
  117.3 10.6 %collective-permute-start.20 = (bf16[256,640]{1,0:T(8,128)(2,1)S(1)}, bf16[256,640]{1,0:T(8,128)(2,1)S(1)}, u32[]{:S(2)}, u32[]{:S(2)}) collective-permute-start(bf16[256,640]{1,0:T(8,128)(2,1)S(1)} %get-tuple-element.101), channel_id=1, source_target_pairs={{0,1},{1,0},{2,3},{3,2},{4,5},{5,4},{6,7},{7,6},{8,9},{9,8},{10,11... | collective-permute-start | bytes 983048 | tf_op jit(solution)/shard_map/ppermute | solution.py:247
  118.7 3.6 %collective-permute-start.22 = (f32[256]{0:T(256)S(1)}, f32[256]{0:T(256)S(1)}, u32[]{:S(2)}, u32[]{:S(2)}) collective-permute-start(f32[256]{0:T(256)S(1)} %bitcast.46), channel_id=1, source_target_pairs={{0,2},{1,3},{2,0},{3,1},{4,6},{5,7},{6,4},{7,5},{8,10},{9,11},{10,... | collective-permute-start | bytes 3080 | tf_op jit(solution)/shard_map/ppermute | solution.py:247
  122.2 4.5 %collective-permute-start.24 = (f32[256]{0:T(256)S(1)}, f32[256]{0:T(256)S(1)}, u32[]{:S(2)}, u32[]{:S(2)}) collective-permute-start(f32[256]{0:T(256)S(1)} %add.41), channel_id=1, source_target_pairs={{0,4},{1,5},{2,6},{3,7},{4,0},{5,1},{6,2},{7,3},{8,12},{9,13},{10,... | collective-permute-start | bytes 3080 | tf_op jit(solution)/shard_map/ppermute | solution.py:247
  124.2 15.8 %collective-permute-start.23 = (bf16[256,640]{1,0:T(8,128)(2,1)S(1)}, bf16[256,640]{1,0:T(8,128)(2,1)S(1)}, u32[]{:S(2)}, u32[]{:S(2)}) collective-permute-start(bf16[256,640]{1,0:T(8,128)(2,1)S(1)} %get-tuple-element.76), channel_id=1, source_target_pairs={{0,1},{1,0},{2,3},{3,2},{4,5},{5,4},{6,7},{7,6},{8,9},{9,8},{10,11... | collective-permute-start | bytes 983048 | tf_op jit(solution)/shard_map/ppermute | solution.py:247
  127.9 24.8 %collective-permute-start.27 = (bf16[256,640]{1,0:T(8,128)(2,1)S(1)}, bf16[256,640]{1,0:T(8,128)(2,1)S(1)}, u32[]{:S(2)}, u32[]{:S(2)}) collective-permute-start(bf16[256,640]{1,0:T(8,128)(2,1)S(1)} %add_convert_fusion.2), channel_id=1, source_target_pairs={{0,4},{1,5},{2,6},{3,7},{4,0},{5,1},{6,2},{7,3},{8,12},{9,13},{10,... | collective-permute-start | bytes 983048 | tf_op jit(solution)/shard_map/ppermute | solution.py:252
  133.7 25.2 %collective-permute-start.21 = (bf16[512,640]{1,0:T(8,128)(2,1)S(1)}, bf16[512,640]{1,0:T(8,128)(2,1)S(1)}, u32[]{:S(2)}, u32[]{:S(2)}) collective-permute-start(bf16[512,640]{1,0:T(8,128)(2,1)S(1)} %get-tuple-element.73), channel_id=1, source_target_pairs={{0,1},{1,0},{2,3},{3,2},{4,5},{5,4},{6,7},{7,6},{8,9},{9,8},{10,11... | collective-permute-start | bytes 1966088 | tf_op jit(solution)/shard_map/ppermute | solution.py:247
  140.1 18.8 %collective-permute-start.25 = (bf16[256,640]{1,0:T(8,128)(2,1)S(1)}, bf16[256,640]{1,0:T(8,128)(2,1)S(1)}, u32[]{:S(2)}, u32[]{:S(2)}) collective-permute-start(bf16[256,640]{1,0:T(8,128)(2,1)S(1)} %add_convert_fusion.3), channel_id=1, source_target_pairs={{0,4},{1,5},{2,6},{3,7},{4,0},{5,1},{6,2},{7,3},{8,12},{9,13},{10,... | collective-permute-start | bytes 983048 | tf_op jit(solution)/shard_map/ppermute | solution.py:252
  152.8 17.7 %collective-permute-start.29 = (bf16[512,640]{1,0:T(8,128)(2,1)S(1)}, bf16[512,640]{1,0:T(8,128)(2,1)S(1)}, u32[]{:S(2)}, u32[]{:S(2)}) collective-permute-start(bf16[512,640]{1,0:T(8,128)(2,1)S(1)} %get-tuple-element.86), channel_id=1, source_target_pairs={{0,1},{1,0},{2,3},{3,2},{4,5},{5,4},{6,7},{7,6},{8,9},{9,8},{10,11... | collective-permute-start | bytes 1966088 | tf_op jit(solution)/shard_map/ppermute | solution.py:247
  158.9 24.6 %collective-permute-start.26 = (bf16[512,640]{1,0:T(8,128)(2,1)S(1)}, bf16[512,640]{1,0:T(8,128)(2,1)S(1)}, u32[]{:S(2)}, u32[]{:S(2)}) collective-permute-start(bf16[512,640]{1,0:T(8,128)(2,1)S(1)} %fusion.5), channel_id=1, source_target_pairs={{0,1},{1,0},{2,3},{3,2},{4,5},{5,4},{6,7},{7,6},{8,9},{9,8},{10,11... | collective-permute-start | bytes 1966088 | tf_op jit(solution)/shard_map/ppermute | solution.py:247
  160.3 23.1 %collective-permute-start.28 = (bf16[512,640]{1,0:T(8,128)(2,1)S(1)}, bf16[512,640]{1,0:T(8,128)(2,1)S(1)}, u32[]{:S(2)}, u32[]{:S(2)}) collective-permute-start(bf16[512,640]{1,0:T(8,128)(2,1)S(1)} %add_convert_fusion.1), channel_id=1, source_target_pairs={{0,2},{1,3},{2,4},{3,5},{4,6},{5,7},{6,0},{7,1},{8,10},{9,11},{10,... | collective-permute-start | bytes 1966088 | tf_op jit(solution)/shard_map/ppermute | solution.py:252
  170.6 21.0 %collective-permute-start.30 = (bf16[512,640]{1,0:T(8,128)(2,1)S(1)}, bf16[512,640]{1,0:T(8,128)(2,1)S(1)}, u32[]{:S(2)}, u32[]{:S(2)}) collective-permute-start(bf16[512,640]{1,0:T(8,128)(2,1)S(1)} %add_convert_fusion), channel_id=1, source_target_pairs={{0,6},{1,7},{2,0},{3,1},{4,2},{5,3},{6,4},{7,5},{8,14},{9,15},{10,... | collective-permute-start | bytes 1966088 | tf_op jit(solution)/shard_map/ppermute | solution.py:252
  173.4 8.3 %collective-permute-start.31 = (f32[256]{0:T(256)S(1)}, f32[256]{0:T(256)S(1)}, u32[]{:S(2)}, u32[]{:S(2)}) collective-permute-start(f32[256]{0:T(256)S(1)} %add.43), channel_id=1, source_target_pairs={{0,1},{1,0},{2,3},{3,2},{4,5},{5,4},{6,7},{7,6},{8,9},{9,8},{10,11... | collective-permute-start | bytes 3080 | tf_op jit(solution)/shard_map/ppermute | solution.py:247
  (1 other events, 12.6 us)

commit v7 on v6

--- a/solution.py
+++ b/solution.py
@@ -10,6 +10,7 @@
 EPS = 1e-06
 NORM_TOKENS = 128
 KEY_TOKENS = 256
+LATE_TOKENS = 384
 VMEM_LIMIT = 24 * 1024 * 1024
 SHORT = pl.CostEstimate(flops=1, bytes_accessed=1, transcendentals=0)
 ANY = pl.BlockSpec(memory_space=pl.ANY)
@@ -146,7 +147,7 @@
     keys_t = part_t_ref[...] + jnp.dot(teacher_ref[...], w_t[...], preferred_element_type=jnp.float32)
     gain_s, gain_t = gain_s_ref[...], gain_t_ref[...]
     gain_sum, loss_sum = 0.0, 0.0
-    tokens = pl.ds(pl.multiple_of(step * keys_s.shape[0], 256), keys_s.shape[0])
+    tokens = pl.ds(pl.multiple_of(step * keys_s.shape[0], 128), keys_s.shape[0])
     for at in range(0, features, head):
         heads, taught = keys_s[:, at : at + head], keys_t[:, at : at + head]
         inverse = lax.rsqrt(jnp.mean(heads * heads, axis=-1, keepdims=True) + EPS)
@@ -182,8 +183,8 @@
     counts, (tokens, wide), head = [len(same)] + [len(blocks) for blocks in choices], part_s.shape, gain_s.shape[1]
     depth = sum(block.shape[0] for block in same)
     last = student.shape[1] // depth - 1
-    token_block = pl.BlockSpec((KEY_TOKENS, depth), lambda i: (i, last))
-    keys = pl.BlockSpec((KEY_TOKENS, wide), lambda i: (i, 0))
+    token_block = pl.BlockSpec((LATE_TOKENS, depth), lambda i: (i, last))
+    keys = pl.BlockSpec((LATE_TOKENS, wide), lambda i: (i, 0))
     gain = pl.BlockSpec((1, head), lambda i: (0, 0))
     far_blocks = [pl.BlockSpec((tokens, rows), lambda i, at=at: (0, at)) for at in far]
     outs = [
@@ -195,7 +196,7 @@
     student, teacher = in_hbm(student), in_hbm(teacher)
     return pl.pallas_call(
         functools.partial(late_kernel, counts),
-        grid=(tokens // KEY_TOKENS,),
+        grid=(tokens // LATE_TOKENS,),
         in_specs=[SMEM, token_block, token_block, keys, keys, gain, gain] + [ANY] * sum(counts) + far_blocks,
         out_specs=[pl.BlockSpec(out.shape, lambda i: (0, 0)) for out in outs],
         out_shape=outs,
@@ -280,11 +281,11 @@
     for step in near:
         same[step, 0] = fetch(own, step)
     same[0, 1] = swap(own, "fsdp", 1)
-    other[0, 0] = swap(own, "mp", 2)
+    flags = [teacher == own_index ^ 2, teacher == own_index ^ 1, partner[own_index ^ 1] == own_index]
+    choice, across, offer = [jnp.where(flag, 0, 1).astype(jnp.int32).reshape(1) for flag in flags]
+    other[0, 0] = swap(after(own, choice), "mp", 2)
     other[0, 1] = swap(same[0, 1], "mp", 2)
     same[far, 0] = fetch(after(own, same[near[0], 0]), far)
-    flags = [teacher == own_index ^ 2, teacher == own_index ^ 1, partner[own_index ^ 1] == own_index]
-    choice, across, offer = [jnp.where(flag, 0, 1).astype(jnp.int32).reshape(1) for flag in flags]
     place, choice, across, offer = phase(place, choice, across, offer)
     student = normed_input(place, hidden_in[0], gain_in.astype(jnp.float32), order, rows)
     gains_own = jnp.concatenate([gain_in, key_gain], axis=1)

time: 196 us -> 197 us (level)
  waiting for transfers between devices: 91.5 us -> 95.1 us
    ppermute x8, waiting for transfers between devices: 50.2 us -> 55.5 us  [fetch(): lax.ppermute(value, 'fsdp', [(i, (i - 2 * step) % size) for i in range(si...]
    ppermute x24, starting transfers between devices: 25.9 us -> 23.6 us  [swap(): lax.ppermute(value, axis, [(i, i ^ bit) for i in range(lax.axis_size(axis...]
  transfers between devices with their start and end apart: 32 -> 32, of which waited for: 15 -> 15; matrix products, arithmetic and copies ran while one was open for 3% -> 3% of each run, Pallas kernels for 23% -> 22%
where the time goes in v7:
time: 197 us; the launch traced here: 196 us
  waiting for transfers between devices  95.1 us (48%)
  Pallas kernels  51.9 us (26%)
  starting transfers between devices  37.6 us (19%)
  between operations  4.67 us (2%)
  local copies, waits for them, and re-layouts  4.32 us (2%)
  other arithmetic  2.53 us (1%)
    ppermute x8, waiting for transfers between devices, fetch(): lax.ppermute(value, 'fsdp', [(i, (i - 2 * step) % size) for i in range(si...  55.5 us
    ppermute x24, waiting for transfers between devices, swap(): lax.ppermute(value, axis, [(i, i ^ bit) for i in range(lax.axis_size(axis...  39.7 us
    ppermute x24, starting transfers between devices, swap(): lax.ppermute(value, axis, [(i, i ^ bit) for i in range(lax.axis_size(axis...  23.6 us
    pallas_call x2, Pallas kernels, normed_input(): pl.pallas_call(functools.partial(norm_kernel, order, rows), grid=(tokens...  19.1 us
    pallas_call x3, Pallas kernels, early_keys(): pl.pallas_call(functools.partial(early_kernel, counts, bool(before)), gri...  14.6 us
    ppermute x8, starting transfers between devices, fetch(): lax.ppermute(value, 'fsdp', [(i, (i - 2 * step) % size) for i in range(si...  14 us
    pallas_call x3, Pallas kernels, grad_blocks(): pl.pallas_call(grad_kernel, grid=(count,), in_specs=[pl.BlockSpec((tokens...  8.62 us
    pallas_call x1, Pallas kernels, late_keys(): pl.pallas_call(functools.partial(late_kernel, counts), grid=(tokens // LA...  7.8 us
  transfers between devices with their start and end apart: 32, of which 15 were waited for; matrix products, arithmetic and copies ran while one was open for 3% of the time, Pallas kernels for 22%

profile of v7, /device:TPU:0, one launch (start us, length us, event | category | flops | bytes accessed | tf_op | source)
XLA Modules:
  0.0 196.1 jit_solution(4676541282526645781)
XLA Ops:
  0.6 3.0 %collective-permute-start.2 = (bf16[640,512]{1,0:T(8,128)(2,1)}, bf16[640,512]{1,0:T(8,128)(2,1)S(1)}, u32[]{:S(2)}, u32[]{:S(2)}) collective-permute-start(bf16[640,512]{1,0:T(8,128)(2,1)} %bitcast.39), channel_id=1, source_target_pairs={{0,1},{1,0},{2,3},{3,2},{4,5},{5,4},{6,7},{7,6},{8,9},{9,8},{10,11... | collective-permute-start | bytes 1966088 | tf_op jit(solution)/shard_map/ppermute | solution.py:248
  3.7 3.6 %collective-permute-start.4 = (bf16[640,512]{1,0:T(8,128)(2,1)}, bf16[640,512]{1,0:T(8,128)(2,1)S(1)}, u32[]{:S(2)}, u32[]{:S(2)}) collective-permute-start(bf16[640,512]{1,0:T(8,128)(2,1)} %bitcast.40), channel_id=1, source_target_pairs={{0,6},{1,7},{2,0},{3,1},{4,2},{5,3},{6,4},{7,5},{8,14},{9,15},{10,... | collective-permute-start | bytes 1966088 | tf_op jit(solution)/shard_map/ppermute | solution.py:253
  9.2 1.6 collective-permute-start.1
  10.8 7.8 %collective-permute-done.2.refs_1_ = bf16[640,512]{1,0:T(8,128)(2,1)S(1)} collective-permute-done((bf16[640,512]{1,0:T(8,128)(2,1)}, bf16[640,512]{1,0:T(8,128)(2,1)S(1)}, u32[]{:S(2)}, u32[]{:S(2)}) %collective-permute-start.2) | collective-permute-done | bytes 655392 | tf_op jit(solution)/shard_map/ppermute | solution.py:248
  18.6 1.7 collective-permute-start.3
  23.5 9.6 %norm_input.2.normed_ref.student_ref.refs_5_.refs_6_ = bf16[768,5120]{1,0:T(8,128)(2,1)} custom-call(s32[1]{0:T(128)} %bitcast.place_ref, bf16[768,5120]{1,0:T(8,128)(2,1)} %bitcast.48, f32[1,5120]{1,0:T(1,128)S(1)} %get-tuple-element.105.gain_ref), custom_call_target="tpu_custom_call" | custom-call | flops 1 | bytes 1 | tf_op jit(solution)/shard_map/norm_input/pallas_call | solution.py:34
  33.1 6.8 %collective-permute-done = bf16[1,5248]{1,0:T(2,128)(2,1)S(1)} collective-permute-done((bf16[1,5248]{1,0:T(2,128)(2,1)S(1)}, bf16[1,5248]{1,0:T(2,128)(2,1)S(1)}, u32[]{:S(2)}, u32[]{:S(2)}) %collective-permute-start) | collective-permute-done | bytes 10528 | tf_op jit(solution)/shard_map/ppermute | solution.py:248
  40.9 1.5 collective-permute-start.10
  43.4 1.5 collective-permute-start.9
  45.0 9.5 %norm_input.3.normed_ref.teacher_ref = bf16[768,5120]{1,0:T(8,128)(2,1)} custom-call(s32[1]{0:T(128)} %bitcast.place_ref, bf16[768,5120]{1,0:T(8,128)(2,1)} %bitcast.49, f32[1,5120]{1,0:T(1,128)S(1)} %slice.67.gain_ref), custom_call_target="tpu_custom_call" | custom-call | flops 1 | bytes 1 | tf_op jit(solution)/shard_map/norm_input/pallas_call | solution.py:34
  54.6 17.6 %collective-permute-done.6.refs_5_.refs_1_ = bf16[640,512]{1,0:T(8,128)(2,1)S(1)} collective-permute-done((bf16[640,512]{1,0:T(8,128)(2,1)S(1)}, bf16[640,512]{1,0:T(8,128)(2,1)S(1)}, u32[]{:S(2)}, u32[]{:S(2)}) %collective-permute-start.6) | collective-permute-done | bytes 655392 | tf_op jit(solution)/shard_map/ppermute | solution.py:253
  75.2 2.0 collective-permute-start.16
  78.7 6.7 %early_keys.3.part_s_ref = f32[768,512]{1,0:T(8,128)S(1)} custom-call(s32[1]{0:T(128)} %bitcast.2.choice_ref, bf16[768,5120]{1,0:T(8,128)(2,1)} %norm_input.2.normed_ref.student_ref.refs_5_.refs_6_, bf16[640,512]{1,0:T(8,128)(2,1)S(1)} %bitcast.45, bf16[640,512]{1,0:T(8,128)(2,1)S(1)} %collective-permute-done.2.refs_1_, ...), custom_call_target="tpu_custom_call" | custom-call | flops 1 | bytes 1 | tf_op jit(solution)/shard_map/early_keys/pallas_call | solution.py:118
  85.4 6.1 %collective-permute-done.13.refs_3_.refs_1_ = bf16[640,512]{1,0:T(8,128)(2,1)S(1)} collective-permute-done((bf16[640,512]{1,0:T(8,128)(2,1)S(1)}, bf16[640,512]{1,0:T(8,128)(2,1)S(1)}, u32[]{:S(2)}, u32[]{:S(2)}) %collective-permute-start.13) | collective-permute-done | bytes 655392 | tf_op jit(solution)/shard_map/ppermute | solution.py:248
  92.5 4.6 %early_keys.4.refs_3_ = f32[768,512]{1,0:T(8,128)S(1)} custom-call(s32[1]{0:T(128)} %bitcast.2.choice_ref, bf16[768,5120]{1,0:T(8,128)(2,1)} %norm_input.3.normed_ref.teacher_ref, bf16[640,512]{1,0:T(8,128)(2,1)S(1)} %collective-permute-done.1.refs_4_.refs_0_, bf16[640,512]{1,0:T(8,128)(2,1)S(1)} %collective-permute-done.3.refs_5_.refs_1_, ...), custom_call_target="tpu_custom_call" | custom-call | flops 1 | bytes 1 | tf_op jit(solution)/shard_map/early_keys/pallas_call | solution.py:118
  97.1 9.6 %collective-permute-done.16.refs_1_ = bf16[640,512]{1,0:T(8,128)(2,1)S(1)} collective-permute-done((bf16[640,512]{1,0:T(8,128)(2,1)S(1)}, bf16[640,512]{1,0:T(8,128)(2,1)S(1)}, u32[]{:S(2)}, u32[]{:S(2)}) %collective-permute-start.16) | collective-permute-done | bytes 655392 | tf_op jit(solution)/shard_map/ppermute | solution.py:253
  107.9 3.3 %early_keys.5.part_t_ref = f32[768,512]{1,0:T(8,128)S(1)} custom-call(s32[1]{0:T(128)} %bitcast.2.choice_ref, bf16[768,5120]{1,0:T(8,128)(2,1)} %norm_input.3.normed_ref.teacher_ref, bf16[640,512]{1,0:T(8,128)(2,1)S(1)} %collective-permute-done.12.refs_2_.refs_0_, bf16[640,512]{1,0:T(8,128)(2,1)S(1)} %collective-permute-done.13.refs_3_.refs_1_, ...), custom_call_target="tpu_custom_call" | custom-call | flops 1 | bytes 1 | tf_op jit(solution)/shard_map/early_keys/pallas_call | solution.py:118
  111.2 7.8 %late_keys.1 = (bf16[768,512]{1,0:T(8,128)(2,1)S(1)}, f32[1,256]{1,0:T(1,128)S(1)}, f32[512,640]{1,0:T(8,128)S(1)}, bf16[512,640]{1,0:T(8,128)(2,1)S(1)}) custom-call(s32[1]{0:T(128)} %bitcast.2.choice_ref, bf16[768,5120]{1,0:T(8,128)(2,1)} %norm_input.2.normed_ref.student_ref.refs_5_.refs_6_, bf16[768,5120]{1,0:T(8,128)(2,1)} %norm_input.3.normed_ref.teacher_ref, ...), custom_call_target="tpu_custom_call" | custom-call | flops 1 | bytes 1 | tf_op jit(solution)/shard_map/late_keys/pallas_call | solution.py:197
  120.0 3.0 %collective-permute-start.22 = (f32[256]{0:T(256)S(1)}, f32[256]{0:T(256)S(1)}, u32[]{:S(2)}, u32[]{:S(2)}) collective-permute-start(f32[256]{0:T(256)S(1)} %bitcast.46), channel_id=1, source_target_pairs={{0,2},{1,3},{2,0},{3,1},{4,6},{5,7},{6,4},{7,5},{8,10},{9,11},{10,... | collective-permute-start | bytes 3080 | tf_op jit(solution)/shard_map/ppermute | solution.py:248
  123.0 1.5 collective-permute-done.22
  125.5 1.6 collective-permute-start.23
  127.1 1.9 collective-permute-done.24
  129.7 2.3 %collective-permute-start.27 = (bf16[256,640]{1,0:T(8,128)(2,1)S(1)}, bf16[256,640]{1,0:T(8,128)(2,1)S(1)}, u32[]{:S(2)}, u32[]{:S(2)}) collective-permute-start(bf16[256,640]{1,0:T(8,128)(2,1)S(1)} %add_convert_fusion.2), channel_id=1, source_target_pairs={{0,4},{1,5},{2,6},{3,7},{4,0},{5,1},{6,2},{7,3},{8,12},{9,13},{10,... | collective-permute-start | bytes 983048 | tf_op jit(solution)/shard_map/ppermute | solution.py:253
  132.0 2.9 %grad_blocks.3 = bf16[2,512,640]{2,1,0:T(8,128)(2,1)S(1)} custom-call(bf16[768,512]{1,0:T(8,128)(2,1)S(1)} %get-tuple-element.74.grad_ref, bf16[768,5120]{1,0:T(8,128)(2,1)} %norm_input.2.normed_ref.student_ref.refs_5_.refs_6_), custom_call_target="tpu_custom_call" | custom-call | flops 1 | bytes 1 | tf_op jit(solution)/shard_map/grad_blocks/pallas_call | solution.py:232
  135.6 2.9 %grad_blocks.4 = f32[2,512,640]{2,1,0:T(8,128)S(1)} custom-call(bf16[768,512]{1,0:T(8,128)(2,1)S(1)} %get-tuple-element.74.grad_ref, bf16[768,5120]{1,0:T(8,128)(2,1)} %norm_input.2.normed_ref.student_ref.refs_5_.refs_6_), custom_call_target="tpu_custom_call" | custom-call | flops 1 | bytes 1 | tf_op jit(solution)/shard_map/grad_blocks/pallas_call | solution.py:232
  138.4 2.9 %grad_blocks.5 = f32[2,512,640]{2,1,0:T(8,128)S(1)} custom-call(bf16[768,512]{1,0:T(8,128)(2,1)S(1)} %get-tuple-element.74.grad_ref, bf16[768,5120]{1,0:T(8,128)(2,1)} %norm_input.2.normed_ref.student_ref.refs_5_.refs_6_), custom_call_target="tpu_custom_call" | custom-call | flops 1 | bytes 1 | tf_op jit(solution)/shard_map/grad_blocks/pallas_call | solution.py:232
  142.6 12.8 %collective-permute-done.27 = bf16[256,640]{1,0:T(8,128)(2,1)S(1)} collective-permute-done((bf16[256,640]{1,0:T(8,128)(2,1)S(1)}, bf16[256,640]{1,0:T(8,128)(2,1)S(1)}, u32[]{:S(2)}, u32[]{:S(2)}) %collective-permute-start.27) | collective-permute-done | bytes 327712 | tf_op jit(solution)/shard_map/ppermute | solution.py:253
  156.6 4.1 %collective-permute-done.25 = bf16[256,640]{1,0:T(8,128)(2,1)S(1)} collective-permute-done((bf16[256,640]{1,0:T(8,128)(2,1)S(1)}, bf16[256,640]{1,0:T(8,128)(2,1)S(1)}, u32[]{:S(2)}, u32[]{:S(2)}) %collective-permute-start.25) | collective-permute-done | bytes 327712 | tf_op jit(solution)/shard_map/ppermute | solution.py:253
  161.8 8.5 %collective-permute-done.29 = bf16[512,640]{1,0:T(8,128)(2,1)S(1)} collective-permute-done((bf16[512,640]{1,0:T(8,128)(2,1)S(1)}, bf16[512,640]{1,0:T(8,128)(2,1)S(1)}, u32[]{:S(2)}, u32[]{:S(2)}) %collective-permute-start.29) | collective-permute-done | bytes 655392 | tf_op jit(solution)/shard_map/ppermute | solution.py:248
  170.5 4.1 %collective-permute-start.30 = (bf16[512,640]{1,0:T(8,128)(2,1)S(1)}, bf16[512,640]{1,0:T(8,128)(2,1)S(1)}, u32[]{:S(2)}, u32[]{:S(2)}) collective-permute-start(bf16[512,640]{1,0:T(8,128)(2,1)S(1)} %add_convert_fusion), channel_id=1, source_target_pairs={{0,6},{1,7},{2,0},{3,1},{4,2},{5,3},{6,4},{7,5},{8,14},{9,15},{10,... | collective-permute-start | bytes 1966088 | tf_op jit(solution)/shard_map/ppermute | solution.py:253
  175.1 4.9 %collective-permute-done.31 = f32[256]{0:T(256)S(1)} collective-permute-done((f32[256]{0:T(256)S(1)}, f32[256]{0:T(256)S(1)}, u32[]{:S(2)}, u32[]{:S(2)}) %collective-permute-start.31) | collective-permute-done | bytes 1056 | tf_op jit(solution)/shard_map/ppermute | solution.py:248
  181.8 11.4 %collective-permute-done.30 = bf16[512,640]{1,0:T(8,128)(2,1)S(1)} collective-permute-done((bf16[512,640]{1,0:T(8,128)(2,1)S(1)}, bf16[512,640]{1,0:T(8,128)(2,1)S(1)}, u32[]{:S(2)}, u32[]{:S(2)}) %collective-permute-start.30) | collective-permute-done | bytes 655392 | tf_op jit(solution)/shard_map/ppermute | solution.py:253
  (69 shorter events, 22.4 us)
Async XLA Ops:
  0.6 18.0 %collective-permute-start.2 = (bf16[640,512]{1,0:T(8,128)(2,1)}, bf16[640,512]{1,0:T(8,128)(2,1)S(1)}, u32[]{:S(2)}, u32[]{:S(2)}) collective-permute-start(bf16[640,512]{1,0:T(8,128)(2,1)} %bitcast.39), channel_id=1, source_target_pairs={{0,1},{1,0},{2,3},{3,2},{4,5},{5,4},{6,7},{7,6},{8,9},{9,8},{10,11... | collective-permute-start | bytes 1966088 | tf_op jit(solution)/shard_map/ppermute | solution.py:248
  3.7 36.3 %collective-permute-start.4 = (bf16[640,512]{1,0:T(8,128)(2,1)}, bf16[640,512]{1,0:T(8,128)(2,1)S(1)}, u32[]{:S(2)}, u32[]{:S(2)}) collective-permute-start(bf16[640,512]{1,0:T(8,128)(2,1)} %bitcast.40), channel_id=1, source_target_pairs={{0,6},{1,7},{2,0},{3,1},{4,2},{5,3},{6,4},{7,5},{8,14},{9,15},{10,... | collective-permute-start | bytes 1966088 | tf_op jit(solution)/shard_map/ppermute | solution.py:253
  7.3 32.7 %collective-permute-start.5 = (bf16[640,512]{1,0:T(8,128)(2,1)}, bf16[640,512]{1,0:T(8,128)(2,1)S(1)}, u32[]{:S(2)}, u32[]{:S(2)}) collective-permute-start(bf16[640,512]{1,0:T(8,128)(2,1)} %bitcast.41), channel_id=1, source_target_pairs={{0,2},{1,3},{2,4},{3,5},{4,6},{5,7},{6,0},{7,1},{8,10},{9,11},{10,... | collective-permute-start | bytes 1966088 | tf_op jit(solution)/shard_map/ppermute | solution.py:253
  9.2 30.7 %collective-permute-start.1 = (bf16[640,512]{1,0:T(8,128)(2,1)}, bf16[640,512]{1,0:T(8,128)(2,1)S(1)}, u32[]{:S(2)}, u32[]{:S(2)}) collective-permute-start(bf16[640,512]{1,0:T(8,128)(2,1)} %bitcast.42), channel_id=1, source_target_pairs={{0,16},{8,24},{16,0},{24,8},{1,17},{9,25},{17,1},{25,9},{2,18},{10... | collective-permute-start | bytes 1966088 | tf_op jit(solution)/shard_map/ppermute | solution.py:248
  18.6 21.3 %collective-permute-start.3 = (bf16[640,512]{1,0:T(8,128)(2,1)S(1)}, bf16[640,512]{1,0:T(8,128)(2,1)S(1)}, u32[]{:S(2)}, u32[]{:S(2)}) collective-permute-start(bf16[640,512]{1,0:T(8,128)(2,1)S(1)} %collective-permute-done.2.refs_1_), channel_id=1, source_target_pairs={{0,16},{8,24},{16,0},{24,8},{1,17},{9,25},{17,1},{25,9},{2,18},{10... | collective-permute-start | bytes 1966088 | tf_op jit(solution)/shard_map/ppermute | solution.py:248
  21.9 18.0 %collective-permute-start = (bf16[1,5248]{1,0:T(2,128)(2,1)S(1)}, bf16[1,5248]{1,0:T(2,128)(2,1)S(1)}, u32[]{:S(2)}, u32[]{:S(2)}) collective-permute-start(bf16[1,5248]{1,0:T(2,128)(2,1)S(1)} %get-tuple-element.107), channel_id=1, source_target_pairs={{0,16},{8,24},{16,0},{24,8},{1,17},{9,25},{17,1},{25,9},{2,18},{10... | collective-permute-start | bytes 31496 | tf_op jit(solution)/shard_map/ppermute | solution.py:248
  40.0 3.4 %collective-permute-start.7 = (bf16[2,5248]{1,0:T(2,128)(2,1)S(1)}, bf16[2,5248]{1,0:T(2,128)(2,1)S(1)}, u32[]{:S(2)}, u32[]{:S(2)}) collective-permute-start(bf16[2,5248]{1,0:T(2,128)(2,1)S(1)} %pad_maximum_fusion), channel_id=1, source_target_pairs={{0,8},{8,0},{16,24},{24,16},{1,9},{9,1},{17,25},{25,17},{2,10},{10... | collective-permute-start | bytes 62984 | tf_op jit(solution)/shard_map/ppermute | solution.py:248
  40.1 32.1 %collective-permute-start.6 = (bf16[640,512]{1,0:T(8,128)(2,1)S(1)}, bf16[640,512]{1,0:T(8,128)(2,1)S(1)}, u32[]{:S(2)}, u32[]{:S(2)}) collective-permute-start(bf16[640,512]{1,0:T(8,128)(2,1)S(1)} %bitcast.43), channel_id=1, source_target_pairs={{0,4},{1,5},{2,6},{3,7},{4,0},{5,1},{6,2},{7,3},{8,12},{9,13},{10,... | collective-permute-start | bytes 1966088 | tf_op jit(solution)/shard_map/ppermute | solution.py:253
  40.9 31.3 %collective-permute-start.10 = (bf16[640,512]{1,0:T(8,128)(2,1)S(1)}, bf16[640,512]{1,0:T(8,128)(2,1)S(1)}, u32[]{:S(2)}, u32[]{:S(2)}) collective-permute-start(bf16[640,512]{1,0:T(8,128)(2,1)S(1)} %collective-permute-done.4.refs_2_), channel_id=1, source_target_pairs={{0,16},{8,24},{16,0},{24,8},{1,17},{9,25},{17,1},{25,9},{2,18},{10... | collective-permute-start | bytes 1966088 | tf_op jit(solution)/shard_map/ppermute | solution.py:248
  42.4 29.8 %collective-permute-start.8 = (bf16[640,512]{1,0:T(8,128)(2,1)S(1)}, bf16[640,512]{1,0:T(8,128)(2,1)S(1)}, u32[]{:S(2)}, u32[]{:S(2)}) collective-permute-start(bf16[640,512]{1,0:T(8,128)(2,1)S(1)} %collective-permute-done.4.refs_2_), channel_id=1, source_target_pairs={{0,1},{1,0},{2,3},{3,2},{4,5},{5,4},{6,7},{7,6},{8,9},{9,8},{10,11... | collective-permute-start | bytes 1966088 | tf_op jit(solution)/shard_map/ppermute | solution.py:248
  42.9 29.3 %collective-permute-start.11 = (bf16[640,512]{1,0:T(8,128)(2,1)S(1)}, bf16[640,512]{1,0:T(8,128)(2,1)S(1)}, u32[]{:S(2)}, u32[]{:S(2)}) collective-permute-start(bf16[640,512]{1,0:T(8,128)(2,1)S(1)} %collective-permute-done.5.refs_3_), channel_id=1, source_target_pairs={{0,16},{8,24},{16,0},{24,8},{1,17},{9,25},{17,1},{25,9},{2,18},{10... | collective-permute-start | bytes 1966088 | tf_op jit(solution)/shard_map/ppermute | solution.py:248
  43.4 29.5 %collective-permute-start.9 = (bf16[640,512]{1,0:T(8,128)(2,1)S(1)}, bf16[640,512]{1,0:T(8,128)(2,1)S(1)}, u32[]{:S(2)}, u32[]{:S(2)}) collective-permute-start(bf16[640,512]{1,0:T(8,128)(2,1)S(1)} %collective-permute-done.5.refs_3_), channel_id=1, source_target_pairs={{0,1},{1,0},{2,3},{3,2},{4,5},{5,4},{6,7},{7,6},{8,9},{9,8},{10,11... | collective-permute-start | bytes 1966088 | tf_op jit(solution)/shard_map/ppermute | solution.py:248
  73.8 18.7 %collective-permute-start.15 = (bf16[2560,512]{1,0:T(8,128)(2,1)S(1)}, bf16[2560,512]{1,0:T(8,128)(2,1)S(1)}, u32[]{:S(2)}, u32[]{:S(2)}) collective-permute-start(bf16[2560,512]{1,0:T(8,128)(2,1)S(1)} %pack_blocks.4), channel_id=1, source_target_pairs={{0,8},{8,0},{16,24},{24,16},{1,9},{9,1},{17,25},{25,17},{2,10},{10... | collective-permute-start | bytes 7864328 | tf_op jit(solution)/shard_map/ppermute | solution.py:248
  73.9 17.6 %collective-permute-start.13 = (bf16[640,512]{1,0:T(8,128)(2,1)S(1)}, bf16[640,512]{1,0:T(8,128)(2,1)S(1)}, u32[]{:S(2)}, u32[]{:S(2)}) collective-permute-start(bf16[640,512]{1,0:T(8,128)(2,1)S(1)} %collective-permute-done.6.refs_5_.refs_1_), channel_id=1, source_target_pairs={{0,16},{8,24},{16,0},{24,8},{1,17},{9,25},{17,1},{25,9},{2,18},{10... | collective-permute-start | bytes 1966088 | tf_op jit(solution)/shard_map/ppermute | solution.py:248
  74.7 17.3 %collective-permute-start.12 = (bf16[640,512]{1,0:T(8,128)(2,1)S(1)}, bf16[640,512]{1,0:T(8,128)(2,1)S(1)}, u32[]{:S(2)}, u32[]{:S(2)}) collective-permute-start(bf16[640,512]{1,0:T(8,128)(2,1)S(1)} %collective-permute-done.10.refs_6_.refs_2_), channel_id=1, source_target_pairs={{0,1},{1,0},{2,3},{3,2},{4,5},{5,4},{6,7},{7,6},{8,9},{9,8},{10,11... | collective-permute-start | bytes 1966088 | tf_op jit(solution)/shard_map/ppermute | solution.py:248
  75.2 31.5 %collective-permute-start.16 = (bf16[640,512]{1,0:T(8,128)(2,1)S(1)}, bf16[640,512]{1,0:T(8,128)(2,1)S(1)}, u32[]{:S(2)}, u32[]{:S(2)}) collective-permute-start(bf16[640,512]{1,0:T(8,128)(2,1)S(1)} %collective-permute-done.2.refs_1_), channel_id=1, source_target_pairs={{0,4},{1,5},{2,6},{3,7},{4,0},{5,1},{6,2},{7,3},{8,12},{9,13},{10,... | collective-permute-start | bytes 1966088 | tf_op jit(solution)/shard_map/ppermute | solution.py:253
  77.2 29.5 %collective-permute-start.17 = (bf16[640,512]{1,0:T(8,128)(2,1)S(1)}, bf16[640,512]{1,0:T(8,128)(2,1)S(1)}, u32[]{:S(2)}, u32[]{:S(2)}) collective-permute-start(bf16[640,512]{1,0:T(8,128)(2,1)S(1)} %collective-permute-done.9.refs_0_), channel_id=1, source_target_pairs={{0,16},{8,24},{16,0},{24,8},{1,17},{9,25},{17,1},{25,9},{2,18},{10... | collective-permute-start | bytes 1966088 | tf_op jit(solution)/shard_map/ppermute | solution.py:248
  91.5 15.8 %collective-permute-start.18 = (bf16[640,512]{1,0:T(8,128)(2,1)S(1)}, bf16[640,512]{1,0:T(8,128)(2,1)S(1)}, u32[]{:S(2)}, u32[]{:S(2)}) collective-permute-start(bf16[640,512]{1,0:T(8,128)(2,1)S(1)} %collective-permute-done.13.refs_3_.refs_1_), channel_id=1, source_target_pairs={{0,1},{1,0},{2,3},{3,2},{4,5},{5,4},{6,7},{7,6},{8,9},{9,8},{10,11... | collective-permute-start | bytes 1966088 | tf_op jit(solution)/shard_map/ppermute | solution.py:248
  92.4 15.4 %collective-permute-start.14 = (bf16[1280,512]{1,0:T(8,128)(2,1)S(1)}, bf16[1280,512]{1,0:T(8,128)(2,1)S(1)}, u32[]{:S(2)}, u32[]{:S(2)}) collective-permute-start(bf16[1280,512]{1,0:T(8,128)(2,1)S(1)} %pack_blocks.3), channel_id=1, source_target_pairs={{0,8},{8,0},{16,24},{24,16},{1,9},{9,1},{17,25},{25,17},{2,10},{10... | collective-permute-start | bytes 3932168 | tf_op jit(solution)/shard_map/ppermute | solution.py:248
  107.8 3.4 %collective-permute-start.19 = (bf16[1280,512]{1,0:T(8,128)(2,1)S(1)}, bf16[1280,512]{1,0:T(8,128)(2,1)S(1)}, u32[]{:S(2)}, u32[]{:S(2)}) collective-permute-start(bf16[1280,512]{1,0:T(8,128)(2,1)S(1)} %pack_blocks.5), channel_id=1, source_target_pairs={{0,8},{8,0},{16,24},{24,16},{1,9},{9,1},{17,25},{25,17},{2,10},{10... | collective-permute-start | bytes 3932168 | tf_op jit(solution)/shard_map/ppermute | solution.py:248
  119.1 10.6 %collective-permute-start.20 = (bf16[256,640]{1,0:T(8,128)(2,1)S(1)}, bf16[256,640]{1,0:T(8,128)(2,1)S(1)}, u32[]{:S(2)}, u32[]{:S(2)}) collective-permute-start(bf16[256,640]{1,0:T(8,128)(2,1)S(1)} %get-tuple-element.103), channel_id=1, source_target_pairs={{0,1},{1,0},{2,3},{3,2},{4,5},{5,4},{6,7},{7,6},{8,9},{9,8},{10,11... | collective-permute-start | bytes 983048 | tf_op jit(solution)/shard_map/ppermute | solution.py:248
  120.0 4.5 %collective-permute-start.22 = (f32[256]{0:T(256)S(1)}, f32[256]{0:T(256)S(1)}, u32[]{:S(2)}, u32[]{:S(2)}) collective-permute-start(f32[256]{0:T(256)S(1)} %bitcast.46), channel_id=1, source_target_pairs={{0,2},{1,3},{2,0},{3,1},{4,6},{5,7},{6,4},{7,5},{8,10},{9,11},{10,... | collective-permute-start | bytes 3080 | tf_op jit(solution)/shard_map/ppermute | solution.py:248
  124.6 4.5 %collective-permute-start.24 = (f32[256]{0:T(256)S(1)}, f32[256]{0:T(256)S(1)}, u32[]{:S(2)}, u32[]{:S(2)}) collective-permute-start(f32[256]{0:T(256)S(1)} %add.41), channel_id=1, source_target_pairs={{0,4},{1,5},{2,6},{3,7},{4,0},{5,1},{6,2},{7,3},{8,12},{9,13},{10,... | collective-permute-start | bytes 3080 | tf_op jit(solution)/shard_map/ppermute | solution.py:248
  125.5 15.8 %collective-permute-start.23 = (bf16[256,640]{1,0:T(8,128)(2,1)S(1)}, bf16[256,640]{1,0:T(8,128)(2,1)S(1)}, u32[]{:S(2)}, u32[]{:S(2)}) collective-permute-start(bf16[256,640]{1,0:T(8,128)(2,1)S(1)} %get-tuple-element.78), channel_id=1, source_target_pairs={{0,1},{1,0},{2,3},{3,2},{4,5},{5,4},{6,7},{7,6},{8,9},{9,8},{10,11... | collective-permute-start | bytes 983048 | tf_op jit(solution)/shard_map/ppermute | solution.py:248
  129.7 25.7 %collective-permute-start.27 = (bf16[256,640]{1,0:T(8,128)(2,1)S(1)}, bf16[256,640]{1,0:T(8,128)(2,1)S(1)}, u32[]{:S(2)}, u32[]{:S(2)}) collective-permute-start(bf16[256,640]{1,0:T(8,128)(2,1)S(1)} %add_convert_fusion.2), channel_id=1, source_target_pairs={{0,4},{1,5},{2,6},{3,7},{4,0},{5,1},{6,2},{7,3},{8,12},{9,13},{10,... | collective-permute-start | bytes 983048 | tf_op jit(solution)/shard_map/ppermute | solution.py:253
  135.0 25.6 %collective-permute-start.21 = (bf16[512,640]{1,0:T(8,128)(2,1)S(1)}, bf16[512,640]{1,0:T(8,128)(2,1)S(1)}, u32[]{:S(2)}, u32[]{:S(2)}) collective-permute-start(bf16[512,640]{1,0:T(8,128)(2,1)S(1)} %get-tuple-element.75), channel_id=1, source_target_pairs={{0,1},{1,0},{2,3},{3,2},{4,5},{5,4},{6,7},{7,6},{8,9},{9,8},{10,11... | collective-permute-start | bytes 1966088 | tf_op jit(solution)/shard_map/ppermute | solution.py:248
  141.4 19.2 %collective-permute-start.25 = (bf16[256,640]{1,0:T(8,128)(2,1)S(1)}, bf16[256,640]{1,0:T(8,128)(2,1)S(1)}, u32[]{:S(2)}, u32[]{:S(2)}) collective-permute-start(bf16[256,640]{1,0:T(8,128)(2,1)S(1)} %add_convert_fusion.3), channel_id=1, source_target_pairs={{0,4},{1,5},{2,6},{3,7},{4,0},{5,1},{6,2},{7,3},{8,12},{9,13},{10,... | collective-permute-start | bytes 983048 | tf_op jit(solution)/shard_map/ppermute | solution.py:253
  155.4 14.9 %collective-permute-start.29 = (bf16[512,640]{1,0:T(8,128)(2,1)S(1)}, bf16[512,640]{1,0:T(8,128)(2,1)S(1)}, u32[]{:S(2)}, u32[]{:S(2)}) collective-permute-start(bf16[512,640]{1,0:T(8,128)(2,1)S(1)} %get-tuple-element.88), channel_id=1, source_target_pairs={{0,1},{1,0},{2,3},{3,2},{4,5},{5,4},{6,7},{7,6},{8,9},{9,8},{10,11... | collective-permute-start | bytes 1966088 | tf_op jit(solution)/shard_map/ppermute | solution.py:248
  160.6 21.1 %collective-permute-start.26 = (bf16[512,640]{1,0:T(8,128)(2,1)S(1)}, bf16[512,640]{1,0:T(8,128)(2,1)S(1)}, u32[]{:S(2)}, u32[]{:S(2)}) collective-permute-start(bf16[512,640]{1,0:T(8,128)(2,1)S(1)} %fusion.5), channel_id=1, source_target_pairs={{0,1},{1,0},{2,3},{3,2},{4,5},{5,4},{6,7},{7,6},{8,9},{9,8},{10,11... | collective-permute-start | bytes 1966088 | tf_op jit(solution)/shard_map/ppermute | solution.py:248
  161.7 20.1 %collective-permute-start.28 = (bf16[512,640]{1,0:T(8,128)(2,1)S(1)}, bf16[512,640]{1,0:T(8,128)(2,1)S(1)}, u32[]{:S(2)}, u32[]{:S(2)}) collective-permute-start(bf16[512,640]{1,0:T(8,128)(2,1)S(1)} %add_convert_fusion.1), channel_id=1, source_target_pairs={{0,2},{1,3},{2,4},{3,5},{4,6},{5,7},{6,0},{7,1},{8,10},{9,11},{10,... | collective-permute-start | bytes 1966088 | tf_op jit(solution)/shard_map/ppermute | solution.py:253
  170.5 22.7 %collective-permute-start.30 = (bf16[512,640]{1,0:T(8,128)(2,1)S(1)}, bf16[512,640]{1,0:T(8,128)(2,1)S(1)}, u32[]{:S(2)}, u32[]{:S(2)}) collective-permute-start(bf16[512,640]{1,0:T(8,128)(2,1)S(1)} %add_convert_fusion), channel_id=1, source_target_pairs={{0,6},{1,7},{2,0},{3,1},{4,2},{5,3},{6,4},{7,5},{8,14},{9,15},{10,... | collective-permute-start | bytes 1966088 | tf_op jit(solution)/shard_map/ppermute | solution.py:253
  174.6 5.5 %collective-permute-start.31 = (f32[256]{0:T(256)S(1)}, f32[256]{0:T(256)S(1)}, u32[]{:S(2)}, u32[]{:S(2)}) collective-permute-start(f32[256]{0:T(256)S(1)} %add.43), channel_id=1, source_target_pairs={{0,1},{1,0},{2,3},{3,2},{4,5},{5,4},{6,7},{7,6},{8,9},{9,8},{10,11... | collective-permute-start | bytes 3080 | tf_op jit(solution)/shard_map/ppermute | solution.py:248
  (1 other events, 16.6 us)

commit v8 on v6

--- a/solution.py
+++ b/solution.py
@@ -289,8 +289,8 @@
     student = normed_input(place, hidden_in[0], gain_in.astype(jnp.float32), order, rows)
     gains_own = jnp.concatenate([gain_in, key_gain], axis=1)
     gains_beside = swap(gains_own, "mp", 2)
-    student, gains_beside, other[0, 0], other[0, 1], *moved = phase(
-        student, gains_beside, other[0, 0], other[0, 1], *[same[step, 0] for step in near]
+    student, other[0, 0], other[0, 1], *moved = phase(
+        student, other[0, 0], other[0, 1], *[same[step, 0] for step in near]
     )
     gains_same = jnp.concatenate([gains_own, gains_beside], axis=0)
     gains_cross = swap(gains_same, "mp", 1)

time: 196 us -> 195 us (level)
  starting transfers between devices: 38.3 us -> 40.7 us
    ppermute x8, starting transfers between devices: 12.4 us -> 16.7 us  [fetch(): lax.ppermute(value, 'fsdp', [(i, (i - 2 * step) % size) for i in range(si...]
    ppermute x24, waiting for transfers between devices: 41.3 us -> 38.1 us  [swap(): lax.ppermute(value, axis, [(i, i ^ bit) for i in range(lax.axis_size(axis...]
    ppermute x8, waiting for transfers between devices: 50.2 us -> 52.4 us  [fetch(): lax.ppermute(value, 'fsdp', [(i, (i - 2 * step) % size) for i in range(si...]
  transfers between devices with their start and end apart: 32 -> 32, of which waited for: 15 -> 16; matrix products, arithmetic and copies ran while one was open for 3% -> 3% of each run, Pallas kernels for 23% -> 22%
where the time goes in v8:
time: 195 us
  waiting for transfers between devices  90.5 us (46%)
  Pallas kernels  51.9 us (27%)
  starting transfers between devices  40.7 us (21%)
  between operations  4.63 us (2%)
  local copies, waits for them, and re-layouts  4.33 us (2%)
  other arithmetic  2.53 us (1%)
    ppermute x8, waiting for transfers between devices, fetch(): lax.ppermute(value, 'fsdp', [(i, (i - 2 * step) % size) for i in range(si...  52.4 us
    ppermute x24, waiting for transfers between devices, swap(): lax.ppermute(value, axis, [(i, i ^ bit) for i in range(lax.axis_size(axis...  38.1 us
    ppermute x24, starting transfers between devices, swap(): lax.ppermute(value, axis, [(i, i ^ bit) for i in range(lax.axis_size(axis...  24 us
    pallas_call x2, Pallas kernels, normed_input(): pl.pallas_call(functools.partial(norm_kernel, order, rows), grid=(tokens...  19.1 us
    ppermute x8, starting transfers between devices, fetch(): lax.ppermute(value, 'fsdp', [(i, (i - 2 * step) % size) for i in range(si...  16.7 us
    pallas_call x3, Pallas kernels, early_keys(): pl.pallas_call(functools.partial(early_kernel, counts, bool(before)), gri...  14.6 us
    pallas_call x3, Pallas kernels, grad_blocks(): pl.pallas_call(grad_kernel, grid=(count,), in_specs=[pl.BlockSpec((tokens...  8.62 us
    pallas_call x1, Pallas kernels, late_keys(): pl.pallas_call(functools.partial(late_kernel, counts), grid=(tokens // KE...  7.86 us
  transfers between devices with their start and end apart: 32, of which 16 were waited for; matrix products, arithmetic and copies ran while one was open for 3% of the time, Pallas kernels for 22%

profile of v8, /device:TPU:0, one launch (start us, length us, event | category | flops | bytes accessed | tf_op | source)
XLA Modules:
  0.0 194.6 jit_solution(18150912006102670724)
XLA Ops:
  0.6 3.0 %collective-permute-start.1 = (bf16[640,512]{1,0:T(8,128)(2,1)}, bf16[640,512]{1,0:T(8,128)(2,1)S(1)}, u32[]{:S(2)}, u32[]{:S(2)}) collective-permute-start(bf16[640,512]{1,0:T(8,128)(2,1)} %bitcast.39), channel_id=1, source_target_pairs={{0,1},{1,0},{2,3},{3,2},{4,5},{5,4},{6,7},{7,6},{8,9},{9,8},{10,11... | collective-permute-start | bytes 1966088 | tf_op jit(solution)/shard_map/ppermute | solution.py:247
  6.7 3.6 %collective-permute-start.3 = (bf16[640,512]{1,0:T(8,128)(2,1)}, bf16[640,512]{1,0:T(8,128)(2,1)S(1)}, u32[]{:S(2)}, u32[]{:S(2)}) collective-permute-start(bf16[640,512]{1,0:T(8,128)(2,1)} %bitcast.40), channel_id=1, source_target_pairs={{0,6},{1,7},{2,0},{3,1},{4,2},{5,3},{6,4},{7,5},{8,14},{9,15},{10,... | collective-permute-start | bytes 1966088 | tf_op jit(solution)/shard_map/ppermute | solution.py:252
  10.9 7.7 %collective-permute-done.1.refs_1_ = bf16[640,512]{1,0:T(8,128)(2,1)S(1)} collective-permute-done((bf16[640,512]{1,0:T(8,128)(2,1)}, bf16[640,512]{1,0:T(8,128)(2,1)S(1)}, u32[]{:S(2)}, u32[]{:S(2)}) %collective-permute-start.1) | collective-permute-done | bytes 655392 | tf_op jit(solution)/shard_map/ppermute | solution.py:247
  18.6 1.7 collective-permute-start.2
  23.8 9.6 %norm_input.2.normed_ref.student_ref.refs_5_.refs_6_ = bf16[768,5120]{1,0:T(8,128)(2,1)} custom-call(s32[1]{0:T(128)} %bitcast.place_ref, bf16[768,5120]{1,0:T(8,128)(2,1)} %bitcast.48, f32[1,5120]{1,0:T(1,128)S(1)} %get-tuple-element.101.gain_ref), custom_call_target="tpu_custom_call" | custom-call | flops 1 | bytes 1 | tf_op jit(solution)/shard_map/norm_input/pallas_call | solution.py:33
  33.4 2.6 %collective-permute-start.5 = (bf16[640,512]{1,0:T(8,128)(2,1)S(1)}, bf16[640,512]{1,0:T(8,128)(2,1)S(1)}, u32[]{:S(2)}, u32[]{:S(2)}) collective-permute-start(bf16[640,512]{1,0:T(8,128)(2,1)S(1)} %bitcast.43), channel_id=1, source_target_pairs={{0,4},{1,5},{2,6},{3,7},{4,0},{5,1},{6,2},{7,3},{8,12},{9,13},{10,... | collective-permute-start | bytes 1966088 | tf_op jit(solution)/shard_map/ppermute | solution.py:252
  36.0 3.7 %collective-permute-done.4.refs_3_ = bf16[640,512]{1,0:T(8,128)(2,1)S(1)} collective-permute-done((bf16[640,512]{1,0:T(8,128)(2,1)}, bf16[640,512]{1,0:T(8,128)(2,1)S(1)}, u32[]{:S(2)}, u32[]{:S(2)}) %collective-permute-start.4) | collective-permute-done | bytes 655392 | tf_op jit(solution)/shard_map/ppermute | solution.py:252
  44.4 9.5 %norm_input.3.normed_ref.teacher_ref = bf16[768,5120]{1,0:T(8,128)(2,1)} custom-call(s32[1]{0:T(128)} %bitcast.place_ref, bf16[768,5120]{1,0:T(8,128)(2,1)} %bitcast.49, f32[1,5120]{1,0:T(1,128)S(1)} %slice.67.gain_ref), custom_call_target="tpu_custom_call" | custom-call | flops 1 | bytes 1 | tf_op jit(solution)/shard_map/norm_input/pallas_call | solution.py:33
  53.9 13.1 %collective-permute-done.5.refs_5_.refs_1_ = bf16[640,512]{1,0:T(8,128)(2,1)S(1)} collective-permute-done((bf16[640,512]{1,0:T(8,128)(2,1)S(1)}, bf16[640,512]{1,0:T(8,128)(2,1)S(1)}, u32[]{:S(2)}, u32[]{:S(2)}) %collective-permute-start.5) | collective-permute-done | bytes 655392 | tf_op jit(solution)/shard_map/ppermute | solution.py:252
  67.0 2.0 %collective-permute-done.11.refs_7_.refs_3_ = bf16[640,512]{1,0:T(8,128)(2,1)S(1)} collective-permute-done((bf16[640,512]{1,0:T(8,128)(2,1)S(1)}, bf16[640,512]{1,0:T(8,128)(2,1)S(1)}, u32[]{:S(2)}, u32[]{:S(2)}) %collective-permute-start.11) | collective-permute-done | bytes 655392 | tf_op jit(solution)/shard_map/ppermute | solution.py:247
  72.2 2.7 %collective-permute-start.16 = (bf16[640,512]{1,0:T(8,128)(2,1)S(1)}, bf16[640,512]{1,0:T(8,128)(2,1)S(1)}, u32[]{:S(2)}, u32[]{:S(2)}) collective-permute-start(bf16[640,512]{1,0:T(8,128)(2,1)S(1)} %collective-permute-done.1.refs_1_), channel_id=1, source_target_pairs={{0,4},{1,5},{2,6},{3,7},{4,0},{5,1},{6,2},{7,3},{8,12},{9,13},{10,... | collective-permute-start | bytes 1966088 | tf_op jit(solution)/shard_map/ppermute | solution.py:252
  74.9 1.9 collective-permute-start.17
  76.8 6.7 %early_keys.3.part_s_ref = f32[768,512]{1,0:T(8,128)S(1)} custom-call(s32[1]{0:T(128)} %bitcast.2.choice_ref, bf16[768,5120]{1,0:T(8,128)(2,1)} %norm_input.2.normed_ref.student_ref.refs_5_.refs_6_, bf16[640,512]{1,0:T(8,128)(2,1)S(1)} %bitcast.45, bf16[640,512]{1,0:T(8,128)(2,1)S(1)} %collective-permute-done.1.refs_1_, ...), custom_call_target="tpu_custom_call" | custom-call | flops 1 | bytes 1 | tf_op jit(solution)/shard_map/early_keys/pallas_call | solution.py:117
  83.5 4.2 %collective-permute-done.13.refs_3_.refs_1_ = bf16[640,512]{1,0:T(8,128)(2,1)S(1)} collective-permute-done((bf16[640,512]{1,0:T(8,128)(2,1)S(1)}, bf16[640,512]{1,0:T(8,128)(2,1)S(1)}, u32[]{:S(2)}, u32[]{:S(2)}) %collective-permute-start.13) | collective-permute-done | bytes 655392 | tf_op jit(solution)/shard_map/ppermute | solution.py:247
  89.1 4.6 %early_keys.4.refs_3_ = f32[768,512]{1,0:T(8,128)S(1)} custom-call(s32[1]{0:T(128)} %bitcast.2.choice_ref, bf16[768,5120]{1,0:T(8,128)(2,1)} %norm_input.3.normed_ref.teacher_ref, bf16[640,512]{1,0:T(8,128)(2,1)S(1)} %collective-permute-done.refs_4_.refs_0_, bf16[640,512]{1,0:T(8,128)(2,1)S(1)} %collective-permute-done.2.refs_5_.refs_1_, ...), custom_call_target="tpu_custom_call" | custom-call | flops 1 | bytes 1 | tf_op jit(solution)/shard_map/early_keys/pallas_call | solution.py:117
  93.6 10.2 %collective-permute-done.16.refs_1_ = bf16[640,512]{1,0:T(8,128)(2,1)S(1)} collective-permute-done((bf16[640,512]{1,0:T(8,128)(2,1)S(1)}, bf16[640,512]{1,0:T(8,128)(2,1)S(1)}, u32[]{:S(2)}, u32[]{:S(2)}) %collective-permute-start.16) | collective-permute-done | bytes 655392 | tf_op jit(solution)/shard_map/ppermute | solution.py:252
  104.4 3.3 %early_keys.5.part_t_ref = f32[768,512]{1,0:T(8,128)S(1)} custom-call(s32[1]{0:T(128)} %bitcast.2.choice_ref, bf16[768,5120]{1,0:T(8,128)(2,1)} %norm_input.3.normed_ref.teacher_ref, bf16[640,512]{1,0:T(8,128)(2,1)S(1)} %collective-permute-done.12.refs_2_.refs_0_, bf16[640,512]{1,0:T(8,128)(2,1)S(1)} %collective-permute-done.13.refs_3_.refs_1_, ...), custom_call_target="tpu_custom_call" | custom-call | flops 1 | bytes 1 | tf_op jit(solution)/shard_map/early_keys/pallas_call | solution.py:117
  107.7 7.9 %late_keys.1 = (bf16[768,512]{1,0:T(8,128)(2,1)S(1)}, f32[1,256]{1,0:T(1,128)S(1)}, f32[512,640]{1,0:T(8,128)S(1)}, bf16[512,640]{1,0:T(8,128)(2,1)S(1)}) custom-call(s32[1]{0:T(128)} %bitcast.2.choice_ref, bf16[768,5120]{1,0:T(8,128)(2,1)} %norm_input.2.normed_ref.student_ref.refs_5_.refs_6_, bf16[768,5120]{1,0:T(8,128)(2,1)} %norm_input.3.normed_ref.teacher_ref, ...), custom_call_target="tpu_custom_call" | custom-call | flops 1 | bytes 1 | tf_op jit(solution)/shard_map/late_keys/pallas_call | solution.py:196
  115.6 1.6 collective-permute-start.20
  117.2 3.6 %collective-permute-done.22 = f32[256]{0:T(256)S(1)} collective-permute-done((f32[256]{0:T(256)S(1)}, f32[256]{0:T(256)S(1)}, u32[]{:S(2)}, u32[]{:S(2)}) %collective-permute-start.22) | collective-permute-done | bytes 1056 | tf_op jit(solution)/shard_map/ppermute | solution.py:247
  120.8 3.1 %collective-permute-start.24 = (f32[256]{0:T(256)S(1)}, f32[256]{0:T(256)S(1)}, u32[]{:S(2)}, u32[]{:S(2)}) collective-permute-start(f32[256]{0:T(256)S(1)} %add.41), channel_id=1, source_target_pairs={{0,4},{1,5},{2,6},{3,7},{4,0},{5,1},{6,2},{7,3},{8,12},{9,13},{10,... | collective-permute-start | bytes 3080 | tf_op jit(solution)/shard_map/ppermute | solution.py:247
  124.0 1.8 collective-permute-start.23
  126.2 4.4 %collective-permute-start.27 = (bf16[256,640]{1,0:T(8,128)(2,1)S(1)}, bf16[256,640]{1,0:T(8,128)(2,1)S(1)}, u32[]{:S(2)}, u32[]{:S(2)}) collective-permute-start(bf16[256,640]{1,0:T(8,128)(2,1)S(1)} %add_convert_fusion.2), channel_id=1, source_target_pairs={{0,4},{1,5},{2,6},{3,7},{4,0},{5,1},{6,2},{7,3},{8,12},{9,13},{10,... | collective-permute-start | bytes 983048 | tf_op jit(solution)/shard_map/ppermute | solution.py:252
  130.7 2.9 %grad_blocks.3 = bf16[2,512,640]{2,1,0:T(8,128)(2,1)S(1)} custom-call(bf16[768,512]{1,0:T(8,128)(2,1)S(1)} %get-tuple-element.70.grad_ref, bf16[768,5120]{1,0:T(8,128)(2,1)} %norm_input.2.normed_ref.student_ref.refs_5_.refs_6_), custom_call_target="tpu_custom_call" | custom-call | flops 1 | bytes 1 | tf_op jit(solution)/shard_map/grad_blocks/pallas_call | solution.py:231
  134.0 2.9 %grad_blocks.4 = f32[2,512,640]{2,1,0:T(8,128)S(1)} custom-call(bf16[768,512]{1,0:T(8,128)(2,1)S(1)} %get-tuple-element.70.grad_ref, bf16[768,5120]{1,0:T(8,128)(2,1)} %norm_input.2.normed_ref.student_ref.refs_5_.refs_6_), custom_call_target="tpu_custom_call" | custom-call | flops 1 | bytes 1 | tf_op jit(solution)/shard_map/grad_blocks/pallas_call | solution.py:231
  136.9 2.9 %grad_blocks.5 = f32[2,512,640]{2,1,0:T(8,128)S(1)} custom-call(bf16[768,512]{1,0:T(8,128)(2,1)S(1)} %get-tuple-element.70.grad_ref, bf16[768,5120]{1,0:T(8,128)(2,1)} %norm_input.2.normed_ref.student_ref.refs_5_.refs_6_), custom_call_target="tpu_custom_call" | custom-call | flops 1 | bytes 1 | tf_op jit(solution)/shard_map/grad_blocks/pallas_call | solution.py:231
  139.9 11.6 %collective-permute-done.27 = bf16[256,640]{1,0:T(8,128)(2,1)S(1)} collective-permute-done((bf16[256,640]{1,0:T(8,128)(2,1)S(1)}, bf16[256,640]{1,0:T(8,128)(2,1)S(1)}, u32[]{:S(2)}, u32[]{:S(2)}) %collective-permute-start.27) | collective-permute-done | bytes 327712 | tf_op jit(solution)/shard_map/ppermute | solution.py:252
  152.3 6.2 %collective-permute-done.25 = bf16[256,640]{1,0:T(8,128)(2,1)S(1)} collective-permute-done((bf16[256,640]{1,0:T(8,128)(2,1)S(1)}, bf16[256,640]{1,0:T(8,128)(2,1)S(1)}, u32[]{:S(2)}, u32[]{:S(2)}) %collective-permute-start.25) | collective-permute-done | bytes 327712 | tf_op jit(solution)/shard_map/ppermute | solution.py:252
  159.2 9.9 %collective-permute-done.29 = bf16[512,640]{1,0:T(8,128)(2,1)S(1)} collective-permute-done((bf16[512,640]{1,0:T(8,128)(2,1)S(1)}, bf16[512,640]{1,0:T(8,128)(2,1)S(1)}, u32[]{:S(2)}, u32[]{:S(2)}) %collective-permute-start.29) | collective-permute-done | bytes 655392 | tf_op jit(solution)/shard_map/ppermute | solution.py:247
  169.3 3.2 %collective-permute-start.30 = (bf16[512,640]{1,0:T(8,128)(2,1)S(1)}, bf16[512,640]{1,0:T(8,128)(2,1)S(1)}, u32[]{:S(2)}, u32[]{:S(2)}) collective-permute-start(bf16[512,640]{1,0:T(8,128)(2,1)S(1)} %add_convert_fusion), channel_id=1, source_target_pairs={{0,6},{1,7},{2,0},{3,1},{4,2},{5,3},{6,4},{7,5},{8,14},{9,15},{10,... | collective-permute-start | bytes 1966088 | tf_op jit(solution)/shard_map/ppermute | solution.py:252
  173.1 9.3 %collective-permute-done.31 = f32[256]{0:T(256)S(1)} collective-permute-done((f32[256]{0:T(256)S(1)}, f32[256]{0:T(256)S(1)}, u32[]{:S(2)}, u32[]{:S(2)}) %collective-permute-start.31) | collective-permute-done | bytes 1056 | tf_op jit(solution)/shard_map/ppermute | solution.py:247
  184.0 7.6 %collective-permute-done.30 = bf16[512,640]{1,0:T(8,128)(2,1)S(1)} collective-permute-done((bf16[512,640]{1,0:T(8,128)(2,1)S(1)}, bf16[512,640]{1,0:T(8,128)(2,1)S(1)}, u32[]{:S(2)}, u32[]{:S(2)}) %collective-permute-start.30) | collective-permute-done | bytes 655392 | tf_op jit(solution)/shard_map/ppermute | solution.py:252
  (69 shorter events, 21.1 us)
Async XLA Ops:
  0.6 18.0 %collective-permute-start.1 = (bf16[640,512]{1,0:T(8,128)(2,1)}, bf16[640,512]{1,0:T(8,128)(2,1)S(1)}, u32[]{:S(2)}, u32[]{:S(2)}) collective-permute-start(bf16[640,512]{1,0:T(8,128)(2,1)} %bitcast.39), channel_id=1, source_target_pairs={{0,1},{1,0},{2,3},{3,2},{4,5},{5,4},{6,7},{7,6},{8,9},{9,8},{10,11... | collective-permute-start | bytes 1966088 | tf_op jit(solution)/shard_map/ppermute | solution.py:247
  5.3 15.1 %collective-permute-start.6 = (bf16[1,5248]{1,0:T(2,128)(2,1)S(1)}, bf16[1,5248]{1,0:T(2,128)(2,1)S(1)}, u32[]{:S(2)}, u32[]{:S(2)}) collective-permute-start(bf16[1,5248]{1,0:T(2,128)(2,1)S(1)} %get-tuple-element.103), channel_id=1, source_target_pairs={{0,16},{8,24},{16,0},{24,8},{1,17},{9,25},{17,1},{25,9},{2,18},{10... | collective-permute-start | bytes 31496 | tf_op jit(solution)/shard_map/ppermute | solution.py:247
  6.7 26.6 %collective-permute-start.3 = (bf16[640,512]{1,0:T(8,128)(2,1)}, bf16[640,512]{1,0:T(8,128)(2,1)S(1)}, u32[]{:S(2)}, u32[]{:S(2)}) collective-permute-start(bf16[640,512]{1,0:T(8,128)(2,1)} %bitcast.40), channel_id=1, source_target_pairs={{0,6},{1,7},{2,0},{3,1},{4,2},{5,3},{6,4},{7,5},{8,14},{9,15},{10,... | collective-permute-start | bytes 1966088 | tf_op jit(solution)/shard_map/ppermute | solution.py:252
  10.3 25.6 %collective-permute-start = (bf16[640,512]{1,0:T(8,128)(2,1)}, bf16[640,512]{1,0:T(8,128)(2,1)S(1)}, u32[]{:S(2)}, u32[]{:S(2)}) collective-permute-start(bf16[640,512]{1,0:T(8,128)(2,1)} %bitcast.41), channel_id=1, source_target_pairs={{0,16},{8,24},{16,0},{24,8},{1,17},{9,25},{17,1},{25,9},{2,18},{10... | collective-permute-start | bytes 1966088 | tf_op jit(solution)/shard_map/ppermute | solution.py:247
  10.9 28.8 %collective-permute-start.4 = (bf16[640,512]{1,0:T(8,128)(2,1)}, bf16[640,512]{1,0:T(8,128)(2,1)S(1)}, u32[]{:S(2)}, u32[]{:S(2)}) collective-permute-start(bf16[640,512]{1,0:T(8,128)(2,1)} %bitcast.42), channel_id=1, source_target_pairs={{0,2},{1,3},{2,4},{3,5},{4,6},{5,7},{6,0},{7,1},{8,10},{9,11},{10,... | collective-permute-start | bytes 1966088 | tf_op jit(solution)/shard_map/ppermute | solution.py:252
  18.6 21.6 %collective-permute-start.2 = (bf16[640,512]{1,0:T(8,128)(2,1)S(1)}, bf16[640,512]{1,0:T(8,128)(2,1)S(1)}, u32[]{:S(2)}, u32[]{:S(2)}) collective-permute-start(bf16[640,512]{1,0:T(8,128)(2,1)S(1)} %collective-permute-done.1.refs_1_), channel_id=1, source_target_pairs={{0,16},{8,24},{16,0},{24,8},{1,17},{9,25},{17,1},{25,9},{2,18},{10... | collective-permute-start | bytes 1966088 | tf_op jit(solution)/shard_map/ppermute | solution.py:247
  20.4 22.4 %collective-permute-start.7 = (bf16[2,5248]{1,0:T(2,128)(2,1)S(1)}, bf16[2,5248]{1,0:T(2,128)(2,1)S(1)}, u32[]{:S(2)}, u32[]{:S(2)}) collective-permute-start(bf16[2,5248]{1,0:T(2,128)(2,1)S(1)} %pad_maximum_fusion), channel_id=1, source_target_pairs={{0,8},{8,0},{16,24},{24,16},{1,9},{9,1},{17,25},{25,17},{2,10},{10... | collective-permute-start | bytes 62984 | tf_op jit(solution)/shard_map/ppermute | solution.py:247
  33.4 33.7 %collective-permute-start.5 = (bf16[640,512]{1,0:T(8,128)(2,1)S(1)}, bf16[640,512]{1,0:T(8,128)(2,1)S(1)}, u32[]{:S(2)}, u32[]{:S(2)}) collective-permute-start(bf16[640,512]{1,0:T(8,128)(2,1)S(1)} %bitcast.43), channel_id=1, source_target_pairs={{0,4},{1,5},{2,6},{3,7},{4,0},{5,1},{6,2},{7,3},{8,12},{9,13},{10,... | collective-permute-start | bytes 1966088 | tf_op jit(solution)/shard_map/ppermute | solution.py:252
  40.2 26.8 %collective-permute-start.10 = (bf16[640,512]{1,0:T(8,128)(2,1)S(1)}, bf16[640,512]{1,0:T(8,128)(2,1)S(1)}, u32[]{:S(2)}, u32[]{:S(2)}) collective-permute-start(bf16[640,512]{1,0:T(8,128)(2,1)S(1)} %collective-permute-done.3.refs_2_), channel_id=1, source_target_pairs={{0,16},{8,24},{16,0},{24,8},{1,17},{9,25},{17,1},{25,9},{2,18},{10... | collective-permute-start | bytes 1966088 | tf_op jit(solution)/shard_map/ppermute | solution.py:247
  40.8 26.3 %collective-permute-start.8 = (bf16[640,512]{1,0:T(8,128)(2,1)S(1)}, bf16[640,512]{1,0:T(8,128)(2,1)S(1)}, u32[]{:S(2)}, u32[]{:S(2)}) collective-permute-start(bf16[640,512]{1,0:T(8,128)(2,1)S(1)} %collective-permute-done.3.refs_2_), channel_id=1, source_target_pairs={{0,1},{1,0},{2,3},{3,2},{4,5},{5,4},{6,7},{7,6},{8,9},{9,8},{10,11... | collective-permute-start | bytes 1966088 | tf_op jit(solution)/shard_map/ppermute | solution.py:247
  41.3 27.7 %collective-permute-start.11 = (bf16[640,512]{1,0:T(8,128)(2,1)S(1)}, bf16[640,512]{1,0:T(8,128)(2,1)S(1)}, u32[]{:S(2)}, u32[]{:S(2)}) collective-permute-start(bf16[640,512]{1,0:T(8,128)(2,1)S(1)} %collective-permute-done.4.refs_3_), channel_id=1, source_target_pairs={{0,16},{8,24},{16,0},{24,8},{1,17},{9,25},{17,1},{25,9},{2,18},{10... | collective-permute-start | bytes 1966088 | tf_op jit(solution)/shard_map/ppermute | solution.py:247
  42.8 26.5 %collective-permute-start.9 = (bf16[640,512]{1,0:T(8,128)(2,1)S(1)}, bf16[640,512]{1,0:T(8,128)(2,1)S(1)}, u32[]{:S(2)}, u32[]{:S(2)}) collective-permute-start(bf16[640,512]{1,0:T(8,128)(2,1)S(1)} %collective-permute-done.4.refs_3_), channel_id=1, source_target_pairs={{0,1},{1,0},{2,3},{3,2},{4,5},{5,4},{6,7},{7,6},{8,9},{9,8},{10,11... | collective-permute-start | bytes 1966088 | tf_op jit(solution)/shard_map/ppermute | solution.py:247
  70.1 19.0 %collective-permute-start.15 = (bf16[2560,512]{1,0:T(8,128)(2,1)S(1)}, bf16[2560,512]{1,0:T(8,128)(2,1)S(1)}, u32[]{:S(2)}, u32[]{:S(2)}) collective-permute-start(bf16[2560,512]{1,0:T(8,128)(2,1)S(1)} %pack_blocks.4), channel_id=1, source_target_pairs={{0,8},{8,0},{16,24},{24,16},{1,9},{9,1},{17,25},{25,17},{2,10},{10... | collective-permute-start | bytes 7864328 | tf_op jit(solution)/shard_map/ppermute | solution.py:247
  70.2 17.6 %collective-permute-start.13 = (bf16[640,512]{1,0:T(8,128)(2,1)S(1)}, bf16[640,512]{1,0:T(8,128)(2,1)S(1)}, u32[]{:S(2)}, u32[]{:S(2)}) collective-permute-start(bf16[640,512]{1,0:T(8,128)(2,1)S(1)} %collective-permute-done.5.refs_5_.refs_1_), channel_id=1, source_target_pairs={{0,16},{8,24},{16,0},{24,8},{1,17},{9,25},{17,1},{25,9},{2,18},{10... | collective-permute-start | bytes 1966088 | tf_op jit(solution)/shard_map/ppermute | solution.py:247
  71.7 16.8 %collective-permute-start.12 = (bf16[640,512]{1,0:T(8,128)(2,1)S(1)}, bf16[640,512]{1,0:T(8,128)(2,1)S(1)}, u32[]{:S(2)}, u32[]{:S(2)}) collective-permute-start(bf16[640,512]{1,0:T(8,128)(2,1)S(1)} %collective-permute-done.10.refs_6_.refs_2_), channel_id=1, source_target_pairs={{0,1},{1,0},{2,3},{3,2},{4,5},{5,4},{6,7},{7,6},{8,9},{9,8},{10,11... | collective-permute-start | bytes 1966088 | tf_op jit(solution)/shard_map/ppermute | solution.py:247
  72.2 31.6 %collective-permute-start.16 = (bf16[640,512]{1,0:T(8,128)(2,1)S(1)}, bf16[640,512]{1,0:T(8,128)(2,1)S(1)}, u32[]{:S(2)}, u32[]{:S(2)}) collective-permute-start(bf16[640,512]{1,0:T(8,128)(2,1)S(1)} %collective-permute-done.1.refs_1_), channel_id=1, source_target_pairs={{0,4},{1,5},{2,6},{3,7},{4,0},{5,1},{6,2},{7,3},{8,12},{9,13},{10,... | collective-permute-start | bytes 1966088 | tf_op jit(solution)/shard_map/ppermute | solution.py:252
  74.9 28.9 %collective-permute-start.17 = (bf16[640,512]{1,0:T(8,128)(2,1)S(1)}, bf16[640,512]{1,0:T(8,128)(2,1)S(1)}, u32[]{:S(2)}, u32[]{:S(2)}) collective-permute-start(bf16[640,512]{1,0:T(8,128)(2,1)S(1)} %collective-permute-done.9.refs_0_), channel_id=1, source_target_pairs={{0,16},{8,24},{16,0},{24,8},{1,17},{9,25},{17,1},{25,9},{2,18},{10... | collective-permute-start | bytes 1966088 | tf_op jit(solution)/shard_map/ppermute | solution.py:247
  87.8 16.0 %collective-permute-start.18 = (bf16[640,512]{1,0:T(8,128)(2,1)S(1)}, bf16[640,512]{1,0:T(8,128)(2,1)S(1)}, u32[]{:S(2)}, u32[]{:S(2)}) collective-permute-start(bf16[640,512]{1,0:T(8,128)(2,1)S(1)} %collective-permute-done.13.refs_3_.refs_1_), channel_id=1, source_target_pairs={{0,1},{1,0},{2,3},{3,2},{4,5},{5,4},{6,7},{7,6},{8,9},{9,8},{10,11... | collective-permute-start | bytes 1966088 | tf_op jit(solution)/shard_map/ppermute | solution.py:247
  89.0 15.4 %collective-permute-start.14 = (bf16[1280,512]{1,0:T(8,128)(2,1)S(1)}, bf16[1280,512]{1,0:T(8,128)(2,1)S(1)}, u32[]{:S(2)}, u32[]{:S(2)}) collective-permute-start(bf16[1280,512]{1,0:T(8,128)(2,1)S(1)} %pack_blocks.3), channel_id=1, source_target_pairs={{0,8},{8,0},{16,24},{24,16},{1,9},{9,1},{17,25},{25,17},{2,10},{10... | collective-permute-start | bytes 3932168 | tf_op jit(solution)/shard_map/ppermute | solution.py:247
  104.2 3.5 %collective-permute-start.19 = (bf16[1280,512]{1,0:T(8,128)(2,1)S(1)}, bf16[1280,512]{1,0:T(8,128)(2,1)S(1)}, u32[]{:S(2)}, u32[]{:S(2)}) collective-permute-start(bf16[1280,512]{1,0:T(8,128)(2,1)S(1)} %pack_blocks.5), channel_id=1, source_target_pairs={{0,8},{8,0},{16,24},{24,16},{1,9},{9,1},{17,25},{25,17},{2,10},{10... | collective-permute-start | bytes 3932168 | tf_op jit(solution)/shard_map/ppermute | solution.py:247
  115.6 10.5 %collective-permute-start.20 = (bf16[256,640]{1,0:T(8,128)(2,1)S(1)}, bf16[256,640]{1,0:T(8,128)(2,1)S(1)}, u32[]{:S(2)}, u32[]{:S(2)}) collective-permute-start(bf16[256,640]{1,0:T(8,128)(2,1)S(1)} %get-tuple-element.99), channel_id=1, source_target_pairs={{0,1},{1,0},{2,3},{3,2},{4,5},{5,4},{6,7},{7,6},{8,9},{9,8},{10,11... | collective-permute-start | bytes 983048 | tf_op jit(solution)/shard_map/ppermute | solution.py:247
  117.2 3.6 %collective-permute-start.22 = (f32[256]{0:T(256)S(1)}, f32[256]{0:T(256)S(1)}, u32[]{:S(2)}, u32[]{:S(2)}) collective-permute-start(f32[256]{0:T(256)S(1)} %bitcast.46), channel_id=1, source_target_pairs={{0,2},{1,3},{2,0},{3,1},{4,6},{5,7},{6,4},{7,5},{8,10},{9,11},{10,... | collective-permute-start | bytes 3080 | tf_op jit(solution)/shard_map/ppermute | solution.py:247
  120.8 5.0 %collective-permute-start.24 = (f32[256]{0:T(256)S(1)}, f32[256]{0:T(256)S(1)}, u32[]{:S(2)}, u32[]{:S(2)}) collective-permute-start(f32[256]{0:T(256)S(1)} %add.41), channel_id=1, source_target_pairs={{0,4},{1,5},{2,6},{3,7},{4,0},{5,1},{6,2},{7,3},{8,12},{9,13},{10,... | collective-permute-start | bytes 3080 | tf_op jit(solution)/shard_map/ppermute | solution.py:247
  124.0 15.8 %collective-permute-start.23 = (bf16[256,640]{1,0:T(8,128)(2,1)S(1)}, bf16[256,640]{1,0:T(8,128)(2,1)S(1)}, u32[]{:S(2)}, u32[]{:S(2)}) collective-permute-start(bf16[256,640]{1,0:T(8,128)(2,1)S(1)} %get-tuple-element.74), channel_id=1, source_target_pairs={{0,1},{1,0},{2,3},{3,2},{4,5},{5,4},{6,7},{7,6},{8,9},{9,8},{10,11... | collective-permute-start | bytes 983048 | tf_op jit(solution)/shard_map/ppermute | solution.py:247
  126.2 25.3 %collective-permute-start.27 = (bf16[256,640]{1,0:T(8,128)(2,1)S(1)}, bf16[256,640]{1,0:T(8,128)(2,1)S(1)}, u32[]{:S(2)}, u32[]{:S(2)}) collective-permute-start(bf16[256,640]{1,0:T(8,128)(2,1)S(1)} %add_convert_fusion.2), channel_id=1, source_target_pairs={{0,4},{1,5},{2,6},{3,7},{4,0},{5,1},{6,2},{7,3},{8,12},{9,13},{10,... | collective-permute-start | bytes 983048 | tf_op jit(solution)/shard_map/ppermute | solution.py:252
  133.7 24.9 %collective-permute-start.21 = (bf16[512,640]{1,0:T(8,128)(2,1)S(1)}, bf16[512,640]{1,0:T(8,128)(2,1)S(1)}, u32[]{:S(2)}, u32[]{:S(2)}) collective-permute-start(bf16[512,640]{1,0:T(8,128)(2,1)S(1)} %get-tuple-element.71), channel_id=1, source_target_pairs={{0,1},{1,0},{2,3},{3,2},{4,5},{5,4},{6,7},{7,6},{8,9},{9,8},{10,11... | collective-permute-start | bytes 1966088 | tf_op jit(solution)/shard_map/ppermute | solution.py:247
  139.9 18.7 %collective-permute-start.25 = (bf16[256,640]{1,0:T(8,128)(2,1)S(1)}, bf16[256,640]{1,0:T(8,128)(2,1)S(1)}, u32[]{:S(2)}, u32[]{:S(2)}) collective-permute-start(bf16[256,640]{1,0:T(8,128)(2,1)S(1)} %add_convert_fusion.3), channel_id=1, source_target_pairs={{0,4},{1,5},{2,6},{3,7},{4,0},{5,1},{6,2},{7,3},{8,12},{9,13},{10,... | collective-permute-start | bytes 983048 | tf_op jit(solution)/shard_map/ppermute | solution.py:252
  151.5 17.6 %collective-permute-start.29 = (bf16[512,640]{1,0:T(8,128)(2,1)S(1)}, bf16[512,640]{1,0:T(8,128)(2,1)S(1)}, u32[]{:S(2)}, u32[]{:S(2)}) collective-permute-start(bf16[512,640]{1,0:T(8,128)(2,1)S(1)} %get-tuple-element.84), channel_id=1, source_target_pairs={{0,1},{1,0},{2,3},{3,2},{4,5},{5,4},{6,7},{7,6},{8,9},{9,8},{10,11... | collective-permute-start | bytes 1966088 | tf_op jit(solution)/shard_map/ppermute | solution.py:247
  158.5 25.5 %collective-permute-start.26 = (bf16[512,640]{1,0:T(8,128)(2,1)S(1)}, bf16[512,640]{1,0:T(8,128)(2,1)S(1)}, u32[]{:S(2)}, u32[]{:S(2)}) collective-permute-start(bf16[512,640]{1,0:T(8,128)(2,1)S(1)} %fusion.5), channel_id=1, source_target_pairs={{0,1},{1,0},{2,3},{3,2},{4,5},{5,4},{6,7},{7,6},{8,9},{9,8},{10,11... | collective-permute-start | bytes 1966088 | tf_op jit(solution)/shard_map/ppermute | solution.py:247
  159.2 24.8 %collective-permute-start.28 = (bf16[512,640]{1,0:T(8,128)(2,1)S(1)}, bf16[512,640]{1,0:T(8,128)(2,1)S(1)}, u32[]{:S(2)}, u32[]{:S(2)}) collective-permute-start(bf16[512,640]{1,0:T(8,128)(2,1)S(1)} %add_convert_fusion.1), channel_id=1, source_target_pairs={{0,2},{1,3},{2,4},{3,5},{4,6},{5,7},{6,0},{7,1},{8,10},{9,11},{10,... | collective-permute-start | bytes 1966088 | tf_op jit(solution)/shard_map/ppermute | solution.py:252
  169.3 22.4 %collective-permute-start.30 = (bf16[512,640]{1,0:T(8,128)(2,1)S(1)}, bf16[512,640]{1,0:T(8,128)(2,1)S(1)}, u32[]{:S(2)}, u32[]{:S(2)}) collective-permute-start(bf16[512,640]{1,0:T(8,128)(2,1)S(1)} %add_convert_fusion), channel_id=1, source_target_pairs={{0,6},{1,7},{2,0},{3,1},{4,2},{5,3},{6,4},{7,5},{8,14},{9,15},{10,... | collective-permute-start | bytes 1966088 | tf_op jit(solution)/shard_map/ppermute | solution.py:252
  172.5 9.8 %collective-permute-start.31 = (f32[256]{0:T(256)S(1)}, f32[256]{0:T(256)S(1)}, u32[]{:S(2)}, u32[]{:S(2)}) collective-permute-start(f32[256]{0:T(256)S(1)} %add.43), channel_id=1, source_target_pairs={{0,1},{1,0},{2,3},{3,2},{4,5},{5,4},{6,7},{7,6},{8,9},{9,8},{10,11... | collective-permute-start | bytes 3080 | tf_op jit(solution)/shard_map/ppermute | solution.py:247
  (1 other events, 9.6 us)
